TPU v7x, 128 devices: a whole 4x4x4 slice. The times are simulated.
128 devices in a mesh: mom: 16 (over x, z), band: 8 (over y, core).
Axes of the slice: x: 4, y: 4, z: 4, core: 2. Of those that a mesh axis runs over, the one named last changes fastest.
Arguments:
- ints: bfloat16 [2, 64, 16, 256, 8, 256], P(None, 'mom', None, 'band'), may hold values from -6 to 6
- vir_coef: bfloat16 [64, 2, 256, 256], P('mom'), may hold values from -0.375 to 0.375
- occ_coef: bfloat16 [64, 2, 256, 16], P(None, None, 'band'), may hold values from -0.5 to 0.5
- k4_table: int32 [64, 16], P('mom'), may hold values from 0 to 63, as said below
- band_mask: int32 [64, 256], replicated, may hold values from 0 to 1, as said below
Outputs:
- mo_ints: float32 [2, 64, 16, 16, 8, 256], P(None, None, 'mom', 'band')
Inputs may be any that keep to these rules, and one draw needn't show every extreme that they name: `k4_table`: each column of the table is a permutation of the 64 k-points. `band_mask`: each k-point's active window is a leading run of at least 128 slots; k-point 0 uses all 256.
All inputs are finite; a program needn't handle non-finite values.
Results may differ from a plain program's by a relative error of at most 0.0029.
Values may be sent and summed in bfloat16 or wider, within the bound.
No kernel may reach another device: no remote copies, remote signals or barrier semaphores. Data moves between devices by JAX's collectives and lax.ppermute only.
A program may use at most 192 MiB of HBM per device.

v0:
```python
import jax
import jax.numpy as jnp
from jax import lax
from jax.sharding import PartitionSpec as P


def occupied_terms(half_real, half_imag, occ_real, occ_imag):
    form = "ktqmb,kqa->ktamb"
    zr = jnp.einsum(form, half_real, occ_real, preferred_element_type=jnp.float32)
    zr = zr - jnp.einsum(form, half_imag, occ_imag, preferred_element_type=jnp.float32)
    zi = jnp.einsum(form, half_real, occ_imag, preferred_element_type=jnp.float32)
    zi = zi + jnp.einsum(form, half_imag, occ_real, preferred_element_type=jnp.float32)
    return jnp.stack([zr, zi])


def per_device(ints, vir_coef, occ_coef, k4_table, band_mask):
    all_vir = lax.all_gather(vir_coef, "mom", axis=0, tiled=True)
    masked = all_vir * band_mask[:, None, None, :].astype(jnp.bfloat16)
    picked = jnp.take(masked, k4_table, axis=0)
    col_real = picked[:, :, 0]
    col_imag = picked[:, :, 1]
    form = "ktqms,ktsb->ktqmb"
    yr = jnp.einsum(form, ints[0], col_real, preferred_element_type=jnp.float32)
    yr = yr - jnp.einsum(form, ints[1], col_imag, preferred_element_type=jnp.float32)
    yi = jnp.einsum(form, ints[0], col_imag, preferred_element_type=jnp.float32)
    yi = yi + jnp.einsum(form, ints[1], col_real, preferred_element_type=jnp.float32)
    half = jnp.stack([yr, yi]).astype(jnp.bfloat16)
    moved = lax.all_to_all(half, "mom", split_axis=2, concat_axis=1, tiled=True)
    partial_sum = occupied_terms(moved[0], moved[1], occ_coef[:, 0], occ_coef[:, 1])
    return lax.psum_scatter(partial_sum, "band", scatter_dimension=3, tiled=True)


def solution(mesh):
    placed = (
        P(None, "mom", None, "band", None, None),
        P("mom", None, None, None),
        P(None, None, "band", None),
        P("mom", None),
        P(),
    )
    return jax.shard_map(
        per_device,
        mesh=mesh,
        in_specs=placed,
        out_specs=P(None, None, "mom", "band", None, None),
        check_vma=False,
    )
```

profile of v0, /device:TPU:1, one launch (start us, length us, event | category | flops | bytes accessed | tf_op | source)
XLA Modules:
  0.0 718.6 jit_solution(435505783474614788)
XLA Ops:
  9.6 11.6 %fusion.21 = (bf16[1,4,16,32,8,256]{5,4,3,2,1,0:T(8,128)(2,1)}, bf16[1,4,16,32,8,256]{5,4,3,2,1,0:T(8,128)(2,1)}) fusion(bf16[2,4,16,32,8,256]{5,4,3,2,1,0:T(8,128)(2,1)} %param.5), kind=kLoop, calls=%fused_computation.34 | loop fusion | bytes 33554432 | tf_op jit(solution)/shard_map/slice | solution.py:24
  21.1 103.0 %all-gather.2.cloned.1.call-done = bf16[64,2,256,256]{3,2,1,0:T(8,128)(2,1)} async-done(((bf16[4,2,256,256]{3,2,1,0:T(8,128)(2,1)}), bf16[64,2,256,256]{3,2,1,0:T(8,128)(2,1)}) %all-gather.2.cloned.1.call-update) | async-done | bytes 16777232 | tf_op jit(solution)/shard_map/all_gather | solution.py:17
  124.2 13.7 %broadcast_multiply_fusion = bf16[64,2,256,256]{3,2,1,0:T(8,128)(2,1)} fusion(bf16[64,2,256,256]{3,2,1,0:T(8,128)(2,1)} %all-gather.2.cloned.1.call-done, bf16[64,256]{1,0:T(8,128)(2,1)S(1)} %convert_element_type.5), kind=kLoop, calls=%fused_computation.13 | loop fusion | flops 8388608 | bytes 33587200 | tf_op jit(solution)/shard_map/mul | solution.py:18
  137.9 13.4 %gather_fusion = bf16[64,2,256,256]{3,2,1,0:T(8,128)(2,1)} fusion(bf16[64,2,256,256]{3,2,1,0:T(8,128)(2,1)} %broadcast_multiply_fusion, s32[1024]{0:T(1024)S(1)} %pad_clamp_fusion), kind=kCustom, calls=%fused_computation | custom fusion | bytes 33554688 | tf_op jit(solution)/shard_map/jit(_take)/gather | solution.py:19
  151.3 8.6 %copy.24 = bf16[64,2,256,256]{3,2,0,1:T(8,128)(2,1)S(1)} copy(bf16[64,2,256,256]{3,2,1,0:T(8,128)(2,1)} %gather_fusion) | data formatting | bytes 33554432 | tf_op jit(solution)/shard_map/jit(_take)/gather | solution.py:19
  159.9 7.1 broadcast_select_fusion
  167.0 12.9 %fusion.1 = f32[4,16,256,32,8]{2,3,4,1,0:T(8,128)} fusion(bf16[1,4,16,32,8,256]{5,4,3,2,1,0:T(8,128)(2,1)} %get-tuple-element.8, bf16[4,16,2,256,256]{4,3,1,0,2:T(8,128)(2,1)} %broadcast_select_fusion), kind=kOutput, calls=%fused_computation.15 | convolution fusion | flops 2147483648 | bytes 33554432 | tf_op jit(solution)/shard_map/ktqms,ktsb->ktqmb/dot_general | solution.py:23
  179.9 12.9 %fusion = f32[4,16,256,32,8]{2,3,4,1,0:T(8,128)} fusion(bf16[1,4,16,32,8,256]{5,4,3,2,1,0:T(8,128)(2,1)} %get-tuple-element.8, bf16[4,16,2,256,256]{4,3,1,0,2:T(8,128)(2,1)} %broadcast_select_fusion), kind=kOutput, calls=%fused_computation.14 | convolution fusion | flops 2147483648 | bytes 33554432 | tf_op jit(solution)/shard_map/ktqms,ktsb->ktqmb/dot_general | solution.py:25
  192.8 15.3 %fusion.10 = bf16[1,4,16,32,8,256]{5,3,4,2,1,0:T(8,128)(2,1)} fusion(f32[4,16,256,32,8]{2,3,4,1,0:T(8,128)} %fusion.1, bf16[1,4,16,32,8,256]{5,4,3,2,1,0:T(8,128)(2,1)} %get-tuple-element.7, bf16[4,16,2,256,256]{4,3,1,0,2:T(8,128)(2,1)} %broadcast_select_fusion), kind=kOutput, calls=%fused_computation.24 | convolution fusion | flops 2155872256 | bytes 41943040 | tf_op jit(solution)/shard_map/ktqms,ktsb->ktqmb/dot_general | solution.py:24
  208.1 15.3 %fusion.11 = bf16[1,4,16,32,8,256]{5,3,4,2,1,0:T(8,128)(2,1)} fusion(f32[4,16,256,32,8]{2,3,4,1,0:T(8,128)} %fusion, bf16[1,4,16,32,8,256]{5,4,3,2,1,0:T(8,128)(2,1)} %get-tuple-element.7, bf16[4,16,2,256,256]{4,3,1,0,2:T(8,128)(2,1)} %broadcast_select_fusion), kind=kOutput, calls=%fused_computation.25 | convolution fusion | flops 2155872256 | bytes 41943040 | tf_op jit(solution)/shard_map/ktqms,ktsb->ktqmb/dot_general | solution.py:26
  223.5 8.0 %pad_maximum_fusion = bf16[2,4,16,32,8,256]{5,3,4,2,1,0:T(8,128)(2,1)S(1)} fusion(bf16[1,4,16,32,8,256]{5,3,4,2,1,0:T(8,128)(2,1)} %fusion.11, bf16[1,4,16,32,8,256]{5,3,4,2,1,0:T(8,128)(2,1)} %fusion.10), kind=kLoop, calls=%fused_computation.1 | loop fusion | flops 8388608 | bytes 33554432 | tf_op jit(solution)/shard_map/stack | solution.py:27
  231.5 6.7 copy.27
  238.2 5.3 all-to-all-start
  244.3 291.1 %all-to-all-done = bf16[2,4,16,32,8,256]{5,3,4,1,0,2:T(8,128)(2,1)} async-done(((bf16[2,4,16,32,8,256]{5,3,4,1,0,2:T(8,128)(2,1)}), bf16[2,4,16,32,8,256]{5,3,4,1,0,2:T(8,128)(2,1)}, u32[]{:S(2)}, u32[]{:S(2)}) %all-to-all-start) | async-done | bytes 16777248 | tf_op jit(solution)/shard_map/all_to_all | solution.py:28
  535.4 17.8 %copy.68 = bf16[2,4,16,32,8,256]{5,4,3,1,2,0:T(8,128)(2,1)} copy(bf16[2,4,16,32,8,256]{5,3,4,1,0,2:T(8,128)(2,1)} %all-to-all-done) | data formatting | bytes 33554432 | tf_op jit(solution)/shard_map/all_to_all | solution.py:28
  553.2 6.6 fusion.20
  559.8 4.7 fusion.2
  564.6 4.7 fusion.4
  569.3 8.7 %subtract_bitcast_fusion = f32[1,64,1,16,8,256]{5,3,4,1,2,0:T(8,128)} fusion(f32[64,8,256,16]{2,3,1,0:T(8,128)} %fusion.2, bf16[64,32,8,256]{3,2,1,0:T(8,128)(2,1)S(1)} %bitcast.70, bf16[64,1,32,16]{2,3,0,1:T(8,128)(2,1)S(1)} %copy.41), kind=kOutput, calls=%fused_computation.12 | convolution fusion | flops 136314880 | bytes 25231360 | tf_op jit(solution)/shard_map/ktqmb,kqa->ktamb/dot_general | solution.py:9
  578.1 5.3 add_bitcast_fusion
  583.4 7.1 pad_maximum_fusion.1
  590.5 19.4 %copy.35 = f32[2,64,1,16,8,256]{5,4,2,1,0,3:T(8,128)} copy(f32[2,64,1,16,8,256]{5,3,4,1,2,0:T(8,128)S(1)} %pad_maximum_fusion.1) | data formatting | bytes 33554432 | tf_op jit(solution)/shard_map/stack | solution.py:13
  609.9 98.6 %reduce-scatter.2.cloned.1.call-done = f32[2,64,1,2,8,256]{5,4,2,1,0,3:T(8,128)} async-done(((f32[2,64,1,16,8,256]{5,4,2,1,0,3:T(8,128)}), f32[2,64,1,2,8,256]{5,4,2,1,0,3:T(8,128)}) %reduce-scatter.2.cloned.1.call-update) | async-done | bytes 2097168 | tf_op jit(solution)/shard_map/reduce_scatter | solution.py:30
  708.6 3.2 copy.36
  (16 shorter events, 3.9 us)
Async XLA Ops:
  6.5 117.6 %all-gather.2.cloned.1.call-start = ((), (), s32[]{:S(2)}) async-start(), calls=%async_computation.2 | async-start | bytes 17825792 | tf_op jit(solution)/shard_map/all_gather | solution.py:17
  238.1 5.5 copy-start.1
  238.2 297.2 %all-to-all-start = ((bf16[2,4,16,32,8,256]{5,3,4,1,0,2:T(8,128)(2,1)}), bf16[2,4,16,32,8,256]{5,3,4,1,0,2:T(8,128)(2,1)}, u32[]{:S(2)}, u32[]{:S(2)}) async-start(bf16[2,4,16,32,8,256]{5,3,4,1,0,2:T(8,128)(2,1)} %copy.27), calls=%async_computation | async-start | bytes 33554432 | tf_op jit(solution)/shard_map/all_to_all | solution.py:28
  243.4 465.1 %reduce-scatter.2.cloned.1.call-start = ((), (), s32[]{:S(2)}) async-start(), calls=%async_computation.3 | async-start | bytes 18874368 | tf_op jit(solution)/shard_map/reduce_scatter | solution.py:30
  569.3 8.8 %copy-start = (f32[64,8,256,16]{2,3,1,0:T(8,128)S(1)}, f32[64,8,256,16]{2,3,1,0:T(8,128)}, u32[]{:S(2)}) copy-start(f32[64,8,256,16]{2,3,1,0:T(8,128)} %fusion.4) | copy-start | bytes 25165828
Sparse Core Ops, SparseCore 0:
  9.5 114.6 all-gather.1
  610.1 98.4 reduce-scatter.1
where the time goes:
time: 719 us
  waiting for transfers between devices  493 us (69%)
  local copies, waits for them, and re-layouts  88 us (12%)
  matrix products  80 us (11%)
  other arithmetic  38.1 us (5%)
  between operations  13.5 us (2%)
    all_to_all x1, waiting for transfers between devices, per_device(): moved = lax.all_to_all(half, 'mom', split_axis=2, concat_axis=1, tiled=True)  291 us
    all_gather x1, waiting for transfers between devices, per_device(): all_vir = lax.all_gather(vir_coef, 'mom', axis=0, tiled=True)  103 us
    reduce_scatter x1, waiting for transfers between devices, per_device(): lax.psum_scatter(partial_sum, 'band', scatter_dimension=3, tiled=True)  98.6 us
    gather x2, local copies, waits for them, and re-layouts, per_device(): picked = jnp.take(masked, k4_table, axis=0)  22 us
    another operation x1, local copies, waits for them, and re-layouts, occupied_terms(): return jnp.stack([zr, zi])  19.4 us
    all_to_all x1, local copies, waits for them, and re-layouts, per_device(): moved = lax.all_to_all(half, 'mom', split_axis=2, concat_axis=1, tiled=True)  17.8 us
    dot_general x1, matrix products, per_device(): jnp.einsum(form, ints[1], col_real, preferred_element_type=jnp.float32)  15.3 us
    dot_general x1, matrix products, per_device(): jnp.einsum(form, ints[1], col_imag, preferred_element_type=jnp.float32)  15.3 us
  transfers between devices with their start and end apart: 3, of which 3 were waited for; matrix products, arithmetic and copies ran while one was open for 2% of the time, Pallas kernels for 0%

commit v1 on v0

v1 whole, which is shorter than its diff:
```python
import functools

import jax
import jax.numpy as jnp
from jax import lax
from jax.experimental import pallas as pl
from jax.experimental.pallas import tpu as pltpu
from jax.sharding import PartitionSpec as P

CHUNKS = 2
PAIR_TYPE = jnp.float32
STEP = 8
MIB = 1 << 20


def contract_occupied(coef, ints, first, count):
    def kernel(coef_ref, ints_ref, mine_ref, theirs_ref, wide):
        @pl.when(pl.program_id(1) == 0)
        def _():
            rows = lax.broadcasted_iota(jnp.int32, (256, 32), 0) // 8
            spread = (rows == lax.broadcasted_iota(jnp.int32, (256, 32), 1)).astype(jnp.bfloat16)
            cols = lax.broadcasted_iota(jnp.int32, (64, 512), 1) // 8
            across = (cols == lax.broadcasted_iota(jnp.int32, (64, 512), 0)).astype(jnp.bfloat16)
            tall = jnp.dot(spread, coef_ref[0], preferred_element_type=jnp.float32).astype(jnp.bfloat16)
            full = jnp.dot(tall, across, preferred_element_type=jnp.float32)
            same = (
                lax.broadcasted_iota(jnp.int32, (256, 512), 0) % 8 == lax.broadcasted_iota(jnp.int32, (256, 512), 1) % 8
            )
            wide[...] = jnp.where(same, full, 0.0).astype(jnp.bfloat16)

        for t in range(STEP):
            got = jnp.dot(wide[:, :256], ints_ref[0, 0, t], preferred_element_type=jnp.float32)
            got = got + jnp.dot(wide[:, 256:], ints_ref[1, 0, t], preferred_element_type=jnp.float32)
            for d in range(4):
                mine_ref[d, 0, t] = got[32 * d : 32 * d + 32]
                theirs_ref[d, 0, t] = got[128 + 32 * d : 160 + 32 * d].astype(theirs_ref.dtype)

    block = pl.BlockSpec((4, 1, STEP, 32, 256), lambda k, t: (0, k, t, 0, 0))
    return pl.pallas_call(
        kernel,
        grid=(count, 16 // STEP),
        in_specs=[
            pl.BlockSpec((1, 32, 64), lambda k, t: (k + first, 0, 0)),
            pl.BlockSpec((2, 1, STEP, 256, 256), lambda k, t: (0, k + first, t, 0, 0)),
        ],
        out_specs=[block, block],
        out_shape=[
            jax.ShapeDtypeStruct((4, count, 16, 32, 256), jnp.float32),
            jax.ShapeDtypeStruct((4, count, 16, 32, 256), PAIR_TYPE),
        ],
        scratch_shapes=[pltpu.VMEM((256, 512), jnp.bfloat16)],
        compiler_params=pltpu.CompilerParams(vmem_limit_bytes=40 * MIB),
        cost_estimate=pl.CostEstimate(
            flops=count * 16 * 2 * 256 * 512 * 256, bytes_accessed=count * 16 * 512 * 1024, transcendentals=0
        ),
        name="contract_occupied",
    )(coef, ints)


def contract_virtual(k4, core, mask, held, other, u, out, first, count):
    n = 16 * count

    def kernel(k4_ref, core_ref, mask_ref, held_ref, other_ref, u_ref, *rest):
        out_ref, own, paired, sems = rest[-4:]

        def copies(k):
            at = k4_ref[(k // count) * 4 + first + k % count]
            return (
                pltpu.make_async_copy(held_ref.at[at], own.at[k], sems.at[0, k]),
                pltpu.make_async_copy(other_ref.at[at], paired.at[k], sems.at[1, k]),
            )

        @pl.loop(0, n)
        def _(k):
            for copy in copies(k):
                copy.start()

        even = core_ref[0] == 0

        @pl.loop(0, n)
        def _(k):
            for copy in copies(k):
                copy.wait()
            at = k4_ref[(k // count) * 4 + first + k % count]
            full = u_ref[k // count, k % count]
            high = full.astype(jnp.bfloat16)
            low = (full - high.astype(jnp.float32)).astype(jnp.bfloat16)
            rows = jnp.concatenate([high, low], axis=0)
            a = jnp.dot(rows, own[k], preferred_element_type=jnp.float32)
            b = jnp.dot(rows, paired[k], preferred_element_type=jnp.float32)
            a = a[:32] + a[32:]
            b = b[:32] + b[32:]
            by_real = jnp.where(even, a, b)
            by_imag = jnp.where(even, b, a)
            keep = mask_ref[pl.ds(at, 1), :].astype(jnp.float32)
            real = (by_real[:16] - by_imag[16:]) * keep
            imag = (by_imag[:16] + by_real[16:]) * keep
            out_ref[0, k // count, k % count] = real
            out_ref[1, k // count, k % count] = imag

    whole = pl.BlockSpec(memory_space=pl.ANY)
    args = [k4, core, mask, held, other, u]
    specs = [
        pl.BlockSpec(memory_space=pltpu.SMEM),
        pl.BlockSpec(memory_space=pltpu.SMEM),
        pl.BlockSpec((64, 256), lambda i: (0, 0)),
        whole,
        whole,
        pl.BlockSpec((16, count, 32, 256), lambda i: (0, 0, 0, 0)),
    ]
    alias = {}
    if out is not None:
        args.append(out)
        specs.append(whole)
        alias = {6: 0}
    return pl.pallas_call(
        kernel,
        grid=(1,),
        in_specs=specs,
        out_specs=pl.BlockSpec((2, 16, count, 16, 256), lambda i: (0, 0, first // count, 0, 0)),
        out_shape=jax.ShapeDtypeStruct((2, 16, 4, 16, 256), jnp.float32),
        scratch_shapes=[
            pltpu.VMEM((n, 256, 256), jnp.bfloat16),
            pltpu.VMEM((n, 256, 256), jnp.bfloat16),
            pltpu.SemaphoreType.DMA((2, n)),
        ],
        input_output_aliases=alias,
        compiler_params=pltpu.CompilerParams(vmem_limit_bytes=48 * MIB),
        cost_estimate=pl.CostEstimate(
            flops=n * 2 * 2 * 64 * 256 * 256, bytes_accessed=n * 300 * 1024, transcendentals=0
        ),
        name="contract_virtual",
    )(*args)


def per_device(ints, vir_coef, occ_coef, k4_table, band_mask):
    mom, band = lax.axis_index("mom"), lax.axis_index("band")
    core, y = band % 2, band // 2

    def across(x):
        return lax.ppermute(x, "band", [(i, i ^ 1) for i in range(8)])

    def along(x, d):
        return lax.ppermute(x, "band", [(i, (i // 2 + d) % 4 * 2 + i % 2) for i in range(8)])

    table = lax.all_gather(k4_table, "mom", axis=0, tiled=True)
    k4 = lax.dynamic_index_in_dim(table, mom, axis=1, keepdims=False)
    half = lax.dynamic_index_in_dim(vir_coef, core, axis=1, keepdims=False)
    held = lax.all_gather(half, "mom", axis=0, tiled=True)

    occ = lax.dynamic_slice_in_dim(occ_coef, 4 * mom, 4, axis=0)
    order = (
        4 * ((y + jnp.arange(4)[None, :, None]) % 4)
        + 2 * ((core + jnp.arange(2)[:, None, None]) % 2)
        + jnp.arange(2)[None, None, :]
    ).reshape(16)
    occ = jnp.take(occ, order, axis=3).reshape(4, 2, 32, 8, 2)
    parts = jnp.stack([jnp.stack([occ[:, 0], -occ[:, 1]], 1), jnp.stack([occ[:, 1], occ[:, 0]], 1)], 1)
    coef = parts.transpose(0, 4, 1, 5, 2, 3).reshape(4, 32, 64)

    ints = ints.reshape(2, 4, 16, 256, 256)
    count = 4 // CHUNKS
    sums = []
    for c in range(CHUNKS):
        mine, theirs = contract_occupied(coef, ints, c * count, count)
        sums.append((mine, across(theirs)))
    moved = []
    for mine, got in sums:
        total = [mine[d] + got[d].astype(jnp.float32) for d in range(4)]
        up = along(total[2][:, :8].astype(jnp.bfloat16), 1)
        down = along(total[2][:, 8:].astype(jnp.bfloat16), -1)
        right = jnp.concatenate([total[1][:, :8] + up.astype(jnp.float32), total[1][:, 8:]], axis=1)
        left = jnp.concatenate([total[3][:, :8], total[3][:, 8:] + down.astype(jnp.float32)], axis=1)
        right = along(right.astype(jnp.bfloat16), 1)
        left = along(left.astype(jnp.bfloat16), -1)
        u = total[0] + right.astype(jnp.float32) + left.astype(jnp.float32)
        u = u.transpose(1, 0, 2, 3)
        moved.append(lax.all_to_all(u, "mom", split_axis=0, concat_axis=0, tiled=True))
    other = across(held)
    out = None
    which = core.reshape(1)
    for c in range(CHUNKS):
        out = contract_virtual(k4, which, band_mask, held, other, moved[c], out, c * count, count)
    return out.reshape(2, 64, 1, 2, 8, 256)


def solution(mesh):
    placed = (
        P(None, "mom", None, "band", None, None),
        P("mom", None, None, None),
        P(None, None, "band", None),
        P("mom", None),
        P(),
    )
    return jax.shard_map(
        per_device,
        mesh=mesh,
        in_specs=placed,
        out_specs=P(None, None, "mom", "band", None, None),
        check_vma=False,
    )
```

time: 719 us -> 200 us (0.28)
  the two profiles are of different devices: /device:TPU:1 before, /device:TPU:24 now
where the time goes in v1:
time: 200 us; the launch traced here: 199 us
  waiting for transfers between devices  77.5 us (39%)
  Pallas kernels  30.6 us (15%)
  blocking collectives  28.9 us (14%)
  starting transfers between devices  22.4 us (11%)
  other arithmetic  14.3 us (7%)
  between operations  13.7 us (7%)
  local copies, waits for them, and re-layouts  11.9 us (6%)
    all_gather x1, waiting for transfers between devices, per_device(): held = lax.all_gather(half, 'mom', axis=0, tiled=True)  50.9 us
    all_gather x1, blocking collectives, per_device(): table = lax.all_gather(k4_table, 'mom', axis=0, tiled=True)  28.9 us
    ppermute x8, waiting for transfers between devices, along(): lax.ppermute(x, 'band', [(i, (i // 2 + d) % 4 * 2 + i % 2) for i in range...  26.6 us
    pallas_call x2, Pallas kernels, contract_virtual(): pl.pallas_call(kernel, grid=(1,), in_specs=specs, out_specs=pl.BlockSpec(...  17.7 us
    pallas_call x2, Pallas kernels, contract_occupied(): pl.pallas_call(kernel, grid=(count, 16 // STEP), in_specs=[pl.BlockSpec((...  12.9 us
    all_to_all x2, starting transfers between devices, per_device(): lax.all_to_all(u, 'mom', split_axis=0, concat_axis=0, tiled=True)  12.2 us
    ppermute x8, starting transfers between devices, along(): lax.ppermute(x, 'band', [(i, (i // 2 + d) % 4 * 2 + i % 2) for i in range...  9.71 us
    add x2, other arithmetic, per_device(): total = [mine[d] + got[d].astype(jnp.float32) for d in range(4)]  6.19 us
  transfers between devices with their start and end apart: 14, of which 5 were waited for; matrix products, arithmetic and copies ran while one was open for 12% of the time, Pallas kernels for 11%

profile of v1, /device:TPU:24, one launch (start us, length us, event | category | flops | bytes accessed | tf_op | source)
XLA Modules:
  0.0 199.3 jit_solution(14220703926937283402)
XLA Ops:
  6.5 1.2 copy-done
  9.0 1.1 constant_dynamic-slice_fusion
  11.7 6.4 %contract_occupied.3 = (f32[4,2,16,32,256]{4,3,2,1,0:T(8,128)S(1)}, f32[4,2,16,32,256]{4,3,2,1,0:T(8,128)S(1)}) custom-call(bf16[4,32,64]{2,1,0:T(8,128)(2,1)S(1)} %reshape.148.coef_ref, bf16[2,4,16,256,256]{4,3,2,1,0:T(8,128)(2,1)} %bitcast.56), custom_call_target="tpu_custom_call" | custom-call | flops 2147483648 | bytes 16777216 | tf_op jit(solution)/shard_map/contract_occupied/pallas_call | solution.py:39
  18.1 3.0 %copy.48 = f32[4,2,16,32,256]{4,3,1,2,0:T(8,128)} copy(f32[4,2,16,32,256]{4,3,2,1,0:T(8,128)S(1)} %get-tuple-element.12) | data formatting | bytes 8388608 | tf_op jit(solution)/shard_map/contract_occupied/pallas_call | solution.py:39
  21.4 6.5 %contract_occupied.2 = (f32[4,2,16,32,256]{4,3,2,1,0:T(8,128)S(1)}, f32[4,2,16,32,256]{4,3,2,1,0:T(8,128)S(1)}) custom-call(bf16[4,32,64]{2,1,0:T(8,128)(2,1)S(1)} %reshape.148.coef_ref, bf16[2,4,16,256,256]{4,3,2,1,0:T(8,128)(2,1)} %bitcast.57), custom_call_target="tpu_custom_call" | custom-call | flops 2147483648 | bytes 16777216 | tf_op jit(solution)/shard_map/contract_occupied/pallas_call | solution.py:39
  27.9 2.9 %copy.43 = f32[4,2,16,32,256]{4,3,1,2,0:T(8,128)} copy(f32[4,2,16,32,256]{4,3,2,1,0:T(8,128)S(1)} %get-tuple-element.10) | data formatting | bytes 8388608 | tf_op jit(solution)/shard_map/contract_occupied/pallas_call | solution.py:39
  31.6 50.9 %all-gather.4.cloned.1.call-done = bf16[64,1,256,256]{3,2,1,0:T(8,128)(2,1)} async-done(((bf16[4,1,256,256]{3,2,1,0:T(8,128)(2,1)}), bf16[64,1,256,256]{3,2,1,0:T(8,128)(2,1)}) %all-gather.4.cloned.1.call-update) | async-done | bytes 8388624 | tf_op jit(solution)/shard_map/all_gather | solution.py:149
  82.5 3.7 %fusion.2 = (f32[2,16,32,256]{3,2,0,1:T(8,128)S(1)}, f32[2,16,32,256]{3,2,0,1:T(8,128)S(1)}, bf16[2,16,32,256]{3,2,0,1:T(8,128)(2,1)S(1)}) fusion(f32[4,2,16,32,256]{4,3,1,2,0:T(8,128)} %collective-permute-done.6, f32[4,2,16,32,256]{4,3,2,1,0:T(8,128)} %copy-done.4), kind=kLoop, calls=%fused_computation.6 | loop fusion | flops 1048576 | bytes 8912896 | tf_op jit(solution)/shard_map/add | solution.py:169
  86.9 1.5 collective-permute-start.9
  88.4 2.5 %fusion.9 = (f32[2,16,32,256]{3,2,0,1:T(8,128)S(1)}, f32[2,16,32,256]{3,2,0,1:T(8,128)S(1)}, bf16[2,16,32,256]{3,2,0,1:T(8,128)(2,1)S(1)}) fusion(f32[4,2,16,32,256]{4,3,1,2,0:T(8,128)} %collective-permute-done.1, f32[4,2,16,32,256]{4,3,2,1,0:T(8,128)S(1)} %copy-done.3), kind=kLoop, calls=%fused_computation.17 | loop fusion | flops 1048576 | bytes 8912896 | tf_op jit(solution)/shard_map/add | solution.py:169
  92.5 4.7 %collective-permute-done.9 = bf16[2,8,32,256]{3,2,0,1:T(8,128)(2,1)S(1)} collective-permute-done((bf16[2,8,32,256]{3,2,0,1:T(8,128)(2,1)S(1)}, bf16[2,8,32,256]{3,2,0,1:T(8,128)(2,1)S(1)}, u32[]{:S(2)}, u32[]{:S(2)}) %collective-permute-start.9) | collective-permute-done | bytes 262176 | tf_op jit(solution)/shard_map/ppermute | solution.py:144
  97.9 3.0 %collective-permute-start.8 = (bf16[2,16,32,256]{3,2,0,1:T(8,128)(2,1)S(1)}, bf16[2,16,32,256]{3,2,0,1:T(8,128)(2,1)S(1)}, u32[]{:S(2)}, u32[]{:S(2)}) collective-permute-start(bf16[2,16,32,256]{3,2,0,1:T(8,128)(2,1)S(1)} %pad_maximum_fusion.2), channel_id=1, source_target_pairs={{0,2},{1,3},{2,4},{3,5},{4,6},{5,7},{6,0},{7,1},{8,10},{9,11},{10,... | collective-permute-start | bytes 1572872 | tf_op jit(solution)/shard_map/ppermute | solution.py:144
  101.1 1.8 collective-permute-done.4
  103.4 10.7 %collective-permute-done.10 = bf16[2,16,32,256]{3,2,0,1:T(8,128)(2,1)S(1)} collective-permute-done((bf16[2,16,32,256]{3,2,0,1:T(8,128)(2,1)S(1)}, bf16[2,16,32,256]{3,2,0,1:T(8,128)(2,1)S(1)}, u32[]{:S(2)}, u32[]{:S(2)}) %collective-permute-start.10) | collective-permute-done | bytes 524320 | tf_op jit(solution)/shard_map/ppermute | solution.py:144
  114.1 2.9 %fusion.6 = f32[16,2,32,256]{3,2,1,0:T(8,128)} fusion(f32[4,2,16,32,256]{4,3,1,2,0:T(8,128)} %collective-permute-done.6, bf16[2,16,32,256]{3,2,0,1:T(8,128)(2,1)S(1)} %collective-permute-done.10, bf16[2,16,32,256]{3,2,0,1:T(8,128)(2,1)S(1)} %collective-permute-done.8, f32[4,2,16,32,256]{4,3,2,1,0:T(8,128)} %copy-done.4), kind=kLoop, calls=%fused_computation.11 | loop fusion | flops 1310720 | bytes 4194304 | tf_op jit(solution)/shard_map/transpose | solution.py:177
  117.0 5.3 %all-to-all-start.1 = ((f32[16,2,32,256]{3,2,1,0:T(8,128)}), f32[16,2,32,256]{3,2,1,0:T(8,128)S(1)}, u32[]{:S(2)}, u32[]{:S(2)}) async-start(f32[16,2,32,256]{3,2,1,0:T(8,128)} %fusion.6), calls=%async_computation.1 | async-start | bytes 2097152 | tf_op jit(solution)/shard_map/all_to_all | solution.py:178
  122.3 1.1 fusion.19
  123.4 2.9 %collective-permute-start.3 = (bf16[2,16,32,256]{3,2,0,1:T(8,128)(2,1)S(1)}, bf16[2,16,32,256]{3,2,0,1:T(8,128)(2,1)S(1)}, u32[]{:S(2)}, u32[]{:S(2)}) collective-permute-start(bf16[2,16,32,256]{3,2,0,1:T(8,128)(2,1)S(1)} %pad_maximum_fusion), channel_id=1, source_target_pairs={{0,2},{1,3},{2,4},{3,5},{4,6},{5,7},{6,0},{7,1},{8,10},{9,11},{10,... | collective-permute-start | bytes 1572872 | tf_op jit(solution)/shard_map/ppermute | solution.py:144
  126.4 9.4 %collective-permute-done.3 = bf16[2,16,32,256]{3,2,0,1:T(8,128)(2,1)S(1)} collective-permute-done((bf16[2,16,32,256]{3,2,0,1:T(8,128)(2,1)S(1)}, bf16[2,16,32,256]{3,2,0,1:T(8,128)(2,1)S(1)}, u32[]{:S(2)}, u32[]{:S(2)}) %collective-permute-start.3) | collective-permute-done | bytes 524320 | tf_op jit(solution)/shard_map/ppermute | solution.py:144
  135.8 2.9 %fusion.13 = f32[16,2,32,256]{3,2,1,0:T(8,128)} fusion(f32[4,2,16,32,256]{4,3,1,2,0:T(8,128)} %collective-permute-done.1, bf16[2,16,32,256]{3,2,0,1:T(8,128)(2,1)S(1)} %collective-permute-done.5, bf16[2,16,32,256]{3,2,0,1:T(8,128)(2,1)S(1)} %collective-permute-done.3, f32[4,2,16,32,256]{4,3,2,1,0:T(8,128)} %copy-done.2), kind=kLoop, calls=%fused_computation.22 | loop fusion | flops 1310720 | bytes 4194304 | tf_op jit(solution)/shard_map/transpose | solution.py:177
  138.7 6.9 %all-to-all-start = ((f32[16,2,32,256]{3,2,1,0:T(8,128)}), f32[16,2,32,256]{3,2,1,0:T(8,128)S(1)}, u32[]{:S(2)}, u32[]{:S(2)}) async-start(f32[16,2,32,256]{3,2,1,0:T(8,128)} %fusion.13), calls=%async_computation | async-start | bytes 2097152 | tf_op jit(solution)/shard_map/all_to_all | solution.py:178
  145.7 28.9 %all-gather.1 = s32[16,4,16]{2,1,0:T(4,128)S(1)} all-gather(s32[1,4,16]{2,1,0:T(4,128)S(1)} %bitcast.63), channel_id=1, replica_groups=mesh['mom'=16,'band'=8] {'mom'}, dimensions={0}, use_global_device_ids=true | all-gather | bytes 4352 | tf_op jit(solution)/shard_map/all_gather | solution.py:146
  174.8 8.8 %contract_virtual.2.rest_0_ = f32[2,16,4,16,256]{4,3,2,1,0:T(8,128)} custom-call(s32[64]{0:T(128)S(1)} %bitcast.54, s32[1]{0:T(128)} %bitcast.3.core_ref, s32[64,256]{1,0:T(8,128)S(1)} %copy-done.5, bf16[64,256,256]{2,1,0:T(8,128)(2,1)} %bitcast.59, bf16[64,256,256]{2,1,0:T(8,128)(2,1)} %collective-permute-done.other_ref, ...), custom_call_target="tpu_custom_call" | custom-call | flops 536870912 | bytes 9830400 | tf_op jit(solution)/shard_map/contract_virtual/pallas_call | solution.py:116
  183.6 8.8 %contract_virtual.3 = f32[2,16,4,16,256]{4,3,2,1,0:T(8,128)} custom-call(s32[64]{0:T(128)S(1)} %bitcast.55, s32[1]{0:T(128)} %bitcast.3.core_ref, s32[64,256]{1,0:T(8,128)S(1)} %copy-done.5, bf16[64,256,256]{2,1,0:T(8,128)(2,1)} %bitcast.60, bf16[64,256,256]{2,1,0:T(8,128)(2,1)} %collective-permute-done.other_ref, ...), custom_call_target="tpu_custom_call", output_to_operand_aliasing={{}: (6, {})} | custom-call | flops 536870912 | bytes 9830400 | tf_op jit(solution)/shard_map/contract_virtual/pallas_call | solution.py:116
  (64 shorter events, 7.6 us)
Async XLA Ops:
  6.5 1.2 copy-start
  6.5 76.0 %all-gather.4.cloned.1.call-start = ((), (), s32[]{:S(2)}) async-start(), calls=%async_computation.2 | async-start | bytes 8912896 | tf_op jit(solution)/shard_map/all_gather | solution.py:149
  18.1 3.3 %copy-start.4 = (f32[4,2,16,32,256]{4,3,2,1,0:T(8,128)}, f32[4,2,16,32,256]{4,3,2,1,0:T(8,128)S(1)}, u32[]{:S(2)}) copy-start(f32[4,2,16,32,256]{4,3,2,1,0:T(8,128)S(1)} %get-tuple-element.11) | copy-start | bytes 12582916
  21.4 61.1 %collective-permute-start.6 = (f32[4,2,16,32,256]{4,3,1,2,0:T(8,128)}, f32[4,2,16,32,256]{4,3,1,2,0:T(8,128)}, u32[]{:S(2)}, u32[]{:S(2)}) collective-permute-start(f32[4,2,16,32,256]{4,3,1,2,0:T(8,128)} %copy.48), channel_id=1, source_target_pairs={{0,1},{1,0},{2,3},{3,2},{4,5},{5,4},{6,7},{7,6},{8,9},{9,8},{10,11... | collective-permute-start | bytes 12582920 | tf_op jit(solution)/shard_map/ppermute | solution.py:141
  27.9 3.2 %copy-start.2 = (f32[4,2,16,32,256]{4,3,2,1,0:T(8,128)}, f32[4,2,16,32,256]{4,3,2,1,0:T(8,128)S(1)}, u32[]{:S(2)}) copy-start(f32[4,2,16,32,256]{4,3,2,1,0:T(8,128)S(1)} %get-tuple-element.9) | copy-start | bytes 12582916
  31.1 57.3 %collective-permute-start.1 = (f32[4,2,16,32,256]{4,3,1,2,0:T(8,128)}, f32[4,2,16,32,256]{4,3,1,2,0:T(8,128)}, u32[]{:S(2)}, u32[]{:S(2)}) collective-permute-start(f32[4,2,16,32,256]{4,3,1,2,0:T(8,128)} %copy.43), channel_id=1, source_target_pairs={{0,1},{1,0},{2,3},{3,2},{4,5},{5,4},{6,7},{7,6},{8,9},{9,8},{10,11... | collective-permute-start | bytes 12582920 | tf_op jit(solution)/shard_map/ppermute | solution.py:141
  82.5 92.3 %collective-permute-start = (bf16[64,256,256]{2,1,0:T(8,128)(2,1)}, bf16[64,256,256]{2,1,0:T(8,128)(2,1)}, u32[]{:S(2)}, u32[]{:S(2)}) collective-permute-start(bf16[64,256,256]{2,1,0:T(8,128)(2,1)} %bitcast.58), channel_id=1, source_target_pairs={{0,1},{1,0},{2,3},{3,2},{4,5},{5,4},{6,7},{7,6},{8,9},{9,8},{10,11... | collective-permute-start | bytes 25165832 | tf_op jit(solution)/shard_map/ppermute | solution.py:141
  82.5 5.9 %copy-start.3 = (f32[4,2,16,32,256]{4,3,2,1,0:T(8,128)S(1)}, f32[4,2,16,32,256]{4,3,2,1,0:T(8,128)}, u32[]{:S(2)}) copy-start(f32[4,2,16,32,256]{4,3,2,1,0:T(8,128)} %copy-done.2) | copy-start | bytes 12582916
  86.3 11.4 %collective-permute-start.7 = (bf16[2,8,32,256]{3,2,0,1:T(8,128)(2,1)S(1)}, bf16[2,8,32,256]{3,2,0,1:T(8,128)(2,1)S(1)}, u32[]{:S(2)}, u32[]{:S(2)}) collective-permute-start(bf16[2,8,32,256]{3,2,0,1:T(8,128)(2,1)S(1)} %get-tuple-element.19), channel_id=1, source_target_pairs={{0,2},{1,3},{2,4},{3,5},{4,6},{5,7},{6,0},{7,1},{8,10},{9,11},{10,... | collective-permute-start | bytes 786440 | tf_op jit(solution)/shard_map/ppermute | solution.py:144
  86.9 10.4 %collective-permute-start.9 = (bf16[2,8,32,256]{3,2,0,1:T(8,128)(2,1)S(1)}, bf16[2,8,32,256]{3,2,0,1:T(8,128)(2,1)S(1)}, u32[]{:S(2)}, u32[]{:S(2)}) collective-permute-start(bf16[2,8,32,256]{3,2,0,1:T(8,128)(2,1)S(1)} %get-tuple-element.20), channel_id=1, source_target_pairs={{0,6},{1,7},{2,0},{3,1},{4,2},{5,3},{6,4},{7,5},{8,14},{9,15},{10,... | collective-permute-start | bytes 786440 | tf_op jit(solution)/shard_map/ppermute | solution.py:144
  91.7 11.2 %collective-permute-start.4 = (bf16[2,8,32,256]{3,2,0,1:T(8,128)(2,1)S(1)}, bf16[2,8,32,256]{3,2,0,1:T(8,128)(2,1)S(1)}, u32[]{:S(2)}, u32[]{:S(2)}) collective-permute-start(bf16[2,8,32,256]{3,2,0,1:T(8,128)(2,1)S(1)} %get-tuple-element.22), channel_id=1, source_target_pairs={{0,6},{1,7},{2,0},{3,1},{4,2},{5,3},{6,4},{7,5},{8,14},{9,15},{10,... | collective-permute-start | bytes 786440 | tf_op jit(solution)/shard_map/ppermute | solution.py:144
  97.4 16.7 %collective-permute-start.10 = (bf16[2,16,32,256]{3,2,0,1:T(8,128)(2,1)S(1)}, bf16[2,16,32,256]{3,2,0,1:T(8,128)(2,1)S(1)}, u32[]{:S(2)}, u32[]{:S(2)}) collective-permute-start(bf16[2,16,32,256]{3,2,0,1:T(8,128)(2,1)S(1)} %pad_maximum_fusion.3), channel_id=1, source_target_pairs={{0,6},{1,7},{2,0},{3,1},{4,2},{5,3},{6,4},{7,5},{8,14},{9,15},{10,... | collective-permute-start | bytes 1572872 | tf_op jit(solution)/shard_map/ppermute | solution.py:144
  97.9 16.2 %collective-permute-start.8 = (bf16[2,16,32,256]{3,2,0,1:T(8,128)(2,1)S(1)}, bf16[2,16,32,256]{3,2,0,1:T(8,128)(2,1)S(1)}, u32[]{:S(2)}, u32[]{:S(2)}) collective-permute-start(bf16[2,16,32,256]{3,2,0,1:T(8,128)(2,1)S(1)} %pad_maximum_fusion.2), channel_id=1, source_target_pairs={{0,2},{1,3},{2,4},{3,5},{4,6},{5,7},{6,0},{7,1},{8,10},{9,11},{10,... | collective-permute-start | bytes 1572872 | tf_op jit(solution)/shard_map/ppermute | solution.py:144
  101.0 21.3 %collective-permute-start.2 = (bf16[2,8,32,256]{3,2,0,1:T(8,128)(2,1)}, bf16[2,8,32,256]{3,2,0,1:T(8,128)(2,1)}, u32[]{:S(2)}, u32[]{:S(2)}) collective-permute-start(bf16[2,8,32,256]{3,2,0,1:T(8,128)(2,1)} %get-tuple-element.21), channel_id=1, source_target_pairs={{0,2},{1,3},{2,4},{3,5},{4,6},{5,7},{6,0},{7,1},{8,10},{9,11},{10,... | collective-permute-start | bytes 786440 | tf_op jit(solution)/shard_map/ppermute | solution.py:144
  103.0 23.4 %collective-permute-start.5 = (bf16[2,16,32,256]{3,2,0,1:T(8,128)(2,1)S(1)}, bf16[2,16,32,256]{3,2,0,1:T(8,128)(2,1)S(1)}, u32[]{:S(2)}, u32[]{:S(2)}) collective-permute-start(bf16[2,16,32,256]{3,2,0,1:T(8,128)(2,1)S(1)} %pad_maximum_fusion.1), channel_id=1, source_target_pairs={{0,6},{1,7},{2,0},{3,1},{4,2},{5,3},{6,4},{7,5},{8,14},{9,15},{10,... | collective-permute-start | bytes 1572872 | tf_op jit(solution)/shard_map/ppermute | solution.py:144
  117.0 21.7 %all-to-all-start.1 = ((f32[16,2,32,256]{3,2,1,0:T(8,128)}), f32[16,2,32,256]{3,2,1,0:T(8,128)S(1)}, u32[]{:S(2)}, u32[]{:S(2)}) async-start(f32[16,2,32,256]{3,2,1,0:T(8,128)} %fusion.6), calls=%async_computation.1 | async-start | bytes 2097152 | tf_op jit(solution)/shard_map/all_to_all | solution.py:178
  122.3 23.4 %copy-start.6 = (s32[4,16]{1,0:T(4,128)S(1)}, s32[4,16]{1,0:T(4,128)}, u32[]{:S(2)}) copy-start(s32[4,16]{1,0:T(4,128)} %param.8) | copy-start | bytes 772
  122.3 52.5 %copy-start.5 = (s32[64,256]{1,0:T(8,128)S(1)}, s32[64,256]{1,0:T(8,128)}, u32[]{:S(2)}) copy-start(s32[64,256]{1,0:T(8,128)} %mask_ref.3) | copy-start | bytes 196612
  123.4 12.3 %collective-permute-start.3 = (bf16[2,16,32,256]{3,2,0,1:T(8,128)(2,1)S(1)}, bf16[2,16,32,256]{3,2,0,1:T(8,128)(2,1)S(1)}, u32[]{:S(2)}, u32[]{:S(2)}) collective-permute-start(bf16[2,16,32,256]{3,2,0,1:T(8,128)(2,1)S(1)} %pad_maximum_fusion), channel_id=1, source_target_pairs={{0,2},{1,3},{2,4},{3,5},{4,6},{5,7},{6,0},{7,1},{8,10},{9,11},{10,... | collective-permute-start | bytes 1572872 | tf_op jit(solution)/shard_map/ppermute | solution.py:144
  138.7 44.9 %all-to-all-start = ((f32[16,2,32,256]{3,2,1,0:T(8,128)}), f32[16,2,32,256]{3,2,1,0:T(8,128)S(1)}, u32[]{:S(2)}, u32[]{:S(2)}) async-start(f32[16,2,32,256]{3,2,1,0:T(8,128)} %fusion.13), calls=%async_computation | async-start | bytes 2097152 | tf_op jit(solution)/shard_map/all_to_all | solution.py:178
  183.6 8.9 %copy-start.1 = (bf16[4,2,256,256]{3,2,1,0:T(8,128)(2,1)S(1)}, bf16[4,2,256,256]{3,2,1,0:T(8,128)(2,1)}, u32[]{:S(2)}) copy-start(bf16[4,2,256,256]{3,2,1,0:T(8,128)(2,1)} %param.6) | copy-start | bytes 3145732
Sparse Core Ops, SparseCore 0:
  9.5 72.9 all-gather.3

commit v2 on v0

v2 whole, which is shorter than its diff:
```python
import jax
import jax.numpy as jnp
from jax import lax
from jax.experimental import pallas as pl
from jax.experimental.pallas import tpu as pltpu
from jax.sharding import PartitionSpec as P

COUNT = 2
PAIR_TYPE = jnp.bfloat16
PIECE = 4
GROUP = 8
MIB = 1 << 20


def wide_rows(coef, wide):
    rows = lax.broadcasted_iota(jnp.int32, (128, 16), 0) // 8
    spread = (rows == lax.broadcasted_iota(jnp.int32, (128, 16), 1)).astype(jnp.bfloat16)
    cols = lax.broadcasted_iota(jnp.int32, (64, 512), 1) // 8
    across = (cols == lax.broadcasted_iota(jnp.int32, (64, 512), 0)).astype(jnp.bfloat16)
    same = lax.broadcasted_iota(jnp.int32, (128, 512), 0) % 8 == lax.broadcasted_iota(jnp.int32, (128, 512), 1) % 8
    tall = jnp.dot(spread, coef, preferred_element_type=jnp.float32).astype(jnp.bfloat16)
    full = jnp.dot(tall, across, preferred_element_type=jnp.float32)
    wide[...] = jnp.where(same, full, 0.0).astype(jnp.bfloat16)


def contract_occupied(coef, ints, first, got=None):
    def kernel(coef_ref, ints_ref, *rest):
        blocks, wide, sems = rest[-3:]
        refs = rest[:-3]

        def copy(c, p):
            return pltpu.make_async_copy(
                ints_ref.at[:, first + c, pl.ds(p * PIECE, PIECE)], blocks.at[c, p], sems.at[c, p]
            )

        for c in range(COUNT):
            for p in range(16 // PIECE):
                copy(c, p).start()
        for c in range(COUNT):
            wide_rows(coef_ref[first + c], wide.at[c])
        for c in range(COUNT):
            for p in range(16 // PIECE):
                copy(c, p).wait()
                for t in range(p * PIECE, p * PIECE + PIECE):
                    sums = jnp.dot(wide[c, :, :256], blocks[c, p, 0, t % PIECE], preferred_element_type=jnp.float32)
                    sums = sums + jnp.dot(
                        wide[c, :, 256:], blocks[c, p, 1, t % PIECE], preferred_element_type=jnp.float32
                    )
                    if got is None:
                        for d in range(4):
                            refs[0][d, t, c] = sums[32 * d : 32 * d + 32].astype(PAIR_TYPE)
                        continue
                    got_ref, own_ref, right_ref, left_ref, up_ref, down_ref = refs
                    total = [sums[32 * d : 32 * d + 32] + got_ref[d, t, c].astype(jnp.float32) for d in range(4)]
                    own_ref[t, c] = total[0]
                    if t < 8:
                        right_ref[t, c] = total[1]
                        up_ref[t, c] = total[2].astype(jnp.bfloat16)
                        down_ref[t, c] = total[3].astype(jnp.bfloat16)
                    else:
                        up_ref[t, c] = total[1].astype(jnp.bfloat16)
                        down_ref[t, c] = total[2].astype(jnp.bfloat16)
                        left_ref[t - 8, c] = total[3]

    vmem = pl.BlockSpec(memory_space=pltpu.VMEM)
    given, shapes = [coef, ints], [jax.ShapeDtypeStruct((4, 16, COUNT, 32, 256), PAIR_TYPE)]
    if got is not None:
        given.append(got)
        shapes = [
            jax.ShapeDtypeStruct((16, COUNT, 32, 256), jnp.float32),
            jax.ShapeDtypeStruct((8, COUNT, 32, 256), jnp.float32),
            jax.ShapeDtypeStruct((8, COUNT, 32, 256), jnp.float32),
            jax.ShapeDtypeStruct((16, COUNT, 32, 256), jnp.bfloat16),
            jax.ShapeDtypeStruct((16, COUNT, 32, 256), jnp.bfloat16),
        ]
    return pl.pallas_call(
        kernel,
        in_specs=[vmem, pl.BlockSpec(memory_space=pltpu.HBM)] + [vmem] * (len(given) - 2),
        out_specs=[vmem] * len(shapes),
        out_shape=shapes,
        scratch_shapes=[
            pltpu.VMEM((COUNT, 16 // PIECE, 2, PIECE, 256, 256), jnp.bfloat16),
            pltpu.VMEM((COUNT, 128, 512), jnp.bfloat16),
            pltpu.SemaphoreType.DMA((COUNT, 16 // PIECE)),
        ],
        compiler_params=pltpu.CompilerParams(vmem_limit_bytes=24 * MIB),
        cost_estimate=pl.CostEstimate(
            flops=COUNT * 16 * 2 * 128 * 512 * 256, bytes_accessed=COUNT * 16 * 300 * 1024, transcendentals=0
        ),
        name="contract_partner" if got is None else "contract_own",
    )(*given)


def code_sums(groups, table):
    def kernel(*refs):
        table_ref, out_ref = refs[-2], refs[-1]
        lane = lax.broadcasted_iota(jnp.int32, (16, 256), 1)
        for t in range(16):
            extra = jnp.zeros((16, 256), jnp.int32)
            for k in range(4):
                own, right, left, up, down = refs[5 * (k // COUNT) : 5 * (k // COUNT) + 5]
                c = k % COUNT
                sums = own[t, c] + (down if t < 8 else up)[t, c].astype(jnp.float32)
                sums = sums + (right[t, c] if t < 8 else left[t - 8, c]).astype(jnp.float32)
                most = jnp.max(jnp.max(jnp.abs(sums), axis=0, keepdims=True), axis=1, keepdims=True)
                power = jnp.floor(jnp.log2(jnp.maximum(most, 1e-30))) + 1.0
                coded = jnp.floor(sums * jnp.exp2(14.5 - power) + 0.5).astype(jnp.int32)
                out_ref[t, 32 * k : 32 * k + 32] = coded.astype(jnp.int16)
                extra = jnp.where(lane == k, table_ref[k, t], extra)
                extra = jnp.where(lane == 4 + k, power.astype(jnp.int32), extra)
            out_ref[t, 128:144] = extra.astype(jnp.int16)

    vmem = pl.BlockSpec(memory_space=pltpu.VMEM)
    given = [x for group in groups for x in group]
    return pl.pallas_call(
        kernel,
        in_specs=[vmem] * len(given) + [pl.BlockSpec(memory_space=pltpu.SMEM)],
        out_specs=vmem,
        out_shape=jax.ShapeDtypeStruct((16, 144, 256), jnp.int16),
        compiler_params=pltpu.CompilerParams(vmem_limit_bytes=24 * MIB),
        name="code_sums",
    )(*given, table)


def contract_virtual(k4, scales, mask, held, u, pair):
    def kernel(k4_ref, scale_ref, mask_ref, held_ref, u_ref, pair_ref, mine_ref, theirs_ref, own, rows, sems):
        def copy(k):
            return pltpu.make_async_copy(held_ref.at[k4_ref[k]], own.at[k], sems.at[k])

        @pl.loop(0, 64)
        def _(k):
            copy(k).start()

        @pl.loop(0, 16)
        def _(j):
            for h, ref in enumerate((u_ref, pair_ref)):
                for c in range(4):
                    full = ref[j, 32 * c : 32 * c + 32].astype(jnp.int32).astype(jnp.float32) * scale_ref[h, 4 * j + c]
                    high = full.astype(jnp.bfloat16)
                    low = (full - high.astype(jnp.float32)).astype(jnp.bfloat16)
                    rows[4 * j + c, 32 * h : 32 * h + 32] = high
                    rows[4 * j + c, 64 + 32 * h : 96 + 32 * h] = low

        @pl.loop(0, 64 // GROUP)
        def _(g):
            for i in range(GROUP):
                copy(g * GROUP + i).wait()
            all_got = []
            for i in range(GROUP):
                k = g * GROUP + i
                both = jnp.concatenate([own[k, 0], own[k, 1]], axis=1)
                all_got.append(jnp.dot(rows[k], both, preferred_element_type=jnp.float32))
            for i in range(GROUP):
                k = g * GROUP + i
                got = all_got[i][:64] + all_got[i][64:]
                keep = mask_ref[pl.ds(k4_ref[k], 1), :]
                for r, ref in ((0, mine_ref), (32, theirs_ref)):
                    ref[0, k] = (got[r : r + 16, :128] - got[r + 16 : r + 32, 128:]) * keep
                    ref[1, k] = (got[r : r + 16, 128:] + got[r + 16 : r + 32, :128]) * keep

    result = jax.ShapeDtypeStruct((2, 64, 16, 128), jnp.float32)
    vmem = pl.BlockSpec(memory_space=pltpu.VMEM)
    return pl.pallas_call(
        kernel,
        in_specs=[pl.BlockSpec(memory_space=pltpu.SMEM)] * 2 + [vmem, pl.BlockSpec(memory_space=pltpu.HBM), vmem, vmem],
        out_specs=[vmem, vmem],
        out_shape=[result, result],
        scratch_shapes=[
            pltpu.VMEM((64, 2, 256, 128), jnp.bfloat16),
            pltpu.VMEM((64, 128, 256), jnp.bfloat16),
            pltpu.SemaphoreType.DMA((64,)),
        ],
        compiler_params=pltpu.CompilerParams(vmem_limit_bytes=24 * MIB),
        cost_estimate=pl.CostEstimate(flops=64 * 2 * 128 * 256 * 256, bytes_accessed=64 * 200 * 1024, transcendentals=0),
        name="contract_virtual",
    )(k4, scales, mask, held, u, pair)


def per_device(ints, vir_coef, occ_coef, k4_table, band_mask):
    mom, band = lax.axis_index("mom"), lax.axis_index("band")
    core, y = band % 2, band // 2

    def across(x):
        return lax.ppermute(x, "band", [(i, i ^ 1) for i in range(8)])

    def along(x, d):
        return lax.ppermute(x, "band", [(i, (i // 2 + d) % 4 * 2 + i % 2) for i in range(8)])

    half = lax.dynamic_slice_in_dim(vir_coef, 128 * core, 128, axis=3)
    held = pltpu.with_memory_space_constraint(lax.all_gather(half, "mom", axis=0, tiled=True), pltpu.HBM)
    mask = lax.dynamic_slice_in_dim(band_mask, 128 * core, 128, axis=1).astype(jnp.float32)

    occ = lax.dynamic_slice_in_dim(occ_coef, 4 * mom, 4, axis=0)
    order = (
        2 * ((core + jnp.arange(2)[:, None, None]) % 2)
        + 4 * ((y + jnp.arange(4)[None, :, None]) % 4)
        + jnp.arange(2)[None, None, :]
    ).reshape(16)
    occ = jnp.take(occ, order, axis=3).reshape(4, 2, 32, 8, 2)
    parts = jnp.stack([jnp.stack([occ[:, 0], -occ[:, 1]], 1), jnp.stack([occ[:, 1], occ[:, 0]], 1)], 1)
    coef = parts.transpose(0, 4, 1, 5, 2, 3).reshape(4, 2, 16, 64)
    coef_own, coef_partner = coef[:, 0], coef[:, 1]

    ints = pltpu.with_memory_space_constraint(ints.reshape(2, 4, 16, 256, 256), pltpu.HBM)
    chunks = range(0, 4, COUNT)
    arrived = [across(contract_occupied(coef_partner, ints, first)[0]) for first in chunks]
    sent = []
    for first, got in zip(chunks, arrived):
        own, right, left, up, down = contract_occupied(coef_own, ints, first, got)
        sent.append((own, right, left, along(up, 1), along(down, -1)))
    groups = []
    for own, right, left, up, down in sent:
        right = along((right + up[:8].astype(jnp.float32)).astype(jnp.bfloat16), 1)
        left = along((left + down[8:].astype(jnp.float32)).astype(jnp.bfloat16), -1)
        groups.append((own, right, left, up, down))
    coded = code_sums(groups, k4_table)
    u = lax.all_to_all(coded, "mom", split_axis=0, concat_axis=0, tiled=True)
    pair = across(u)
    k4 = u[:, 128, :4].astype(jnp.int32).reshape(64)
    powers = jnp.stack([u[:, 128, 4:8], pair[:, 128, 4:8]]).astype(jnp.float32).reshape(2, 64)
    mine, theirs = contract_virtual(k4, jnp.exp2(powers - 14.5), mask, held, u, pair)
    theirs = across(theirs)
    first = jnp.where(core == 0, mine, theirs)
    second = jnp.where(core == 0, theirs, mine)
    return jnp.concatenate([first, second], axis=-1).reshape(2, 64, 1, 2, 8, 256)


def solution(mesh):
    placed = (
        P(None, "mom", None, "band", None, None),
        P("mom", None, None, None),
        P(None, None, "band", None),
        P("mom", None),
        P(),
    )
    return jax.shard_map(
        per_device,
        mesh=mesh,
        in_specs=placed,
        out_specs=P(None, None, "mom", "band", None, None),
        check_vma=False,
    )
```

time: 719 us -> 122 us (0.17)
  waiting for transfers between devices: 493 us -> 26.4 us
  local copies, waits for them, and re-layouts: 88 us -> 5.87 us
  matrix products: 80 us -> 0 us
  other arithmetic: 38.1 us -> 3.98 us
  blocking collectives: 0 us -> 33.5 us
  Pallas kernels: 0 us -> 23.6 us
  starting transfers between devices: 5.5 us -> 14.2 us
    all_to_all x1 -> x0, waiting for transfers between devices: 291 us -> none  [per_device(): moved = lax.all_to_all(half, 'mom', split_axis=2, concat_axis=1, tiled=True)]
    all_gather x1, waiting for transfers between devices: 103 us -> 0.02 us  [per_device(): lax.all_gather(half, 'mom', axis=0, tiled=True)]
    reduce_scatter x1 -> x0, waiting for transfers between devices: 98.6 us -> none  [per_device(): lax.psum_scatter(partial_sum, 'band', scatter_dimension=3, tiled=True)]
    dot_general x8 -> x0, matrix products: 80 us -> none  [the longest x1 15.3 us: per_device(): jnp.einsum(form, ints[1], col_real, preferred_element_type=jnp.float32)]
    all_to_all x0 -> x1, blocking collectives: none -> 33.5 us  [per_device(): u = lax.all_to_all(coded, 'mom', split_axis=0, concat_axis=0, tiled=True)]
    ppermute x0 -> x12, waiting for transfers between devices: none -> 26.4 us  [the longest x8 21.8 us: along(): lax.ppermute(x, 'band', [(i, (i // 2 + d) % 4 * 2 + i % 2) for i in range...]
    another operation x2, local copies, waits for them, and re-layouts: 26.1 us -> 0.2 us  [per_device(): jnp.stack([u[:, 128, 4:8], pair[:, 128, 4:8]]).astype(jnp.float32)]
    pallas_call x0 -> x6, Pallas kernels: none -> 23.6 us  [the longest x4 16 us: contract_occupied(): pl.pallas_call(kernel, in_specs=[vmem, pl.BlockSpec(memory_space=pltpu.HB...]
  transfers between devices with their start and end apart: 3 -> 13, of which waited for: 3 -> 6; matrix products, arithmetic and copies ran while one was open for 2% -> 3% of each run, Pallas kernels for 0% -> 14%
where the time goes in v2:
time: 122 us; the launch traced here: 121 us
  blocking collectives  33.5 us (27%)
  waiting for transfers between devices  26.4 us (22%)
  Pallas kernels  23.6 us (19%)
  starting transfers between devices  14.2 us (12%)
  between operations  13.6 us (11%)
  local copies, waits for them, and re-layouts  5.87 us (5%)
  other arithmetic  3.98 us (3%)
    all_to_all x1, blocking collectives, per_device(): u = lax.all_to_all(coded, 'mom', split_axis=0, concat_axis=0, tiled=True)  33.5 us
    ppermute x8, waiting for transfers between devices, along(): lax.ppermute(x, 'band', [(i, (i // 2 + d) % 4 * 2 + i % 2) for i in range...  21.8 us
    pallas_call x4, Pallas kernels, contract_occupied(): pl.pallas_call(kernel, in_specs=[vmem, pl.BlockSpec(memory_space=pltpu.HB...  16 us
    ppermute x8, starting transfers between devices, along(): lax.ppermute(x, 'band', [(i, (i // 2 + d) % 4 * 2 + i % 2) for i in range...  10.6 us
    pallas_call x1, Pallas kernels, contract_virtual(): pl.pallas_call(kernel, in_specs=[pl.BlockSpec(memory_space=pltpu.SMEM)] *...  6.15 us
    ppermute x4, waiting for transfers between devices, across(): return lax.ppermute(x, 'band', [(i, i ^ 1) for i in range(8)])  4.64 us
    ppermute x4, starting transfers between devices, across(): return lax.ppermute(x, 'band', [(i, i ^ 1) for i in range(8)])  3.59 us
    unnamed x9, local copies, waits for them, and re-layouts  2.54 us
  transfers between devices with their start and end apart: 13, of which 6 were waited for; matrix products, arithmetic and copies ran while one was open for 3% of the time, Pallas kernels for 14%

profile of v2, /device:TPU:1, one launch (start us, length us, event | category | flops | bytes accessed | tf_op | source)
XLA Modules:
  0.0 121.2 jit_solution(16256824739160399829)
XLA Ops:
  6.5 1.2 %copy-done = bf16[4,2,256,256]{3,2,1,0:T(8,128)(2,1)S(1)} copy-done((bf16[4,2,256,256]{3,2,1,0:T(8,128)(2,1)S(1)}, bf16[4,2,256,256]{3,2,1,0:T(8,128)(2,1)}, u32[]{:S(2)}) %copy-start) | copy-done | bytes 1048600
  9.0 1.1 constant_dynamic-slice_fusion.1
  11.8 3.8 %contract_partner.3 = bf16[4,16,2,32,256]{4,3,2,1,0:T(8,128)(2,1)S(1)} custom-call(bf16[4,16,64]{2,1,0:T(8,128)(2,1)S(1)} %get-tuple-element.31.coef_ref, bf16[2,4,16,256,256]{4,3,2,1,0:T(8,128)(2,1)} %bitcast.26), custom_call_target="tpu_custom_call" | custom-call | flops 1073741824 | bytes 9830400 | tf_op jit(solution)/shard_map/contract_partner/pallas_call | solution.py:76
  15.6 1.5 %collective-permute-start.5 = (bf16[4,16,2,32,256]{4,3,2,1,0:T(8,128)(2,1)S(1)}, bf16[4,16,2,32,256]{4,3,2,1,0:T(8,128)(2,1)S(1)}, u32[]{:S(2)}, u32[]{:S(2)}) collective-permute-start(bf16[4,16,2,32,256]{4,3,2,1,0:T(8,128)(2,1)S(1)} %contract_partner.3), channel_id=1, source_target_pairs={{0,1},{1,0},{2,3},{3,2},{4,5},{5,4},{6,7},{7,6},{8,9},{9,8},{10,11... | collective-permute-start | bytes 6291464 | tf_op jit(solution)/shard_map/ppermute | solution.py:184
  17.1 3.8 %contract_partner.2 = bf16[4,16,2,32,256]{4,3,2,1,0:T(8,128)(2,1)S(1)} custom-call(bf16[4,16,64]{2,1,0:T(8,128)(2,1)S(1)} %get-tuple-element.31.coef_ref, bf16[2,4,16,256,256]{4,3,2,1,0:T(8,128)(2,1)} %bitcast.27), custom_call_target="tpu_custom_call" | custom-call | flops 1073741824 | bytes 9830400 | tf_op jit(solution)/shard_map/contract_partner/pallas_call | solution.py:76
  21.1 4.3 %contract_own.3 = (f32[16,2,32,256]{3,2,1,0:T(8,128)S(1)}, f32[8,2,32,256]{3,2,1,0:T(8,128)S(1)}, f32[8,2,32,256]{3,2,1,0:T(8,128)S(1)}, bf16[16,2,32,256]{3,2,1...) custom-call(bf16[4,16,64]{2,1,0:T(8,128)(2,1)S(1)} %get-tuple-element.32.coef_ref, bf16[2,4,16,256,256]{4,3,2,1,0:T(8,128)(2,1)} %bitcast.28, ...), custom_call_target="tpu_custom_call" | custom-call | flops 1073741824 | bytes 9830400 | tf_op jit(solution)/shard_map/contract_own/pallas_call | solution.py:76
  25.4 1.5 %collective-permute-start.6 = (bf16[16,2,32,256]{3,2,1,0:T(8,128)(2,1)S(1)}, bf16[16,2,32,256]{3,2,1,0:T(8,128)(2,1)S(1)}, u32[]{:S(2)}, u32[]{:S(2)}) collective-permute-start(bf16[16,2,32,256]{3,2,1,0:T(8,128)(2,1)S(1)} %get-tuple-element.24), channel_id=1, source_target_pairs={{0,2},{1,3},{2,4},{3,5},{4,6},{5,7},{6,0},{7,1},{8,10},{9,11},{10,... | collective-permute-start | bytes 1572872 | tf_op jit(solution)/shard_map/ppermute | solution.py:187
  26.8 1.5 %collective-permute-start.8 = (bf16[16,2,32,256]{3,2,1,0:T(8,128)(2,1)S(1)}, bf16[16,2,32,256]{3,2,1,0:T(8,128)(2,1)S(1)}, u32[]{:S(2)}, u32[]{:S(2)}) collective-permute-start(bf16[16,2,32,256]{3,2,1,0:T(8,128)(2,1)S(1)} %get-tuple-element.26), channel_id=1, source_target_pairs={{0,6},{1,7},{2,0},{3,1},{4,2},{5,3},{6,4},{7,5},{8,14},{9,15},{10,... | collective-permute-start | bytes 1572872 | tf_op jit(solution)/shard_map/ppermute | solution.py:187
  28.4 4.0 %contract_own.2 = (f32[16,2,32,256]{3,2,1,0:T(8,128)S(1)}, f32[8,2,32,256]{3,2,1,0:T(8,128)S(1)}, f32[8,2,32,256]{3,2,1,0:T(8,128)S(1)}, bf16[16,2,32,256]{3,2,1...) custom-call(bf16[4,16,64]{2,1,0:T(8,128)(2,1)S(1)} %get-tuple-element.32.coef_ref, bf16[2,4,16,256,256]{4,3,2,1,0:T(8,128)(2,1)} %bitcast.29, ...), custom_call_target="tpu_custom_call" | custom-call | flops 1073741824 | bytes 9830400 | tf_op jit(solution)/shard_map/contract_own/pallas_call | solution.py:76
  32.3 1.4 %collective-permute-start.3 = (bf16[16,2,32,256]{3,2,1,0:T(8,128)(2,1)S(1)}, bf16[16,2,32,256]{3,2,1,0:T(8,128)(2,1)S(1)}, u32[]{:S(2)}, u32[]{:S(2)}) collective-permute-start(bf16[16,2,32,256]{3,2,1,0:T(8,128)(2,1)S(1)} %get-tuple-element.21), channel_id=1, source_target_pairs={{0,6},{1,7},{2,0},{3,1},{4,2},{5,3},{6,4},{7,5},{8,14},{9,15},{10,... | collective-permute-start | bytes 1572872 | tf_op jit(solution)/shard_map/ppermute | solution.py:187
  33.9 6.1 %collective-permute-done.6.refs_8_ = bf16[16,2,32,256]{3,2,1,0:T(8,128)(2,1)S(1)} collective-permute-done((bf16[16,2,32,256]{3,2,1,0:T(8,128)(2,1)S(1)}, bf16[16,2,32,256]{3,2,1,0:T(8,128)(2,1)S(1)}, u32[]{:S(2)}, u32[]{:S(2)}) %collective-permute-start.6) | collective-permute-done | bytes 524320 | tf_op jit(solution)/shard_map/ppermute | solution.py:187
  40.2 2.7 %collective-permute-start.9 = (bf16[8,2,32,256]{3,2,1,0:T(8,128)(2,1)S(1)}, bf16[8,2,32,256]{3,2,1,0:T(8,128)(2,1)S(1)}, u32[]{:S(2)}, u32[]{:S(2)}) collective-permute-start(bf16[8,2,32,256]{3,2,1,0:T(8,128)(2,1)S(1)} %add_convert_fusion), channel_id=1, source_target_pairs={{0,6},{1,7},{2,0},{3,1},{4,2},{5,3},{6,4},{7,5},{8,14},{9,15},{10,... | collective-permute-start | bytes 786440 | tf_op jit(solution)/shard_map/ppermute | solution.py:187
  43.0 7.9 %collective-permute-done.3.refs_4_ = bf16[16,2,32,256]{3,2,1,0:T(8,128)(2,1)S(1)} collective-permute-done((bf16[16,2,32,256]{3,2,1,0:T(8,128)(2,1)S(1)}, bf16[16,2,32,256]{3,2,1,0:T(8,128)(2,1)S(1)}, u32[]{:S(2)}, u32[]{:S(2)}) %collective-permute-start.3) | collective-permute-done | bytes 524320 | tf_op jit(solution)/shard_map/ppermute | solution.py:187
  50.9 3.2 %collective-permute-start.4 = (bf16[8,2,32,256]{3,2,1,0:T(8,128)(2,1)S(1)}, bf16[8,2,32,256]{3,2,1,0:T(8,128)(2,1)S(1)}, u32[]{:S(2)}, u32[]{:S(2)}) collective-permute-start(bf16[8,2,32,256]{3,2,1,0:T(8,128)(2,1)S(1)} %add_convert_fusion.2), channel_id=1, source_target_pairs={{0,6},{1,7},{2,0},{3,1},{4,2},{5,3},{6,4},{7,5},{8,14},{9,15},{10,... | collective-permute-start | bytes 786440 | tf_op jit(solution)/shard_map/ppermute | solution.py:187
  54.3 2.6 %collective-permute-done.7.refs_6_ = bf16[8,2,32,256]{3,2,1,0:T(8,128)(2,1)S(1)} collective-permute-done((bf16[8,2,32,256]{3,2,1,0:T(8,128)(2,1)S(1)}, bf16[8,2,32,256]{3,2,1,0:T(8,128)(2,1)S(1)}, u32[]{:S(2)}, u32[]{:S(2)}) %collective-permute-start.7) | collective-permute-done | bytes 262176 | tf_op jit(solution)/shard_map/ppermute | solution.py:187
  56.9 5.2 %collective-permute-done.4.refs_2_ = bf16[8,2,32,256]{3,2,1,0:T(8,128)(2,1)S(1)} collective-permute-done((bf16[8,2,32,256]{3,2,1,0:T(8,128)(2,1)S(1)}, bf16[8,2,32,256]{3,2,1,0:T(8,128)(2,1)S(1)}, u32[]{:S(2)}, u32[]{:S(2)}) %collective-permute-start.4) | collective-permute-done | bytes 262176 | tf_op jit(solution)/shard_map/ppermute | solution.py:187
  62.1 1.5 %code_sums.1 = s16[16,144,256]{2,1,0:T(8,128)(2,1)S(1)} custom-call(f32[16,2,32,256]{3,2,1,0:T(8,128)S(1)} %get-tuple-element.17.refs_0_, bf16[8,2,32,256]{3,2,1,0:T(8,128)(2,1)S(1)} %collective-permute-done.2.refs_1_, bf16[8,2,32,256]{3,2,1,0:T(8,128)(2,1)S(1)} %collective-permute-done.4.refs_2_, ...), custom_call_target="tpu_custom_call" | custom-call | tf_op jit(solution)/shard_map/code_sums/pallas_call | solution.py:115
  63.6 33.5 %all_to_all.5.u_ref = s16[16,144,256]{2,1,0:T(8,128)(2,1)S(1)} all-to-all(s16[16,144,256]{2,1,0:T(8,128)(2,1)S(1)} %code_sums.1), channel_id=1, replica_groups=mesh['mom'=16,'band'=8] {'mom'}, dimensions={0} | all-to-all | bytes 2359296 | tf_op jit(solution)/shard_map/all_to_all | solution.py:217
  97.1 1.6 %collective-permute-start.10 = (s16[16,144,256]{2,1,0:T(8,128)(2,1)S(1)}, s16[16,144,256]{2,1,0:T(8,128)(2,1)S(1)}, u32[]{:S(2)}, u32[]{:S(2)}) collective-permute-start(s16[16,144,256]{2,1,0:T(8,128)(2,1)S(1)} %all_to_all.5.u_ref), channel_id=1, source_target_pairs={{0,1},{1,0},{2,3},{3,2},{4,5},{5,4},{6,7},{7,6},{8,9},{9,8},{10,11... | collective-permute-start | bytes 3538952 | tf_op jit(solution)/shard_map/ppermute | solution.py:184
  99.1 2.1 %collective-permute-done.10.pair_ref = s16[16,144,256]{2,1,0:T(8,128)(2,1)S(1)} collective-permute-done((s16[16,144,256]{2,1,0:T(8,128)(2,1)S(1)}, s16[16,144,256]{2,1,0:T(8,128)(2,1)S(1)}, u32[]{:S(2)}, u32[]{:S(2)}) %collective-permute-start.10) | collective-permute-done | bytes 1179680 | tf_op jit(solution)/shard_map/ppermute | solution.py:184
  101.5 6.1 %contract_virtual.1 = (f32[2,64,16,128]{3,2,1,0:T(8,128)S(1)}, f32[2,64,16,128]{3,2,1,0:T(8,128)}) custom-call(s32[64]{0:T(128)S(1)} %reshape.148.k4_ref, f32[2,64]{1,0:T(2,128)S(1)} %multiply_exponential_fusion.scale_ref, f32[64,128]{1,0:T(8,128)S(1)} %dynamic-slice_convert_fusion.mask_ref, bf16[64,2,256,128]{3,2,1,0:T(8,128)(2,1)} %all-gather.2.cloned.1.call-done.held_ref, ...), custom_call_target="tpu_custom_call" | custom-call | flops 1073741824 | bytes 13107200 | tf_op jit(solution)/shard_map/contract_virtual/pallas_call | solution.py:163
  109.0 2.5 %collective-permute-done.11 = f32[2,64,16,128]{3,2,1,0:T(8,128)S(1)} collective-permute-done((f32[2,64,16,128]{3,2,1,0:T(8,128)}, f32[2,64,16,128]{3,2,1,0:T(8,128)S(1)}, u32[]{:S(2)}, u32[]{:S(2)}) %collective-permute-start.11) | collective-permute-done | bytes 1048608 | tf_op jit(solution)/shard_map/ppermute | solution.py:184
  111.5 1.4 %broadcast_select_fusion.1 = (f32[2,64,16,128]{3,2,1,0:T(8,128)S(1)}, f32[2,64,16,128]{3,2,1,0:T(8,128)S(1)}) fusion(f32[2,64,16,128]{3,2,1,0:T(8,128)} %copy-done.1, f32[2,64,16,128]{3,2,1,0:T(8,128)S(1)} %collective-permute-done.11, pred[]{:T(512)S(6)} %eq.10), kind=kLoop, calls=%fused_computation.7 | loop fusion | flops 524288 | bytes 4194305 | tf_op jit(solution)/shard_map/jit(_where)/select_n | solution.py:223
  112.9 1.5 %maximum_bitcast_fusion = f32[2,64,1,2,8,256]{5,4,3,2,1,0:T(8,128)} fusion(f32[2,64,16,128]{3,2,1,0:T(8,128)S(1)} %get-tuple-element.30, f32[2,64,16,128]{3,2,1,0:T(8,128)S(1)} %get-tuple-element.29), kind=kLoop, calls=%fused_computation.1 | loop fusion | flops 524288 | bytes 4194304 | tf_op jit(solution)/shard_map/reshape | solution.py:225
  (51 shorter events, 5.4 us)
Async XLA Ops:
  6.5 1.2 %copy-start = (bf16[4,2,256,256]{3,2,1,0:T(8,128)(2,1)S(1)}, bf16[4,2,256,256]{3,2,1,0:T(8,128)(2,1)}, u32[]{:S(2)}) copy-start(bf16[4,2,256,256]{3,2,1,0:T(8,128)(2,1)} %param.6) | copy-start | bytes 3145732
  6.5 94.9 %all-gather.2.cloned.1.call-start = ((), (), s32[]{:S(2)}) async-start(), calls=%async_computation.1 | async-start | bytes 8912896 | tf_op jit(solution)/shard_map/all_gather | solution.py:190
  15.6 5.4 %collective-permute-start.5 = (bf16[4,16,2,32,256]{4,3,2,1,0:T(8,128)(2,1)S(1)}, bf16[4,16,2,32,256]{4,3,2,1,0:T(8,128)(2,1)S(1)}, u32[]{:S(2)}, u32[]{:S(2)}) collective-permute-start(bf16[4,16,2,32,256]{4,3,2,1,0:T(8,128)(2,1)S(1)} %contract_partner.3), channel_id=1, source_target_pairs={{0,1},{1,0},{2,3},{3,2},{4,5},{5,4},{6,7},{7,6},{8,9},{9,8},{10,11... | collective-permute-start | bytes 6291464 | tf_op jit(solution)/shard_map/ppermute | solution.py:184
  21.0 7.4 %collective-permute-start = (bf16[4,16,2,32,256]{4,3,2,1,0:T(8,128)(2,1)S(1)}, bf16[4,16,2,32,256]{4,3,2,1,0:T(8,128)(2,1)S(1)}, u32[]{:S(2)}, u32[]{:S(2)}) collective-permute-start(bf16[4,16,2,32,256]{4,3,2,1,0:T(8,128)(2,1)S(1)} %contract_partner.2), channel_id=1, source_target_pairs={{0,1},{1,0},{2,3},{3,2},{4,5},{5,4},{6,7},{7,6},{8,9},{9,8},{10,11... | collective-permute-start | bytes 6291464 | tf_op jit(solution)/shard_map/ppermute | solution.py:184
  25.4 14.6 %collective-permute-start.6 = (bf16[16,2,32,256]{3,2,1,0:T(8,128)(2,1)S(1)}, bf16[16,2,32,256]{3,2,1,0:T(8,128)(2,1)S(1)}, u32[]{:S(2)}, u32[]{:S(2)}) collective-permute-start(bf16[16,2,32,256]{3,2,1,0:T(8,128)(2,1)S(1)} %get-tuple-element.24), channel_id=1, source_target_pairs={{0,2},{1,3},{2,4},{3,5},{4,6},{5,7},{6,0},{7,1},{8,10},{9,11},{10,... | collective-permute-start | bytes 1572872 | tf_op jit(solution)/shard_map/ppermute | solution.py:187
  26.8 13.3 %collective-permute-start.8 = (bf16[16,2,32,256]{3,2,1,0:T(8,128)(2,1)S(1)}, bf16[16,2,32,256]{3,2,1,0:T(8,128)(2,1)S(1)}, u32[]{:S(2)}, u32[]{:S(2)}) collective-permute-start(bf16[16,2,32,256]{3,2,1,0:T(8,128)(2,1)S(1)} %get-tuple-element.26), channel_id=1, source_target_pairs={{0,6},{1,7},{2,0},{3,1},{4,2},{5,3},{6,4},{7,5},{8,14},{9,15},{10,... | collective-permute-start | bytes 1572872 | tf_op jit(solution)/shard_map/ppermute | solution.py:187
  32.3 18.5 %collective-permute-start.3 = (bf16[16,2,32,256]{3,2,1,0:T(8,128)(2,1)S(1)}, bf16[16,2,32,256]{3,2,1,0:T(8,128)(2,1)S(1)}, u32[]{:S(2)}, u32[]{:S(2)}) collective-permute-start(bf16[16,2,32,256]{3,2,1,0:T(8,128)(2,1)S(1)} %get-tuple-element.21), channel_id=1, source_target_pairs={{0,6},{1,7},{2,0},{3,1},{4,2},{5,3},{6,4},{7,5},{8,14},{9,15},{10,... | collective-permute-start | bytes 1572872 | tf_op jit(solution)/shard_map/ppermute | solution.py:187
  33.8 20.4 %collective-permute-start.1 = (bf16[16,2,32,256]{3,2,1,0:T(8,128)(2,1)S(1)}, bf16[16,2,32,256]{3,2,1,0:T(8,128)(2,1)S(1)}, u32[]{:S(2)}, u32[]{:S(2)}) collective-permute-start(bf16[16,2,32,256]{3,2,1,0:T(8,128)(2,1)S(1)} %get-tuple-element.19), channel_id=1, source_target_pairs={{0,2},{1,3},{2,4},{3,5},{4,6},{5,7},{6,0},{7,1},{8,10},{9,11},{10,... | collective-permute-start | bytes 1572872 | tf_op jit(solution)/shard_map/ppermute | solution.py:187
  40.0 22.1 %copy-start.2 = (s32[4,16]{1,0:T(4,128)S(1)}, s32[4,16]{1,0:T(4,128)}, u32[]{:S(2)}) copy-start(s32[4,16]{1,0:T(4,128)} %refs_10_.1) | copy-start | bytes 772
  40.1 16.9 %collective-permute-start.7 = (bf16[8,2,32,256]{3,2,1,0:T(8,128)(2,1)S(1)}, bf16[8,2,32,256]{3,2,1,0:T(8,128)(2,1)S(1)}, u32[]{:S(2)}, u32[]{:S(2)}) collective-permute-start(bf16[8,2,32,256]{3,2,1,0:T(8,128)(2,1)S(1)} %add_convert_fusion.1), channel_id=1, source_target_pairs={{0,2},{1,3},{2,4},{3,5},{4,6},{5,7},{6,0},{7,1},{8,10},{9,11},{10,... | collective-permute-start | bytes 786440 | tf_op jit(solution)/shard_map/ppermute | solution.py:187
  40.2 16.7 %collective-permute-start.9 = (bf16[8,2,32,256]{3,2,1,0:T(8,128)(2,1)S(1)}, bf16[8,2,32,256]{3,2,1,0:T(8,128)(2,1)S(1)}, u32[]{:S(2)}, u32[]{:S(2)}) collective-permute-start(bf16[8,2,32,256]{3,2,1,0:T(8,128)(2,1)S(1)} %add_convert_fusion), channel_id=1, source_target_pairs={{0,6},{1,7},{2,0},{3,1},{4,2},{5,3},{6,4},{7,5},{8,14},{9,15},{10,... | collective-permute-start | bytes 786440 | tf_op jit(solution)/shard_map/ppermute | solution.py:187
  50.9 11.2 %collective-permute-start.4 = (bf16[8,2,32,256]{3,2,1,0:T(8,128)(2,1)S(1)}, bf16[8,2,32,256]{3,2,1,0:T(8,128)(2,1)S(1)}, u32[]{:S(2)}, u32[]{:S(2)}) collective-permute-start(bf16[8,2,32,256]{3,2,1,0:T(8,128)(2,1)S(1)} %add_convert_fusion.2), channel_id=1, source_target_pairs={{0,6},{1,7},{2,0},{3,1},{4,2},{5,3},{6,4},{7,5},{8,14},{9,15},{10,... | collective-permute-start | bytes 786440 | tf_op jit(solution)/shard_map/ppermute | solution.py:187
  54.3 7.8 %collective-permute-start.2 = (bf16[8,2,32,256]{3,2,1,0:T(8,128)(2,1)S(1)}, bf16[8,2,32,256]{3,2,1,0:T(8,128)(2,1)S(1)}, u32[]{:S(2)}, u32[]{:S(2)}) collective-permute-start(bf16[8,2,32,256]{3,2,1,0:T(8,128)(2,1)S(1)} %add_convert_fusion.3), channel_id=1, source_target_pairs={{0,2},{1,3},{2,4},{3,5},{4,6},{5,7},{6,0},{7,1},{8,10},{9,11},{10,... | collective-permute-start | bytes 786440 | tf_op jit(solution)/shard_map/ppermute | solution.py:187
  63.6 35.2 %copy-start.3 = (s32[64,256]{1,0:T(8,128)S(1)}, s32[64,256]{1,0:T(8,128)}, u32[]{:S(2)}) copy-start(s32[64,256]{1,0:T(8,128)} %param.9) | copy-start | bytes 196612
  97.1 4.1 %collective-permute-start.10 = (s16[16,144,256]{2,1,0:T(8,128)(2,1)S(1)}, s16[16,144,256]{2,1,0:T(8,128)(2,1)S(1)}, u32[]{:S(2)}, u32[]{:S(2)}) collective-permute-start(s16[16,144,256]{2,1,0:T(8,128)(2,1)S(1)} %all_to_all.5.u_ref), channel_id=1, source_target_pairs={{0,1},{1,0},{2,3},{3,2},{4,5},{5,4},{6,7},{7,6},{8,9},{9,8},{10,11... | collective-permute-start | bytes 3538952 | tf_op jit(solution)/shard_map/ppermute | solution.py:184
  107.6 1.0 copy-start.1
  108.6 2.9 %collective-permute-start.11 = (f32[2,64,16,128]{3,2,1,0:T(8,128)}, f32[2,64,16,128]{3,2,1,0:T(8,128)S(1)}, u32[]{:S(2)}, u32[]{:S(2)}) collective-permute-start(f32[2,64,16,128]{3,2,1,0:T(8,128)} %get-tuple-element.28), channel_id=1, source_target_pairs={{0,1},{1,0},{2,3},{3,2},{4,5},{5,4},{6,7},{7,6},{8,9},{9,8},{10,11... | collective-permute-start | bytes 3145736 | tf_op jit(solution)/shard_map/ppermute | solution.py:184
Sparse Core Ops, SparseCore 0:
  9.5 84.9 all-gather.1

commit v3 on v2

--- a/solution.py
+++ b/solution.py
@@ -8,8 +8,8 @@
 COUNT = 2
 PAIR_TYPE = jnp.bfloat16
 PIECE = 4
-GROUP = 8
 MIB = 1 << 20
+LIGHT = pl.CostEstimate(flops=1, bytes_accessed=1, transcendentals=0)
 
 
 def wide_rows(coef, wide):
@@ -83,77 +83,81 @@
             pltpu.VMEM((COUNT, 128, 512), jnp.bfloat16),
             pltpu.SemaphoreType.DMA((COUNT, 16 // PIECE)),
         ],
-        compiler_params=pltpu.CompilerParams(vmem_limit_bytes=24 * MIB),
-        cost_estimate=pl.CostEstimate(
-            flops=COUNT * 16 * 2 * 128 * 512 * 256, bytes_accessed=COUNT * 16 * 300 * 1024, transcendentals=0
-        ),
+        compiler_params=pltpu.CompilerParams(vmem_limit_bytes=18 * MIB),
+        cost_estimate=LIGHT,
         name="contract_partner" if got is None else "contract_own",
     )(*given)
 
 
-def code_sums(groups, table):
+def code_sums(owns, ups, downs, right, left, table):
+    n = len(owns)
+
     def kernel(*refs):
-        table_ref, out_ref = refs[-2], refs[-1]
+        own_refs, up_refs, down_refs = refs[:n], refs[n : 2 * n], refs[2 * n : 3 * n]
+        right_ref, left_ref, table_ref, out_ref = refs[3 * n :]
+        line = lax.broadcasted_iota(jnp.int32, (16, 256), 0)
         lane = lax.broadcasted_iota(jnp.int32, (16, 256), 1)
         for t in range(16):
             extra = jnp.zeros((16, 256), jnp.int32)
             for k in range(4):
-                own, right, left, up, down = refs[5 * (k // COUNT) : 5 * (k // COUNT) + 5]
-                c = k % COUNT
-                sums = own[t, c] + (down if t < 8 else up)[t, c].astype(jnp.float32)
-                sums = sums + (right[t, c] if t < 8 else left[t - 8, c]).astype(jnp.float32)
+                i, c = k // COUNT, k % COUNT
+                sums = own_refs[i][t, c] + (down_refs if t < 8 else up_refs)[i][t, c].astype(jnp.float32)
+                sums = sums + (right_ref[t, k] if t < 8 else left_ref[t - 8, k]).astype(jnp.float32)
                 most = jnp.max(jnp.max(jnp.abs(sums), axis=0, keepdims=True), axis=1, keepdims=True)
                 power = jnp.floor(jnp.log2(jnp.maximum(most, 1e-30))) + 1.0
                 coded = jnp.floor(sums * jnp.exp2(14.5 - power) + 0.5).astype(jnp.int32)
                 out_ref[t, 32 * k : 32 * k + 32] = coded.astype(jnp.int16)
-                extra = jnp.where(lane == k, table_ref[k, t], extra)
-                extra = jnp.where(lane == 4 + k, power.astype(jnp.int32), extra)
+                extra = jnp.where((line == 0) & (lane == k), table_ref[k, t], extra)
+                extra = jnp.where(line == 1 + k, power.astype(jnp.int32), extra)
             out_ref[t, 128:144] = extra.astype(jnp.int16)
 
     vmem = pl.BlockSpec(memory_space=pltpu.VMEM)
-    given = [x for group in groups for x in group]
     return pl.pallas_call(
         kernel,
-        in_specs=[vmem] * len(given) + [pl.BlockSpec(memory_space=pltpu.SMEM)],
+        in_specs=[vmem] * (3 * n + 2) + [pl.BlockSpec(memory_space=pltpu.SMEM)],
         out_specs=vmem,
         out_shape=jax.ShapeDtypeStruct((16, 144, 256), jnp.int16),
-        compiler_params=pltpu.CompilerParams(vmem_limit_bytes=24 * MIB),
+        compiler_params=pltpu.CompilerParams(vmem_limit_bytes=18 * MIB),
+        cost_estimate=LIGHT,
         name="code_sums",
-    )(*given, table)
-
-
-def contract_virtual(k4, scales, mask, held, u, pair):
-    def kernel(k4_ref, scale_ref, mask_ref, held_ref, u_ref, pair_ref, mine_ref, theirs_ref, own, rows, sems):
-        def copy(k):
-            return pltpu.make_async_copy(held_ref.at[k4_ref[k]], own.at[k], sems.at[k])
-
-        @pl.loop(0, 64)
-        def _(k):
-            copy(k).start()
+    )(*owns, *ups, *downs, right, left, table)
+
+
+def contract_virtual(k4, k2, mask, held, u, pair):
+    sizes = [x.shape[0] for x in held]
+    starts = [sum(sizes[:i]) for i in range(len(held))]
+
+    def kernel(k4_ref, k2_ref, mask_ref, u_ref, pair_ref, *rest):
+        held_refs, (mine_ref, theirs_ref, blocks, rows, sems) = rest[: len(held)], rest[len(held) :]
+
+        def copy(i):
+            return pltpu.make_async_copy(held_refs[i], blocks.at[pl.ds(starts[i], sizes[i])], sems.at[i])
+
+        for i in range(len(held)):
+            copy(i).start()
 
         @pl.loop(0, 16)
         def _(j):
             for h, ref in enumerate((u_ref, pair_ref)):
+                scale = jnp.exp2(ref[j, 128:144].astype(jnp.int32).astype(jnp.float32) - 14.5)
                 for c in range(4):
-                    full = ref[j, 32 * c : 32 * c + 32].astype(jnp.int32).astype(jnp.float32) * scale_ref[h, 4 * j + c]
+                    full = ref[j, 32 * c : 32 * c + 32].astype(jnp.int32).astype(jnp.float32) * scale[1 + c : 2 + c]
                     high = full.astype(jnp.bfloat16)
                     low = (full - high.astype(jnp.float32)).astype(jnp.bfloat16)
                     rows[4 * j + c, 32 * h : 32 * h + 32] = high
                     rows[4 * j + c, 64 + 32 * h : 96 + 32 * h] = low
 
-        @pl.loop(0, 64 // GROUP)
-        def _(g):
-            for i in range(GROUP):
-                copy(g * GROUP + i).wait()
+        for first in range(0, 64, 8):
+            if first in starts:
+                copy(starts.index(first)).wait()
             all_got = []
-            for i in range(GROUP):
-                k = g * GROUP + i
-                both = jnp.concatenate([own[k, 0], own[k, 1]], axis=1)
-                all_got.append(jnp.dot(rows[k], both, preferred_element_type=jnp.float32))
-            for i in range(GROUP):
-                k = g * GROUP + i
-                got = all_got[i][:64] + all_got[i][64:]
-                keep = mask_ref[pl.ds(k4_ref[k], 1), :]
+            for n in range(first, first + 8):
+                both = jnp.concatenate([blocks[n, 0], blocks[n, 1]], axis=1)
+                all_got.append(jnp.dot(rows[k2_ref[n]], both, preferred_element_type=jnp.float32))
+            for n in range(first, first + 8):
+                k = k2_ref[n]
+                got = all_got[n - first][:64] + all_got[n - first][64:]
+                keep = mask_ref[pl.ds(k4_ref[n], 1), :]
                 for r, ref in ((0, mine_ref), (32, theirs_ref)):
                     ref[0, k] = (got[r : r + 16, :128] - got[r + 16 : r + 32, 128:]) * keep
                     ref[1, k] = (got[r : r + 16, 128:] + got[r + 16 : r + 32, :128]) * keep
@@ -162,18 +166,20 @@
     vmem = pl.BlockSpec(memory_space=pltpu.VMEM)
     return pl.pallas_call(
         kernel,
-        in_specs=[pl.BlockSpec(memory_space=pltpu.SMEM)] * 2 + [vmem, pl.BlockSpec(memory_space=pltpu.HBM), vmem, vmem],
+        in_specs=[pl.BlockSpec(memory_space=pltpu.SMEM)] * 2
+        + [vmem] * 3
+        + [pl.BlockSpec(memory_space=pltpu.HBM)] * len(held),
         out_specs=[vmem, vmem],
         out_shape=[result, result],
         scratch_shapes=[
             pltpu.VMEM((64, 2, 256, 128), jnp.bfloat16),
             pltpu.VMEM((64, 128, 256), jnp.bfloat16),
-            pltpu.SemaphoreType.DMA((64,)),
+            pltpu.SemaphoreType.DMA((len(held),)),
         ],
-        compiler_params=pltpu.CompilerParams(vmem_limit_bytes=24 * MIB),
-        cost_estimate=pl.CostEstimate(flops=64 * 2 * 128 * 256 * 256, bytes_accessed=64 * 200 * 1024, transcendentals=0),
+        compiler_params=pltpu.CompilerParams(vmem_limit_bytes=18 * MIB),
+        cost_estimate=LIGHT,
         name="contract_virtual",
-    )(k4, scales, mask, held, u, pair)
+    )(k4, k2, mask, u, pair, *held)
 
 
 def per_device(ints, vir_coef, occ_coef, k4_table, band_mask):
@@ -187,7 +193,21 @@
         return lax.ppermute(x, "band", [(i, (i // 2 + d) % 4 * 2 + i % 2) for i in range(8)])
 
     half = lax.dynamic_slice_in_dim(vir_coef, 128 * core, 128, axis=3)
-    held = pltpu.with_memory_space_constraint(lax.all_gather(half, "mom", axis=0, tiled=True), pltpu.HBM)
+
+    def onward(v, second, d):
+        pairs = []
+        for i in range(16):
+            for j in range(8):
+                to = (i // 4 + d) % 4 * 4 + i % 4 if (j % 2 == 1) != second else i // 4 * 4 + (i % 4 + d) % 4
+                pairs.append((8 * i + j, 8 * to + j))
+        return lax.ppermute(v, ("mom", "band"), pairs)
+
+    offset = jnp.array([0, -1, 1, 2])
+    n = jnp.arange(64)
+    within, beyond, local = offset[n // 4 % 4], offset[n // 16], n % 4
+    x = mom // 4 + jnp.where(core == 0, beyond, within)
+    z = mom % 4 + jnp.where(core == 0, within, beyond)
+    held_k4 = 4 * (4 * (x % 4) + z % 4) + local
     mask = lax.dynamic_slice_in_dim(band_mask, 128 * core, 128, axis=1).astype(jnp.float32)
 
     occ = lax.dynamic_slice_in_dim(occ_coef, 4 * mom, 4, axis=0)
@@ -202,27 +222,41 @@
     coef_own, coef_partner = coef[:, 0], coef[:, 1]
 
     ints = pltpu.with_memory_space_constraint(ints.reshape(2, 4, 16, 256, 256), pltpu.HBM)
-    chunks = range(0, 4, COUNT)
-    arrived = [across(contract_occupied(coef_partner, ints, first)[0]) for first in chunks]
-    sent = []
-    for first, got in zip(chunks, arrived):
-        own, right, left, up, down = contract_occupied(coef_own, ints, first, got)
-        sent.append((own, right, left, along(up, 1), along(down, -1)))
-    groups = []
-    for own, right, left, up, down in sent:
-        right = along((right + up[:8].astype(jnp.float32)).astype(jnp.bfloat16), 1)
-        left = along((left + down[8:].astype(jnp.float32)).astype(jnp.bfloat16), -1)
-        groups.append((own, right, left, up, down))
-    coded = code_sums(groups, k4_table)
+    def after(x, *others):
+        return lax.optimization_barrier((x, *others))[0]
+
+    theirs = contract_occupied(coef_partner, ints, 0)[0]
+    got = across(theirs)
+    half = after(half, theirs)
+    near = [onward(half, False, d) for d in (1, -1, 2)]
+    own, right, left, up, down = contract_occupied(coef_own, ints, 0, got)
+    ups, downs = [along(up, 1)], [along(down, -1)]
+    owns, rights, lefts = [own], [right], [left]
+    near = lax.optimization_barrier((*near, up))[:3]
+    row = jnp.concatenate([half, *near])
+    below, above = onward(row, True, 1), onward(row, True, -1)
+    got = across(contract_occupied(after(coef_partner, up), ints, COUNT)[0])
+    own, right, left, up, down = contract_occupied(coef_own, ints, COUNT, got)
+    ups.append(along(up, 1))
+    downs.append(along(down, -1))
+    owns, rights, lefts = owns + [own], rights + [right], lefts + [left]
+    right = [(r + x[:8].astype(jnp.float32)).astype(jnp.bfloat16) for r, x in zip(rights, ups)]
+    left = [(r + x[8:].astype(jnp.float32)).astype(jnp.bfloat16) for r, x in zip(lefts, downs)]
+    right, left = jnp.concatenate(right, axis=1), jnp.concatenate(left, axis=1)
+    low, high = lax.optimization_barrier((below[:8], above[8:], up, down))[:2]
+    opposite = [onward(low, True, 1), onward(high, True, -1)]
+    held = [row, below, above] + opposite
+    owns[0] = after(owns[0], *opposite)
+    coded = code_sums(owns, ups, downs, along(right, 1), along(left, -1), k4_table)
     u = lax.all_to_all(coded, "mom", split_axis=0, concat_axis=0, tiled=True)
     pair = across(u)
     k4 = u[:, 128, :4].astype(jnp.int32).reshape(64)
-    powers = jnp.stack([u[:, 128, 4:8], pair[:, 128, 4:8]]).astype(jnp.float32).reshape(2, 64)
-    mine, theirs = contract_virtual(k4, jnp.exp2(powers - 14.5), mask, held, u, pair)
+    k2 = jnp.sum(jnp.where(held_k4[:, None] == k4[None, :], n[None, :], 0), axis=1)
+    held = [pltpu.with_memory_space_constraint(x, pltpu.HBM) for x in held]
+    mine, theirs = contract_virtual(held_k4, k2, mask, held, u, pair)
     theirs = across(theirs)
-    first = jnp.where(core == 0, mine, theirs)
-    second = jnp.where(core == 0, theirs, mine)
-    return jnp.concatenate([first, second], axis=-1).reshape(2, 64, 1, 2, 8, 256)
+    low, high = jnp.concatenate([mine, theirs], axis=-1), jnp.concatenate([theirs, mine], axis=-1)
+    return jnp.where(core == 0, low, high).reshape(2, 64, 1, 2, 8, 256)
 
 
 def solution(mesh):

time: 122 us -> 110 us (0.902)
  starting transfers between devices: 14.2 us -> 27.8 us
  blocking collectives: 33.5 us -> 20.2 us
  between operations: 13.6 us -> 0.33 us
  waiting for transfers between devices: 26.4 us -> 31.4 us
  local copies, waits for them, and re-layouts: 5.87 us -> 4.04 us
    ppermute x0 -> x7, waiting for transfers between devices: none -> 20 us  [onward(): return lax.ppermute(v, ('mom', 'band'), pairs)]
    ppermute x8 -> x6, waiting for transfers between devices: 21.8 us -> 7.03 us  [along(): lax.ppermute(x, 'band', [(i, (i // 2 + d) % 4 * 2 + i % 2) for i in range...]
    all_to_all x1, blocking collectives: 33.5 us -> 20.2 us  [per_device(): u = lax.all_to_all(coded, 'mom', split_axis=0, concat_axis=0, tiled=True)]
    ppermute x0 -> x7, starting transfers between devices: none -> 10.7 us  [onward(): return lax.ppermute(v, ('mom', 'band'), pairs)]
    ppermute x4, starting transfers between devices: 3.59 us -> 7.73 us  [across(): return lax.ppermute(x, 'band', [(i, i ^ 1) for i in range(8)])]
    pallas_call x1, Pallas kernels: 6.15 us -> 4.57 us  [contract_virtual(): pl.pallas_call(kernel, in_specs=[pl.BlockSpec(memory_space=pltpu.SMEM)] *...]
    reshape x1 -> x0, other arithmetic: 1.51 us -> none  [per_device(): jnp.concatenate([first, second], axis=-1).reshape(2, 64, 1, 2, 8, 256)]
    ppermute x8 -> x6, starting transfers between devices: 10.6 us -> 9.37 us  [along(): lax.ppermute(x, 'band', [(i, (i // 2 + d) % 4 * 2 + i % 2) for i in range...]
  transfers between devices with their start and end apart: 13 -> 17, of which waited for: 6 -> 8; matrix products, arithmetic and copies ran while one was open for 3% -> 1% of each run, Pallas kernels for 14% -> 11%
where the time goes in v3:
time: 110 us; the launch traced here: 109 us
  waiting for transfers between devices  31.4 us (29%)
  starting transfers between devices  27.8 us (25%)
  Pallas kernels  22.7 us (21%)
  blocking collectives  20.2 us (18%)
  local copies, waits for them, and re-layouts  4.04 us (4%)
  other arithmetic  2.94 us (3%)
    all_to_all x1, blocking collectives, per_device(): u = lax.all_to_all(coded, 'mom', split_axis=0, concat_axis=0, tiled=True)  20.2 us
    ppermute x7, waiting for transfers between devices, onward(): return lax.ppermute(v, ('mom', 'band'), pairs)  20 us
    pallas_call x4, Pallas kernels, contract_occupied(): pl.pallas_call(kernel, in_specs=[vmem, pl.BlockSpec(memory_space=pltpu.HB...  16.6 us
    ppermute x7, starting transfers between devices, onward(): return lax.ppermute(v, ('mom', 'band'), pairs)  10.7 us
    ppermute x6, starting transfers between devices, along(): lax.ppermute(x, 'band', [(i, (i // 2 + d) % 4 * 2 + i % 2) for i in range...  9.37 us
    ppermute x4, starting transfers between devices, across(): return lax.ppermute(x, 'band', [(i, i ^ 1) for i in range(8)])  7.73 us
    ppermute x6, waiting for transfers between devices, along(): lax.ppermute(x, 'band', [(i, (i // 2 + d) % 4 * 2 + i % 2) for i in range...  7.03 us
    pallas_call x1, Pallas kernels, contract_virtual(): pl.pallas_call(kernel, in_specs=[pl.BlockSpec(memory_space=pltpu.SMEM)] *...  4.57 us
  transfers between devices with their start and end apart: 17, of which 8 were waited for; matrix products, arithmetic and copies ran while one was open for 1% of the time, Pallas kernels for 11%

profile of v3, /device:TPU:1, one launch (start us, length us, event | category | flops | bytes accessed | tf_op | source)
XLA Modules:
  0.0 109.4 jit_solution(3142912161059179238)
XLA Ops:
  3.1 5.1 %contract_partner.2 = bf16[4,16,2,32,256]{4,3,2,1,0:T(8,128)(2,1)} custom-call(bf16[4,16,64]{2,1,0:T(8,128)(2,1)S(1)} %get-tuple-element.31.coef_ref, bf16[2,4,16,256,256]{4,3,2,1,0:T(8,128)(2,1)} %bitcast.45), custom_call_target="tpu_custom_call" | custom-call | flops 1 | bytes 1 | tf_op jit(solution)/shard_map/contract_partner/pallas_call | solution.py:76
  8.3 1.5 %collective-permute-start = (bf16[4,16,2,32,256]{4,3,2,1,0:T(8,128)(2,1)}, bf16[4,16,2,32,256]{4,3,2,1,0:T(8,128)(2,1)S(1)}, u32[]{:S(2)}, u32[]{:S(2)}) collective-permute-start(bf16[4,16,2,32,256]{4,3,2,1,0:T(8,128)(2,1)} %contract_partner.2), channel_id=1, source_target_pairs={{0,1},{1,0},{2,3},{3,2},{4,5},{5,4},{6,7},{7,6},{8,9},{9,8},{10,11... | collective-permute-start | bytes 6291464 | tf_op jit(solution)/shard_map/ppermute | solution.py:190
  12.6 1.6 %collective-permute-start.3 = (bf16[4,2,256,128]{3,2,1,0:T(8,128)(2,1)S(1)}, bf16[4,2,256,128]{3,2,1,0:T(8,128)(2,1)S(1)}, u32[]{:S(2)}, u32[]{:S(2)}) collective-permute-start(bf16[4,2,256,128]{3,2,1,0:T(8,128)(2,1)S(1)} %constant_dynamic-slice_fusion), channel_id=1, source_target_pairs={{0,16},{1,65},{2,18},{3,67},{4,20},{5,69},{6,22},{7,71},{8,24},{9,... | collective-permute-start | bytes 1572872 | tf_op jit(solution)/shard_map/ppermute | solution.py:203
  14.2 3.8 %contract_own.2 = (f32[16,2,32,256]{3,2,1,0:T(8,128)S(1)}, f32[8,2,32,256]{3,2,1,0:T(8,128)S(1)}, f32[8,2,32,256]{3,2,1,0:T(8,128)S(1)}, bf16[16,2,32,256]{3,2,1...) custom-call(bf16[4,16,64]{2,1,0:T(8,128)(2,1)S(1)} %get-tuple-element.46.coef_ref, bf16[2,4,16,256,256]{4,3,2,1,0:T(8,128)(2,1)} %bitcast.46, ...), custom_call_target="tpu_custom_call" | custom-call | flops 1 | bytes 1 | tf_op jit(solution)/shard_map/contract_own/pallas_call | solution.py:76
  18.1 3.8 %contract_partner.3 = bf16[4,16,2,32,256]{4,3,2,1,0:T(8,128)(2,1)S(1)} custom-call(bf16[4,16,64]{2,1,0:T(8,128)(2,1)S(1)} %get-tuple-element.31.coef_ref, bf16[2,4,16,256,256]{4,3,2,1,0:T(8,128)(2,1)} %bitcast.47), custom_call_target="tpu_custom_call" | custom-call | flops 1 | bytes 1 | tf_op jit(solution)/shard_map/contract_partner/pallas_call | solution.py:76
  21.9 1.8 %collective-permute-start.6 = (bf16[4,16,2,32,256]{4,3,2,1,0:T(8,128)(2,1)S(1)}, bf16[4,16,2,32,256]{4,3,2,1,0:T(8,128)(2,1)S(1)}, u32[]{:S(2)}, u32[]{:S(2)}) collective-permute-start(bf16[4,16,2,32,256]{4,3,2,1,0:T(8,128)(2,1)S(1)} %contract_partner.3), channel_id=1, source_target_pairs={{0,1},{1,0},{2,3},{3,2},{4,5},{5,4},{6,7},{7,6},{8,9},{9,8},{10,11... | collective-permute-start | bytes 6291464 | tf_op jit(solution)/shard_map/ppermute | solution.py:190
  23.8 2.4 %collective-permute-done.3 = bf16[4,2,256,128]{3,2,1,0:T(8,128)(2,1)S(1)} collective-permute-done((bf16[4,2,256,128]{3,2,1,0:T(8,128)(2,1)S(1)}, bf16[4,2,256,128]{3,2,1,0:T(8,128)(2,1)S(1)}, u32[]{:S(2)}, u32[]{:S(2)}) %collective-permute-start.3) | collective-permute-done | bytes 524320 | tf_op jit(solution)/shard_map/ppermute | solution.py:203
  27.8 2.2 %collective-permute-start.5 = (bf16[16,2,256,128]{3,2,1,0:T(8,128)(2,1)S(1)}, bf16[16,2,256,128]{3,2,1,0:T(8,128)(2,1)S(1)}, u32[]{:S(2)}, u32[]{:S(2)}) collective-permute-start(bf16[16,2,256,128]{3,2,1,0:T(8,128)(2,1)S(1)} %constant_dynamic-update-slice_fusion.rest_0_), channel_id=1, source_target_pairs={{0,96},{1,25},{2,98},{3,27},{4,100},{5,29},{6,102},{7,31},{8,104},... | collective-permute-start | bytes 6291464 | tf_op jit(solution)/shard_map/ppermute | solution.py:203
  30.0 2.7 %collective-permute-start.11 = (bf16[16,2,32,256]{3,2,1,0:T(8,128)(2,1)S(1)}, bf16[16,2,32,256]{3,2,1,0:T(8,128)(2,1)S(1)}, u32[]{:S(2)}, u32[]{:S(2)}) collective-permute-start(bf16[16,2,32,256]{3,2,1,0:T(8,128)(2,1)S(1)} %get-tuple-element.38), channel_id=1, source_target_pairs={{0,6},{1,7},{2,0},{3,1},{4,2},{5,3},{6,4},{7,5},{8,14},{9,15},{10,... | collective-permute-start | bytes 1572872 | tf_op jit(solution)/shard_map/ppermute | solution.py:193
  32.7 3.8 %contract_own.3 = (f32[16,2,32,256]{3,2,1,0:T(8,128)S(1)}, f32[8,2,32,256]{3,2,1,0:T(8,128)S(1)}, f32[8,2,32,256]{3,2,1,0:T(8,128)S(1)}, bf16[16,2,32,256]{3,2,1...) custom-call(bf16[4,16,64]{2,1,0:T(8,128)(2,1)S(1)} %get-tuple-element.46.coef_ref, bf16[2,4,16,256,256]{4,3,2,1,0:T(8,128)(2,1)} %bitcast.48, ...), custom_call_target="tpu_custom_call" | custom-call | flops 1 | bytes 1 | tf_op jit(solution)/shard_map/contract_own/pallas_call | solution.py:76
  36.6 2.9 %collective-permute-start.12 = (bf16[16,2,32,256]{3,2,1,0:T(8,128)(2,1)S(1)}, bf16[16,2,32,256]{3,2,1,0:T(8,128)(2,1)S(1)}, u32[]{:S(2)}, u32[]{:S(2)}) collective-permute-start(bf16[16,2,32,256]{3,2,1,0:T(8,128)(2,1)S(1)} %get-tuple-element.33), channel_id=1, source_target_pairs={{0,6},{1,7},{2,0},{3,1},{4,2},{5,3},{6,4},{7,5},{8,14},{9,15},{10,... | collective-permute-start | bytes 1572872 | tf_op jit(solution)/shard_map/ppermute | solution.py:193
  39.5 2.6 %collective-permute-done.11.refs_4_ = bf16[16,2,32,256]{3,2,1,0:T(8,128)(2,1)S(1)} collective-permute-done((bf16[16,2,32,256]{3,2,1,0:T(8,128)(2,1)S(1)}, bf16[16,2,32,256]{3,2,1,0:T(8,128)(2,1)S(1)}, u32[]{:S(2)}, u32[]{:S(2)}) %collective-permute-start.11) | collective-permute-done | bytes 524320 | tf_op jit(solution)/shard_map/ppermute | solution.py:193
  43.0 2.2 %collective-permute-done.9.refs_2_ = bf16[16,2,32,256]{3,2,1,0:T(8,128)(2,1)S(1)} collective-permute-done((bf16[16,2,32,256]{3,2,1,0:T(8,128)(2,1)S(1)}, bf16[16,2,32,256]{3,2,1,0:T(8,128)(2,1)S(1)}, u32[]{:S(2)}, u32[]{:S(2)}) %collective-permute-start.9) | collective-permute-done | bytes 524320 | tf_op jit(solution)/shard_map/ppermute | solution.py:193
  45.3 8.3 %collective-permute-done.4.rest_1_ = bf16[16,2,256,128]{3,2,1,0:T(8,128)(2,1)S(1)} collective-permute-done((bf16[16,2,256,128]{3,2,1,0:T(8,128)(2,1)S(1)}, bf16[16,2,256,128]{3,2,1,0:T(8,128)(2,1)S(1)}, u32[]{:S(2)}, u32[]{:S(2)}) %collective-permute-start.4) | collective-permute-done | bytes 2097184 | tf_op jit(solution)/shard_map/ppermute | solution.py:203
  55.0 2.7 %collective-permute-start.8 = (bf16[8,2,256,128]{3,2,1,0:T(8,128)(2,1)S(1)}, bf16[8,2,256,128]{3,2,1,0:T(8,128)(2,1)S(1)}, u32[]{:S(2)}, u32[]{:S(2)}) collective-permute-start(bf16[8,2,256,128]{3,2,1,0:T(8,128)(2,1)S(1)} %slice.63), channel_id=1, source_target_pairs={{0,96},{1,25},{2,98},{3,27},{4,100},{5,29},{6,102},{7,31},{8,104},... | collective-permute-start | bytes 3145736 | tf_op jit(solution)/shard_map/ppermute | solution.py:203
  57.8 2.8 %collective-permute-start.14 = (bf16[8,4,32,256]{3,2,1,0:T(8,128)(2,1)S(1)}, bf16[8,4,32,256]{3,2,1,0:T(8,128)(2,1)S(1)}, u32[]{:S(2)}, u32[]{:S(2)}) collective-permute-start(bf16[8,4,32,256]{3,2,1,0:T(8,128)(2,1)S(1)} %pad_maximum_fusion.1), channel_id=1, source_target_pairs={{0,6},{1,7},{2,0},{3,1},{4,2},{5,3},{6,4},{7,5},{8,14},{9,15},{10,... | collective-permute-start | bytes 1572872 | tf_op jit(solution)/shard_map/ppermute | solution.py:193
  60.8 9.3 %collective-permute-done.7.rest_3_ = bf16[8,2,256,128]{3,2,1,0:T(8,128)(2,1)S(1)} collective-permute-done((bf16[8,2,256,128]{3,2,1,0:T(8,128)(2,1)S(1)}, bf16[8,2,256,128]{3,2,1,0:T(8,128)(2,1)S(1)}, u32[]{:S(2)}, u32[]{:S(2)}) %collective-permute-start.7) | collective-permute-done | bytes 1048608 | tf_op jit(solution)/shard_map/ppermute | solution.py:203
  70.1 2.2 %collective-permute-done.13.refs_6_ = bf16[8,4,32,256]{3,2,1,0:T(8,128)(2,1)S(1)} collective-permute-done((bf16[8,4,32,256]{3,2,1,0:T(8,128)(2,1)S(1)}, bf16[8,4,32,256]{3,2,1,0:T(8,128)(2,1)S(1)}, u32[]{:S(2)}, u32[]{:S(2)}) %collective-permute-start.13) | collective-permute-done | bytes 524320 | tf_op jit(solution)/shard_map/ppermute | solution.py:193
  73.9 20.2 %all_to_all.5.u_ref = s16[16,144,256]{2,1,0:T(8,128)(2,1)S(1)} all-to-all(s16[16,144,256]{2,1,0:T(8,128)(2,1)S(1)} %code_sums.1), channel_id=1, replica_groups=mesh['mom'=16,'band'=8] {'mom'}, dimensions={0} | all-to-all | bytes 2359296 | tf_op jit(solution)/shard_map/all_to_all | solution.py:251
  94.1 4.0 %collective-permute-start.15 = (s16[16,144,256]{2,1,0:T(8,128)(2,1)S(1)}, s16[16,144,256]{2,1,0:T(8,128)(2,1)S(1)}, u32[]{:S(2)}, u32[]{:S(2)}) collective-permute-start(s16[16,144,256]{2,1,0:T(8,128)(2,1)S(1)} %all_to_all.5.u_ref), channel_id=1, source_target_pairs={{0,1},{1,0},{2,3},{3,2},{4,5},{5,4},{6,7},{7,6},{8,9},{9,8},{10,11... | collective-permute-start | bytes 3538952 | tf_op jit(solution)/shard_map/ppermute | solution.py:190
  98.4 2.1 %collective-permute-done.15.pair_ref = s16[16,144,256]{2,1,0:T(8,128)(2,1)S(1)} collective-permute-done((s16[16,144,256]{2,1,0:T(8,128)(2,1)S(1)}, s16[16,144,256]{2,1,0:T(8,128)(2,1)S(1)}, u32[]{:S(2)}, u32[]{:S(2)}) %collective-permute-start.15) | collective-permute-done | bytes 1179680 | tf_op jit(solution)/shard_map/ppermute | solution.py:190
  100.5 4.6 %contract_virtual.1 = (f32[2,64,16,128]{3,2,1,0:T(8,128)S(1)}, f32[2,64,16,128]{3,2,1,0:T(8,128)S(1)}) custom-call(s32[64]{0:T(128)S(1)} %fusion.5.k4_ref, s32[64]{0:T(128)S(1)} %select_reduce_fusion.k2_ref, f32[64,128]{1,0:T(8,128)S(1)} %dynamic-slice_convert_fusion.mask_ref, s16[16,144,256]{2,1,0:T(8,128)(2,1)S(1)} %all_to_all.5.u_ref, ...), custom_call_target="tpu_custom_call" | custom-call | flops 1 | bytes 1 | tf_op jit(solution)/shard_map/contract_virtual/pallas_call | solution.py:167
  105.6 2.3 %collective-permute-done.16 = f32[2,64,16,128]{3,2,1,0:T(8,128)S(1)} collective-permute-done((f32[2,64,16,128]{3,2,1,0:T(8,128)S(1)}, f32[2,64,16,128]{3,2,1,0:T(8,128)S(1)}, u32[]{:S(2)}, u32[]{:S(2)}) %collective-permute-start.16) | collective-permute-done | bytes 1048608 | tf_op jit(solution)/shard_map/ppermute | solution.py:190
  107.9 1.6 %maximum_select_fusion = f32[2,64,1,2,8,256]{5,4,3,2,1,0:T(8,128)} fusion(f32[2,64,1,2,8,128]{5,4,3,2,1,0:T(8,128)S(1)} %bitcast.49, f32[2,64,1,2,8,128]{5,4,3,2,1,0:T(8,128)S(1)} %bitcast.44, pred[]{:T(512)S(6)} %eq.30), kind=kLoop, calls=%fused_computation.1 | loop fusion | flops 1572864 | bytes 4194305 | tf_op jit(solution)/shard_map/jit(_where)/select_n | solution.py:259
  (70 shorter events, 12.5 us)
Async XLA Ops:
  0.0 9.8 %copy-start = (bf16[4,2,256,256]{3,2,1,0:T(8,128)(2,1)S(1)}, bf16[4,2,256,256]{3,2,1,0:T(8,128)(2,1)}, u32[]{:S(2)}) copy-start(bf16[4,2,256,256]{3,2,1,0:T(8,128)(2,1)} %param.7) | copy-start | bytes 3145732
  8.3 6.0 %collective-permute-start = (bf16[4,16,2,32,256]{4,3,2,1,0:T(8,128)(2,1)}, bf16[4,16,2,32,256]{4,3,2,1,0:T(8,128)(2,1)S(1)}, u32[]{:S(2)}, u32[]{:S(2)}) collective-permute-start(bf16[4,16,2,32,256]{4,3,2,1,0:T(8,128)(2,1)} %contract_partner.2), channel_id=1, source_target_pairs={{0,1},{1,0},{2,3},{3,2},{4,5},{5,4},{6,7},{7,6},{8,9},{9,8},{10,11... | collective-permute-start | bytes 6291464 | tf_op jit(solution)/shard_map/ppermute | solution.py:190
  9.9 13.9 %collective-permute-start.1 = (bf16[4,2,256,128]{3,2,1,0:T(8,128)(2,1)S(1)}, bf16[4,2,256,128]{3,2,1,0:T(8,128)(2,1)S(1)}, u32[]{:S(2)}, u32[]{:S(2)}) collective-permute-start(bf16[4,2,256,128]{3,2,1,0:T(8,128)(2,1)S(1)} %constant_dynamic-slice_fusion), channel_id=1, source_target_pairs={{0,8},{1,33},{2,10},{3,35},{4,12},{5,37},{6,14},{7,39},{8,16},{9,4... | collective-permute-start | bytes 1572872 | tf_op jit(solution)/shard_map/ppermute | solution.py:203
  11.2 12.5 %collective-permute-start.2 = (bf16[4,2,256,128]{3,2,1,0:T(8,128)(2,1)S(1)}, bf16[4,2,256,128]{3,2,1,0:T(8,128)(2,1)S(1)}, u32[]{:S(2)}, u32[]{:S(2)}) collective-permute-start(bf16[4,2,256,128]{3,2,1,0:T(8,128)(2,1)S(1)} %constant_dynamic-slice_fusion), channel_id=1, source_target_pairs={{0,24},{1,97},{2,26},{3,99},{4,28},{5,101},{6,30},{7,103},{8,0},{9... | collective-permute-start | bytes 1572872 | tf_op jit(solution)/shard_map/ppermute | solution.py:203
  12.6 13.5 %collective-permute-start.3 = (bf16[4,2,256,128]{3,2,1,0:T(8,128)(2,1)S(1)}, bf16[4,2,256,128]{3,2,1,0:T(8,128)(2,1)S(1)}, u32[]{:S(2)}, u32[]{:S(2)}) collective-permute-start(bf16[4,2,256,128]{3,2,1,0:T(8,128)(2,1)S(1)} %constant_dynamic-slice_fusion), channel_id=1, source_target_pairs={{0,16},{1,65},{2,18},{3,67},{4,20},{5,69},{6,22},{7,71},{8,24},{9,... | collective-permute-start | bytes 1572872 | tf_op jit(solution)/shard_map/ppermute | solution.py:203
  21.9 10.8 %collective-permute-start.6 = (bf16[4,16,2,32,256]{4,3,2,1,0:T(8,128)(2,1)S(1)}, bf16[4,16,2,32,256]{4,3,2,1,0:T(8,128)(2,1)S(1)}, u32[]{:S(2)}, u32[]{:S(2)}) collective-permute-start(bf16[4,16,2,32,256]{4,3,2,1,0:T(8,128)(2,1)S(1)} %contract_partner.3), channel_id=1, source_target_pairs={{0,1},{1,0},{2,3},{3,2},{4,5},{5,4},{6,7},{7,6},{8,9},{9,8},{10,11... | collective-permute-start | bytes 6291464 | tf_op jit(solution)/shard_map/ppermute | solution.py:190
  26.4 10.2 %copy-start.4 = (bf16[16,2,256,128]{3,2,1,0:T(8,128)(2,1)}, bf16[16,2,256,128]{3,2,1,0:T(8,128)(2,1)S(1)}, u32[]{:S(2)}) copy-start(bf16[16,2,256,128]{3,2,1,0:T(8,128)(2,1)S(1)} %constant_dynamic-update-slice_fusion.rest_0_) | copy-start | bytes 6291460
  26.4 27.3 %collective-permute-start.4 = (bf16[16,2,256,128]{3,2,1,0:T(8,128)(2,1)S(1)}, bf16[16,2,256,128]{3,2,1,0:T(8,128)(2,1)S(1)}, u32[]{:S(2)}, u32[]{:S(2)}) collective-permute-start(bf16[16,2,256,128]{3,2,1,0:T(8,128)(2,1)S(1)} %constant_dynamic-update-slice_fusion.rest_0_), channel_id=1, source_target_pairs={{0,32},{1,9},{2,34},{3,11},{4,36},{5,13},{6,38},{7,15},{8,40},{9,1... | collective-permute-start | bytes 6291464 | tf_op jit(solution)/shard_map/ppermute | solution.py:203
  27.8 25.9 %collective-permute-start.5 = (bf16[16,2,256,128]{3,2,1,0:T(8,128)(2,1)S(1)}, bf16[16,2,256,128]{3,2,1,0:T(8,128)(2,1)S(1)}, u32[]{:S(2)}, u32[]{:S(2)}) collective-permute-start(bf16[16,2,256,128]{3,2,1,0:T(8,128)(2,1)S(1)} %constant_dynamic-update-slice_fusion.rest_0_), channel_id=1, source_target_pairs={{0,96},{1,25},{2,98},{3,27},{4,100},{5,29},{6,102},{7,31},{8,104},... | collective-permute-start | bytes 6291464 | tf_op jit(solution)/shard_map/ppermute | solution.py:203
  30.0 12.1 %collective-permute-start.11 = (bf16[16,2,32,256]{3,2,1,0:T(8,128)(2,1)S(1)}, bf16[16,2,32,256]{3,2,1,0:T(8,128)(2,1)S(1)}, u32[]{:S(2)}, u32[]{:S(2)}) collective-permute-start(bf16[16,2,32,256]{3,2,1,0:T(8,128)(2,1)S(1)} %get-tuple-element.38), channel_id=1, source_target_pairs={{0,6},{1,7},{2,0},{3,1},{4,2},{5,3},{6,4},{7,5},{8,14},{9,15},{10,... | collective-permute-start | bytes 1572872 | tf_op jit(solution)/shard_map/ppermute | solution.py:193
  32.7 12.5 %collective-permute-start.9 = (bf16[16,2,32,256]{3,2,1,0:T(8,128)(2,1)S(1)}, bf16[16,2,32,256]{3,2,1,0:T(8,128)(2,1)S(1)}, u32[]{:S(2)}, u32[]{:S(2)}) collective-permute-start(bf16[16,2,32,256]{3,2,1,0:T(8,128)(2,1)S(1)} %get-tuple-element.27), channel_id=1, source_target_pairs={{0,2},{1,3},{2,4},{3,5},{4,6},{5,7},{6,0},{7,1},{8,10},{9,11},{10,... | collective-permute-start | bytes 1572872 | tf_op jit(solution)/shard_map/ppermute | solution.py:193
  36.6 21.1 %collective-permute-start.12 = (bf16[16,2,32,256]{3,2,1,0:T(8,128)(2,1)S(1)}, bf16[16,2,32,256]{3,2,1,0:T(8,128)(2,1)S(1)}, u32[]{:S(2)}, u32[]{:S(2)}) collective-permute-start(bf16[16,2,32,256]{3,2,1,0:T(8,128)(2,1)S(1)} %get-tuple-element.33), channel_id=1, source_target_pairs={{0,6},{1,7},{2,0},{3,1},{4,2},{5,3},{6,4},{7,5},{8,14},{9,15},{10,... | collective-permute-start | bytes 1572872 | tf_op jit(solution)/shard_map/ppermute | solution.py:193
  42.2 18.4 %collective-permute-start.10 = (bf16[16,2,32,256]{3,2,1,0:T(8,128)(2,1)S(1)}, bf16[16,2,32,256]{3,2,1,0:T(8,128)(2,1)S(1)}, u32[]{:S(2)}, u32[]{:S(2)}) collective-permute-start(bf16[16,2,32,256]{3,2,1,0:T(8,128)(2,1)S(1)} %get-tuple-element.32), channel_id=1, source_target_pairs={{0,2},{1,3},{2,4},{3,5},{4,6},{5,7},{6,0},{7,1},{8,10},{9,11},{10,... | collective-permute-start | bytes 1572872 | tf_op jit(solution)/shard_map/ppermute | solution.py:193
  53.7 4.1 %copy-start.3 = (bf16[16,2,256,128]{3,2,1,0:T(8,128)(2,1)}, bf16[16,2,256,128]{3,2,1,0:T(8,128)(2,1)S(1)}, u32[]{:S(2)}) copy-start(bf16[16,2,256,128]{3,2,1,0:T(8,128)(2,1)S(1)} %collective-permute-done.5.rest_2_) | copy-start | bytes 6291460
  55.0 15.2 %collective-permute-start.7 = (bf16[8,2,256,128]{3,2,1,0:T(8,128)(2,1)S(1)}, bf16[8,2,256,128]{3,2,1,0:T(8,128)(2,1)S(1)}, u32[]{:S(2)}, u32[]{:S(2)}) collective-permute-start(bf16[8,2,256,128]{3,2,1,0:T(8,128)(2,1)S(1)} %slice.62), channel_id=1, source_target_pairs={{0,32},{1,9},{2,34},{3,11},{4,36},{5,13},{6,38},{7,15},{8,40},{9,1... | collective-permute-start | bytes 3145736 | tf_op jit(solution)/shard_map/ppermute | solution.py:203
  55.0 15.2 %collective-permute-start.8 = (bf16[8,2,256,128]{3,2,1,0:T(8,128)(2,1)S(1)}, bf16[8,2,256,128]{3,2,1,0:T(8,128)(2,1)S(1)}, u32[]{:S(2)}, u32[]{:S(2)}) collective-permute-start(bf16[8,2,256,128]{3,2,1,0:T(8,128)(2,1)S(1)} %slice.63), channel_id=1, source_target_pairs={{0,96},{1,25},{2,98},{3,27},{4,100},{5,29},{6,102},{7,31},{8,104},... | collective-permute-start | bytes 3145736 | tf_op jit(solution)/shard_map/ppermute | solution.py:203
  57.7 14.7 %copy-start.1 = (s32[4,16]{1,0:T(4,128)S(1)}, s32[4,16]{1,0:T(4,128)}, u32[]{:S(2)}) copy-start(s32[4,16]{1,0:T(4,128)} %refs_8_.1) | copy-start | bytes 772
  57.8 12.3 %collective-permute-start.14 = (bf16[8,4,32,256]{3,2,1,0:T(8,128)(2,1)S(1)}, bf16[8,4,32,256]{3,2,1,0:T(8,128)(2,1)S(1)}, u32[]{:S(2)}, u32[]{:S(2)}) collective-permute-start(bf16[8,4,32,256]{3,2,1,0:T(8,128)(2,1)S(1)} %pad_maximum_fusion.1), channel_id=1, source_target_pairs={{0,6},{1,7},{2,0},{3,1},{4,2},{5,3},{6,4},{7,5},{8,14},{9,15},{10,... | collective-permute-start | bytes 1572872 | tf_op jit(solution)/shard_map/ppermute | solution.py:193
  60.8 11.6 %collective-permute-start.13 = (bf16[8,4,32,256]{3,2,1,0:T(8,128)(2,1)S(1)}, bf16[8,4,32,256]{3,2,1,0:T(8,128)(2,1)S(1)}, u32[]{:S(2)}, u32[]{:S(2)}) collective-permute-start(bf16[8,4,32,256]{3,2,1,0:T(8,128)(2,1)S(1)} %pad_maximum_fusion), channel_id=1, source_target_pairs={{0,2},{1,3},{2,4},{3,5},{4,6},{5,7},{6,0},{7,1},{8,10},{9,11},{10,... | collective-permute-start | bytes 1572872 | tf_op jit(solution)/shard_map/ppermute | solution.py:193
  70.1 2.2 %copy-start.5 = (bf16[8,2,256,128]{3,2,1,0:T(8,128)(2,1)}, bf16[8,2,256,128]{3,2,1,0:T(8,128)(2,1)S(1)}, u32[]{:S(2)}) copy-start(bf16[8,2,256,128]{3,2,1,0:T(8,128)(2,1)S(1)} %collective-permute-done.7.rest_3_) | copy-start | bytes 3145732
  70.1 2.2 %copy-start.6 = (bf16[8,2,256,128]{3,2,1,0:T(8,128)(2,1)}, bf16[8,2,256,128]{3,2,1,0:T(8,128)(2,1)S(1)}, u32[]{:S(2)}) copy-start(bf16[8,2,256,128]{3,2,1,0:T(8,128)(2,1)S(1)} %collective-permute-done.8.rest_4_) | copy-start | bytes 3145732
  73.9 24.2 %copy-start.7 = (s32[64,256]{1,0:T(8,128)S(1)}, s32[64,256]{1,0:T(8,128)}, u32[]{:S(2)}) copy-start(s32[64,256]{1,0:T(8,128)} %param.10) | copy-start | bytes 196612
  94.1 6.4 %collective-permute-start.15 = (s16[16,144,256]{2,1,0:T(8,128)(2,1)S(1)}, s16[16,144,256]{2,1,0:T(8,128)(2,1)S(1)}, u32[]{:S(2)}, u32[]{:S(2)}) collective-permute-start(s16[16,144,256]{2,1,0:T(8,128)(2,1)S(1)} %all_to_all.5.u_ref), channel_id=1, source_target_pairs={{0,1},{1,0},{2,3},{3,2},{4,5},{5,4},{6,7},{7,6},{8,9},{9,8},{10,11... | collective-permute-start | bytes 3538952 | tf_op jit(solution)/shard_map/ppermute | solution.py:190
  105.1 2.7 %collective-permute-start.16 = (f32[2,64,16,128]{3,2,1,0:T(8,128)S(1)}, f32[2,64,16,128]{3,2,1,0:T(8,128)S(1)}, u32[]{:S(2)}, u32[]{:S(2)}) collective-permute-start(f32[2,64,16,128]{3,2,1,0:T(8,128)S(1)} %get-tuple-element.44), channel_id=1, source_target_pairs={{0,1},{1,0},{2,3},{3,2},{4,5},{5,4},{6,7},{7,6},{8,9},{9,8},{10,11... | collective-permute-start | bytes 3145736 | tf_op jit(solution)/shard_map/ppermute | solution.py:190
  (1 other events, 1.3 us)

commit v4 on v3

--- a/solution.py
+++ b/solution.py
@@ -225,25 +225,20 @@
     def after(x, *others):
         return lax.optimization_barrier((x, *others))[0]
 
-    theirs = contract_occupied(coef_partner, ints, 0)[0]
-    got = across(theirs)
-    half = after(half, theirs)
     near = [onward(half, False, d) for d in (1, -1, 2)]
-    own, right, left, up, down = contract_occupied(coef_own, ints, 0, got)
-    ups, downs = [along(up, 1)], [along(down, -1)]
-    owns, rights, lefts = [own], [right], [left]
-    near = lax.optimization_barrier((*near, up))[:3]
     row = jnp.concatenate([half, *near])
     below, above = onward(row, True, 1), onward(row, True, -1)
-    got = across(contract_occupied(after(coef_partner, up), ints, COUNT)[0])
-    own, right, left, up, down = contract_occupied(coef_own, ints, COUNT, got)
-    ups.append(along(up, 1))
-    downs.append(along(down, -1))
-    owns, rights, lefts = owns + [own], rights + [right], lefts + [left]
+    chunks = range(0, 4, COUNT)
+    partner = [contract_occupied(coef_partner, ints, first)[0] for first in chunks]
+    arrived = [across(x) for x in partner]
+    arrived[0] = after(arrived[0], row)
+    sent = [contract_occupied(coef_own, ints, first, got) for first, got in zip(chunks, arrived)]
+    owns, rights, lefts = [x[0] for x in sent], [x[1] for x in sent], [x[2] for x in sent]
+    ups, downs = [along(x[3], 1) for x in sent], [along(x[4], -1) for x in sent]
     right = [(r + x[:8].astype(jnp.float32)).astype(jnp.bfloat16) for r, x in zip(rights, ups)]
     left = [(r + x[8:].astype(jnp.float32)).astype(jnp.bfloat16) for r, x in zip(lefts, downs)]
     right, left = jnp.concatenate(right, axis=1), jnp.concatenate(left, axis=1)
-    low, high = lax.optimization_barrier((below[:8], above[8:], up, down))[:2]
+    low, high = lax.optimization_barrier((below[:8], above[8:], left))[:2]
     opposite = [onward(low, True, 1), onward(high, True, -1)]
     held = [row, below, above] + opposite
     owns[0] = after(owns[0], *opposite)

time: 110 us -> 110 us (level)
  starting transfers between devices: 27.8 us -> 25 us
  waiting for transfers between devices: 31.4 us -> 34.1 us
  blocking collectives: 20.2 us -> 21.6 us
  Pallas kernels: 22.7 us -> 21.4 us
    ppermute x6, waiting for transfers between devices: 7.03 us -> 14.1 us  [along(): lax.ppermute(x, 'band', [(i, (i // 2 + d) % 4 * 2 + i % 2) for i in range...]
    ppermute x7, waiting for transfers between devices: 20 us -> 15.6 us  [onward(): return lax.ppermute(v, ('mom', 'band'), pairs)]
    all_to_all x1, blocking collectives: 20.2 us -> 21.6 us  [per_device(): u = lax.all_to_all(coded, 'mom', split_axis=0, concat_axis=0, tiled=True)]
    pallas_call x4, Pallas kernels: 16.6 us -> 15.3 us  [contract_occupied(): pl.pallas_call(kernel, in_specs=[vmem, pl.BlockSpec(memory_space=pltpu.HB...]
    ppermute x7, starting transfers between devices: 10.7 us -> 9.39 us  [onward(): return lax.ppermute(v, ('mom', 'band'), pairs)]
  transfers between devices with their start and end apart: 17 -> 17, of which waited for: 8 -> 8; matrix products, arithmetic and copies ran while one was open for 1% -> 4% of each run, Pallas kernels for 11% -> 14%
where the time goes in v4:
time: 110 us; the launch traced here: 109 us
  waiting for transfers between devices  34.1 us (31%)
  starting transfers between devices  25 us (23%)
  blocking collectives  21.6 us (20%)
  Pallas kernels  21.4 us (19%)
  local copies, waits for them, and re-layouts  3.86 us (4%)
  other arithmetic  3.2 us (3%)
    all_to_all x1, blocking collectives, per_device(): u = lax.all_to_all(coded, 'mom', split_axis=0, concat_axis=0, tiled=True)  21.6 us
    ppermute x7, waiting for transfers between devices, onward(): return lax.ppermute(v, ('mom', 'band'), pairs)  15.6 us
    pallas_call x4, Pallas kernels, contract_occupied(): pl.pallas_call(kernel, in_specs=[vmem, pl.BlockSpec(memory_space=pltpu.HB...  15.3 us
    ppermute x6, waiting for transfers between devices, along(): lax.ppermute(x, 'band', [(i, (i // 2 + d) % 4 * 2 + i % 2) for i in range...  14.1 us
    ppermute x7, starting transfers between devices, onward(): return lax.ppermute(v, ('mom', 'band'), pairs)  9.39 us
    ppermute x6, starting transfers between devices, along(): lax.ppermute(x, 'band', [(i, (i // 2 + d) % 4 * 2 + i % 2) for i in range...  8.38 us
    ppermute x4, starting transfers between devices, across(): return lax.ppermute(x, 'band', [(i, i ^ 1) for i in range(8)])  7.22 us
    pallas_call x1, Pallas kernels, contract_virtual(): pl.pallas_call(kernel, in_specs=[pl.BlockSpec(memory_space=pltpu.SMEM)] *...  4.57 us
  transfers between devices with their start and end apart: 17, of which 8 were waited for; matrix products, arithmetic and copies ran while one was open for 4% of the time, Pallas kernels for 14%

profile of v4, /device:TPU:1, one launch (start us, length us, event | category | flops | bytes accessed | tf_op | source)
XLA Modules:
  0.0 109.4 jit_solution(13035657851305351256)
XLA Ops:
  1.3 2.1 %collective-permute-start.1 = (bf16[4,2,256,128]{3,2,1,0:T(8,128)(2,1)S(1)}, bf16[4,2,256,128]{3,2,1,0:T(8,128)(2,1)S(1)}, u32[]{:S(2)}, u32[]{:S(2)}) collective-permute-start(bf16[4,2,256,128]{3,2,1,0:T(8,128)(2,1)S(1)} %constant_dynamic-slice_fusion), channel_id=1, source_target_pairs={{0,8},{1,33},{2,10},{3,35},{4,12},{5,37},{6,14},{7,39},{8,16},{9,4... | collective-permute-start | bytes 1572872 | tf_op jit(solution)/shard_map/ppermute | solution.py:203
  3.4 1.4 %collective-permute-start.2 = (bf16[4,2,256,128]{3,2,1,0:T(8,128)(2,1)S(1)}, bf16[4,2,256,128]{3,2,1,0:T(8,128)(2,1)S(1)}, u32[]{:S(2)}, u32[]{:S(2)}) collective-permute-start(bf16[4,2,256,128]{3,2,1,0:T(8,128)(2,1)S(1)} %constant_dynamic-slice_fusion), channel_id=1, source_target_pairs={{0,24},{1,97},{2,26},{3,99},{4,28},{5,101},{6,30},{7,103},{8,0},{9... | collective-permute-start | bytes 1572872 | tf_op jit(solution)/shard_map/ppermute | solution.py:203
  4.8 1.6 %collective-permute-start.3 = (bf16[4,2,256,128]{3,2,1,0:T(8,128)(2,1)S(1)}, bf16[4,2,256,128]{3,2,1,0:T(8,128)(2,1)S(1)}, u32[]{:S(2)}, u32[]{:S(2)}) collective-permute-start(bf16[4,2,256,128]{3,2,1,0:T(8,128)(2,1)S(1)} %constant_dynamic-slice_fusion), channel_id=1, source_target_pairs={{0,16},{1,65},{2,18},{3,67},{4,20},{5,69},{6,22},{7,71},{8,24},{9,... | collective-permute-start | bytes 1572872 | tf_op jit(solution)/shard_map/ppermute | solution.py:203
  9.5 3.8 %contract_partner.2 = bf16[4,16,2,32,256]{4,3,2,1,0:T(8,128)(2,1)S(1)} custom-call(bf16[4,16,64]{2,1,0:T(8,128)(2,1)S(1)} %get-tuple-element.37.coef_ref, bf16[2,4,16,256,256]{4,3,2,1,0:T(8,128)(2,1)} %bitcast.45), custom_call_target="tpu_custom_call" | custom-call | flops 1 | bytes 1 | tf_op jit(solution)/shard_map/contract_partner/pallas_call | solution.py:76
  13.4 2.4 %collective-permute-start = (bf16[4,16,2,32,256]{4,3,2,1,0:T(8,128)(2,1)S(1)}, bf16[4,16,2,32,256]{4,3,2,1,0:T(8,128)(2,1)S(1)}, u32[]{:S(2)}, u32[]{:S(2)}) collective-permute-start(bf16[4,16,2,32,256]{4,3,2,1,0:T(8,128)(2,1)S(1)} %contract_partner.2), channel_id=1, source_target_pairs={{0,1},{1,0},{2,3},{3,2},{4,5},{5,4},{6,7},{7,6},{8,9},{9,8},{10,11... | collective-permute-start | bytes 6291464 | tf_op jit(solution)/shard_map/ppermute | solution.py:190
  15.8 3.8 %contract_partner.3 = bf16[4,16,2,32,256]{4,3,2,1,0:T(8,128)(2,1)S(1)} custom-call(bf16[4,16,64]{2,1,0:T(8,128)(2,1)S(1)} %get-tuple-element.37.coef_ref, bf16[2,4,16,256,256]{4,3,2,1,0:T(8,128)(2,1)} %bitcast.46), custom_call_target="tpu_custom_call" | custom-call | flops 1 | bytes 1 | tf_op jit(solution)/shard_map/contract_partner/pallas_call | solution.py:76
  20.9 1.9 %collective-permute-start.5 = (bf16[16,2,256,128]{3,2,1,0:T(8,128)(2,1)S(1)}, bf16[16,2,256,128]{3,2,1,0:T(8,128)(2,1)S(1)}, u32[]{:S(2)}, u32[]{:S(2)}) collective-permute-start(bf16[16,2,256,128]{3,2,1,0:T(8,128)(2,1)S(1)} %pad_maximum_fusion.rest_0_), channel_id=1, source_target_pairs={{0,96},{1,25},{2,98},{3,27},{4,100},{5,29},{6,102},{7,31},{8,104},... | collective-permute-start | bytes 6291464 | tf_op jit(solution)/shard_map/ppermute | solution.py:203
  22.8 3.8 %contract_own.2 = (f32[16,2,32,256]{3,2,1,0:T(8,128)S(1)}, f32[8,2,32,256]{3,2,1,0:T(8,128)S(1)}, f32[8,2,32,256]{3,2,1,0:T(8,128)S(1)}, bf16[16,2,32,256]{3,2,1...) custom-call(bf16[4,16,64]{2,1,0:T(8,128)(2,1)S(1)} %get-tuple-element.38.coef_ref, bf16[2,4,16,256,256]{4,3,2,1,0:T(8,128)(2,1)} %bitcast.47, ...), custom_call_target="tpu_custom_call" | custom-call | flops 1 | bytes 1 | tf_op jit(solution)/shard_map/contract_own/pallas_call | solution.py:76
  26.6 2.8 %collective-permute-start.6 = (bf16[16,2,32,256]{3,2,1,0:T(8,128)(2,1)S(1)}, bf16[16,2,32,256]{3,2,1,0:T(8,128)(2,1)S(1)}, u32[]{:S(2)}, u32[]{:S(2)}) collective-permute-start(bf16[16,2,32,256]{3,2,1,0:T(8,128)(2,1)S(1)} %get-tuple-element.24), channel_id=1, source_target_pairs={{0,6},{1,7},{2,0},{3,1},{4,2},{5,3},{6,4},{7,5},{8,14},{9,15},{10,... | collective-permute-start | bytes 1572872 | tf_op jit(solution)/shard_map/ppermute | solution.py:193
  29.5 3.8 %contract_own.3 = (f32[16,2,32,256]{3,2,1,0:T(8,128)S(1)}, f32[8,2,32,256]{3,2,1,0:T(8,128)S(1)}, f32[8,2,32,256]{3,2,1,0:T(8,128)S(1)}, bf16[16,2,32,256]{3,2,1...) custom-call(bf16[4,16,64]{2,1,0:T(8,128)(2,1)S(1)} %get-tuple-element.38.coef_ref, bf16[2,4,16,256,256]{4,3,2,1,0:T(8,128)(2,1)} %bitcast.48, ...), custom_call_target="tpu_custom_call" | custom-call | flops 1 | bytes 1 | tf_op jit(solution)/shard_map/contract_own/pallas_call | solution.py:76
  34.8 11.7 %collective-permute-done.4.rest_1_ = bf16[16,2,256,128]{3,2,1,0:T(8,128)(2,1)S(1)} collective-permute-done((bf16[16,2,256,128]{3,2,1,0:T(8,128)(2,1)S(1)}, bf16[16,2,256,128]{3,2,1,0:T(8,128)(2,1)S(1)}, u32[]{:S(2)}, u32[]{:S(2)}) %collective-permute-start.4) | collective-permute-done | bytes 2097184 | tf_op jit(solution)/shard_map/ppermute | solution.py:203
  48.1 1.9 %collective-permute-done.8.refs_5_ = bf16[16,2,32,256]{3,2,1,0:T(8,128)(2,1)S(1)} collective-permute-done((bf16[16,2,32,256]{3,2,1,0:T(8,128)(2,1)S(1)}, bf16[16,2,32,256]{3,2,1,0:T(8,128)(2,1)S(1)}, u32[]{:S(2)}, u32[]{:S(2)}) %collective-permute-start.8) | collective-permute-done | bytes 524320 | tf_op jit(solution)/shard_map/ppermute | solution.py:193
  51.7 7.3 %collective-permute-done.12.refs_3_ = bf16[16,2,32,256]{3,2,1,0:T(8,128)(2,1)S(1)} collective-permute-done((bf16[16,2,32,256]{3,2,1,0:T(8,128)(2,1)S(1)}, bf16[16,2,32,256]{3,2,1,0:T(8,128)(2,1)S(1)}, u32[]{:S(2)}, u32[]{:S(2)}) %collective-permute-start.12) | collective-permute-done | bytes 524320 | tf_op jit(solution)/shard_map/ppermute | solution.py:193
  59.2 2.7 %collective-permute-start.14 = (bf16[8,4,32,256]{3,2,1,0:T(8,128)(2,1)S(1)}, bf16[8,4,32,256]{3,2,1,0:T(8,128)(2,1)S(1)}, u32[]{:S(2)}, u32[]{:S(2)}) collective-permute-start(bf16[8,4,32,256]{3,2,1,0:T(8,128)(2,1)S(1)} %pad_maximum_fusion.1), channel_id=1, source_target_pairs={{0,6},{1,7},{2,0},{3,1},{4,2},{5,3},{6,4},{7,5},{8,14},{9,15},{10,... | collective-permute-start | bytes 1572872 | tf_op jit(solution)/shard_map/ppermute | solution.py:193
  61.9 2.2 %collective-permute-done.10.rest_4_ = bf16[8,2,256,128]{3,2,1,0:T(8,128)(2,1)S(1)} collective-permute-done((bf16[8,2,256,128]{3,2,1,0:T(8,128)(2,1)S(1)}, bf16[8,2,256,128]{3,2,1,0:T(8,128)(2,1)S(1)}, u32[]{:S(2)}, u32[]{:S(2)}) %collective-permute-start.10) | collective-permute-done | bytes 1048608 | tf_op jit(solution)/shard_map/ppermute | solution.py:203
  64.1 1.6 %collective-permute-done.9.rest_3_ = bf16[8,2,256,128]{3,2,1,0:T(8,128)(2,1)S(1)} collective-permute-done((bf16[8,2,256,128]{3,2,1,0:T(8,128)(2,1)S(1)}, bf16[8,2,256,128]{3,2,1,0:T(8,128)(2,1)S(1)}, u32[]{:S(2)}, u32[]{:S(2)}) %collective-permute-start.9) | collective-permute-done | bytes 1048608 | tf_op jit(solution)/shard_map/ppermute | solution.py:203
  65.8 5.0 %collective-permute-done.13.refs_6_ = bf16[8,4,32,256]{3,2,1,0:T(8,128)(2,1)S(1)} collective-permute-done((bf16[8,4,32,256]{3,2,1,0:T(8,128)(2,1)S(1)}, bf16[8,4,32,256]{3,2,1,0:T(8,128)(2,1)S(1)}, u32[]{:S(2)}, u32[]{:S(2)}) %collective-permute-start.13) | collective-permute-done | bytes 524320 | tf_op jit(solution)/shard_map/ppermute | solution.py:193
  70.8 1.5 %code_sums.1 = s16[16,144,256]{2,1,0:T(8,128)(2,1)S(1)} custom-call(f32[16,2,32,256]{3,2,1,0:T(8,128)S(1)} %get-tuple-element.29.refs_0_, f32[16,2,32,256]{3,2,1,0:T(8,128)S(1)} %get-tuple-element.30.refs_1_, bf16[16,2,32,256]{3,2,1,0:T(8,128)(2,1)S(1)} %collective-permute-done.11.refs_2_, bf16[16,2,32,256]{3,2,1,0:T(8,128)(2,1)S(1)} %collective-permute-done.12.refs_3_, ...), custom_call_target="tpu_custom_call" | custom-call | flops 1 | bytes 1 | tf_op jit(solution)/shard_map/code_sums/pallas_call | solution.py:115
  72.3 21.6 %all_to_all.5.u_ref = s16[16,144,256]{2,1,0:T(8,128)(2,1)S(1)} all-to-all(s16[16,144,256]{2,1,0:T(8,128)(2,1)S(1)} %code_sums.1), channel_id=1, replica_groups=mesh['mom'=16,'band'=8] {'mom'}, dimensions={0} | all-to-all | bytes 2359296 | tf_op jit(solution)/shard_map/all_to_all | solution.py:246
  93.8 4.2 %collective-permute-start.15 = (s16[16,144,256]{2,1,0:T(8,128)(2,1)S(1)}, s16[16,144,256]{2,1,0:T(8,128)(2,1)S(1)}, u32[]{:S(2)}, u32[]{:S(2)}) collective-permute-start(s16[16,144,256]{2,1,0:T(8,128)(2,1)S(1)} %all_to_all.5.u_ref), channel_id=1, source_target_pairs={{0,1},{1,0},{2,3},{3,2},{4,5},{5,4},{6,7},{7,6},{8,9},{9,8},{10,11... | collective-permute-start | bytes 3538952 | tf_op jit(solution)/shard_map/ppermute | solution.py:190
  98.4 2.1 %collective-permute-done.15.pair_ref = s16[16,144,256]{2,1,0:T(8,128)(2,1)S(1)} collective-permute-done((s16[16,144,256]{2,1,0:T(8,128)(2,1)S(1)}, s16[16,144,256]{2,1,0:T(8,128)(2,1)S(1)}, u32[]{:S(2)}, u32[]{:S(2)}) %collective-permute-start.15) | collective-permute-done | bytes 1179680 | tf_op jit(solution)/shard_map/ppermute | solution.py:190
  100.5 4.6 %contract_virtual.1 = (f32[2,64,16,128]{3,2,1,0:T(8,128)S(1)}, f32[2,64,16,128]{3,2,1,0:T(8,128)S(1)}) custom-call(s32[64]{0:T(128)S(1)} %fusion.5.k4_ref, s32[64]{0:T(128)S(1)} %select_reduce_fusion.k2_ref, f32[64,128]{1,0:T(8,128)S(1)} %dynamic-slice_convert_fusion.mask_ref, s16[16,144,256]{2,1,0:T(8,128)(2,1)S(1)} %all_to_all.5.u_ref, ...), custom_call_target="tpu_custom_call" | custom-call | flops 1 | bytes 1 | tf_op jit(solution)/shard_map/contract_virtual/pallas_call | solution.py:167
  105.6 2.3 %collective-permute-done.16 = f32[2,64,16,128]{3,2,1,0:T(8,128)S(1)} collective-permute-done((f32[2,64,16,128]{3,2,1,0:T(8,128)S(1)}, f32[2,64,16,128]{3,2,1,0:T(8,128)S(1)}, u32[]{:S(2)}, u32[]{:S(2)}) %collective-permute-start.16) | collective-permute-done | bytes 1048608 | tf_op jit(solution)/shard_map/ppermute | solution.py:190
  107.9 1.6 %maximum_select_fusion = f32[2,64,1,2,8,256]{5,4,3,2,1,0:T(8,128)} fusion(f32[2,64,1,2,8,128]{5,4,3,2,1,0:T(8,128)S(1)} %bitcast.49, f32[2,64,1,2,8,128]{5,4,3,2,1,0:T(8,128)S(1)} %bitcast.44, pred[]{:T(512)S(6)} %eq.30), kind=kLoop, calls=%fused_computation.2 | loop fusion | flops 1572864 | bytes 4194305 | tf_op jit(solution)/shard_map/jit(_where)/select_n | solution.py:254
  (67 shorter events, 11.3 us)
Async XLA Ops:
  1.3 18.4 %collective-permute-start.1 = (bf16[4,2,256,128]{3,2,1,0:T(8,128)(2,1)S(1)}, bf16[4,2,256,128]{3,2,1,0:T(8,128)(2,1)S(1)}, u32[]{:S(2)}, u32[]{:S(2)}) collective-permute-start(bf16[4,2,256,128]{3,2,1,0:T(8,128)(2,1)S(1)} %constant_dynamic-slice_fusion), channel_id=1, source_target_pairs={{0,8},{1,33},{2,10},{3,35},{4,12},{5,37},{6,14},{7,39},{8,16},{9,4... | collective-permute-start | bytes 1572872 | tf_op jit(solution)/shard_map/ppermute | solution.py:203
  3.4 16.3 %collective-permute-start.2 = (bf16[4,2,256,128]{3,2,1,0:T(8,128)(2,1)S(1)}, bf16[4,2,256,128]{3,2,1,0:T(8,128)(2,1)S(1)}, u32[]{:S(2)}, u32[]{:S(2)}) collective-permute-start(bf16[4,2,256,128]{3,2,1,0:T(8,128)(2,1)S(1)} %constant_dynamic-slice_fusion), channel_id=1, source_target_pairs={{0,24},{1,97},{2,26},{3,99},{4,28},{5,101},{6,30},{7,103},{8,0},{9... | collective-permute-start | bytes 1572872 | tf_op jit(solution)/shard_map/ppermute | solution.py:203
  4.8 15.0 %collective-permute-start.3 = (bf16[4,2,256,128]{3,2,1,0:T(8,128)(2,1)S(1)}, bf16[4,2,256,128]{3,2,1,0:T(8,128)(2,1)S(1)}, u32[]{:S(2)}, u32[]{:S(2)}) collective-permute-start(bf16[4,2,256,128]{3,2,1,0:T(8,128)(2,1)S(1)} %constant_dynamic-slice_fusion), channel_id=1, source_target_pairs={{0,16},{1,65},{2,18},{3,67},{4,20},{5,69},{6,22},{7,71},{8,24},{9,... | collective-permute-start | bytes 1572872 | tf_op jit(solution)/shard_map/ppermute | solution.py:203
  13.4 9.4 %collective-permute-start = (bf16[4,16,2,32,256]{4,3,2,1,0:T(8,128)(2,1)S(1)}, bf16[4,16,2,32,256]{4,3,2,1,0:T(8,128)(2,1)S(1)}, u32[]{:S(2)}, u32[]{:S(2)}) collective-permute-start(bf16[4,16,2,32,256]{4,3,2,1,0:T(8,128)(2,1)S(1)} %contract_partner.2), channel_id=1, source_target_pairs={{0,1},{1,0},{2,3},{3,2},{4,5},{5,4},{6,7},{7,6},{8,9},{9,8},{10,11... | collective-permute-start | bytes 6291464 | tf_op jit(solution)/shard_map/ppermute | solution.py:190
  19.6 9.8 %collective-permute-start.7 = (bf16[4,16,2,32,256]{4,3,2,1,0:T(8,128)(2,1)S(1)}, bf16[4,16,2,32,256]{4,3,2,1,0:T(8,128)(2,1)S(1)}, u32[]{:S(2)}, u32[]{:S(2)}) collective-permute-start(bf16[4,16,2,32,256]{4,3,2,1,0:T(8,128)(2,1)S(1)} %contract_partner.3), channel_id=1, source_target_pairs={{0,1},{1,0},{2,3},{3,2},{4,5},{5,4},{6,7},{7,6},{8,9},{9,8},{10,11... | collective-permute-start | bytes 6291464 | tf_op jit(solution)/shard_map/ppermute | solution.py:190
  20.0 6.6 %copy-start.2 = (bf16[16,2,256,128]{3,2,1,0:T(8,128)(2,1)}, bf16[16,2,256,128]{3,2,1,0:T(8,128)(2,1)S(1)}, u32[]{:S(2)}) copy-start(bf16[16,2,256,128]{3,2,1,0:T(8,128)(2,1)S(1)} %pad_maximum_fusion.rest_0_) | copy-start | bytes 6291460
  20.1 26.5 %collective-permute-start.4 = (bf16[16,2,256,128]{3,2,1,0:T(8,128)(2,1)S(1)}, bf16[16,2,256,128]{3,2,1,0:T(8,128)(2,1)S(1)}, u32[]{:S(2)}, u32[]{:S(2)}) collective-permute-start(bf16[16,2,256,128]{3,2,1,0:T(8,128)(2,1)S(1)} %pad_maximum_fusion.rest_0_), channel_id=1, source_target_pairs={{0,32},{1,9},{2,34},{3,11},{4,36},{5,13},{6,38},{7,15},{8,40},{9,1... | collective-permute-start | bytes 6291464 | tf_op jit(solution)/shard_map/ppermute | solution.py:203
  20.9 27.0 %collective-permute-start.5 = (bf16[16,2,256,128]{3,2,1,0:T(8,128)(2,1)S(1)}, bf16[16,2,256,128]{3,2,1,0:T(8,128)(2,1)S(1)}, u32[]{:S(2)}, u32[]{:S(2)}) collective-permute-start(bf16[16,2,256,128]{3,2,1,0:T(8,128)(2,1)S(1)} %pad_maximum_fusion.rest_0_), channel_id=1, source_target_pairs={{0,96},{1,25},{2,98},{3,27},{4,100},{5,29},{6,102},{7,31},{8,104},... | collective-permute-start | bytes 6291464 | tf_op jit(solution)/shard_map/ppermute | solution.py:203
  26.6 21.3 %collective-permute-start.6 = (bf16[16,2,32,256]{3,2,1,0:T(8,128)(2,1)S(1)}, bf16[16,2,32,256]{3,2,1,0:T(8,128)(2,1)S(1)}, u32[]{:S(2)}, u32[]{:S(2)}) collective-permute-start(bf16[16,2,32,256]{3,2,1,0:T(8,128)(2,1)S(1)} %get-tuple-element.24), channel_id=1, source_target_pairs={{0,6},{1,7},{2,0},{3,1},{4,2},{5,3},{6,4},{7,5},{8,14},{9,15},{10,... | collective-permute-start | bytes 1572872 | tf_op jit(solution)/shard_map/ppermute | solution.py:193
  33.3 16.7 %collective-permute-start.8 = (bf16[16,2,32,256]{3,2,1,0:T(8,128)(2,1)S(1)}, bf16[16,2,32,256]{3,2,1,0:T(8,128)(2,1)S(1)}, u32[]{:S(2)}, u32[]{:S(2)}) collective-permute-start(bf16[16,2,32,256]{3,2,1,0:T(8,128)(2,1)S(1)} %get-tuple-element.26), channel_id=1, source_target_pairs={{0,6},{1,7},{2,0},{3,1},{4,2},{5,3},{6,4},{7,5},{8,14},{9,15},{10,... | collective-permute-start | bytes 1572872 | tf_op jit(solution)/shard_map/ppermute | solution.py:193
  33.8 17.8 %collective-permute-start.11 = (bf16[16,2,32,256]{3,2,1,0:T(8,128)(2,1)S(1)}, bf16[16,2,32,256]{3,2,1,0:T(8,128)(2,1)S(1)}, u32[]{:S(2)}, u32[]{:S(2)}) collective-permute-start(bf16[16,2,32,256]{3,2,1,0:T(8,128)(2,1)S(1)} %get-tuple-element.31), channel_id=1, source_target_pairs={{0,2},{1,3},{2,4},{3,5},{4,6},{5,7},{6,0},{7,1},{8,10},{9,11},{10,... | collective-permute-start | bytes 1572872 | tf_op jit(solution)/shard_map/ppermute | solution.py:193
  46.5 1.5 %copy-start.3 = (bf16[16,2,256,128]{3,2,1,0:T(8,128)(2,1)}, bf16[16,2,256,128]{3,2,1,0:T(8,128)(2,1)S(1)}, u32[]{:S(2)}) copy-start(bf16[16,2,256,128]{3,2,1,0:T(8,128)(2,1)S(1)} %collective-permute-done.4.rest_1_) | copy-start | bytes 6291460
  46.5 12.5 %collective-permute-start.12 = (bf16[16,2,32,256]{3,2,1,0:T(8,128)(2,1)S(1)}, bf16[16,2,32,256]{3,2,1,0:T(8,128)(2,1)S(1)}, u32[]{:S(2)}, u32[]{:S(2)}) collective-permute-start(bf16[16,2,32,256]{3,2,1,0:T(8,128)(2,1)S(1)} %get-tuple-element.32), channel_id=1, source_target_pairs={{0,2},{1,3},{2,4},{3,5},{4,6},{5,7},{6,0},{7,1},{8,10},{9,11},{10,... | collective-permute-start | bytes 1572872 | tf_op jit(solution)/shard_map/ppermute | solution.py:193
  47.9 2.1 %copy-start.4 = (bf16[16,2,256,128]{3,2,1,0:T(8,128)(2,1)}, bf16[16,2,256,128]{3,2,1,0:T(8,128)(2,1)S(1)}, u32[]{:S(2)}) copy-start(bf16[16,2,256,128]{3,2,1,0:T(8,128)(2,1)S(1)} %collective-permute-done.5.rest_2_) | copy-start | bytes 6291460
  50.0 20.7 %copy-start.1 = (s32[4,16]{1,0:T(4,128)S(1)}, s32[4,16]{1,0:T(4,128)}, u32[]{:S(2)}) copy-start(s32[4,16]{1,0:T(4,128)} %refs_8_.1) | copy-start | bytes 772
  50.1 14.0 %collective-permute-start.10 = (bf16[8,2,256,128]{3,2,1,0:T(8,128)(2,1)S(1)}, bf16[8,2,256,128]{3,2,1,0:T(8,128)(2,1)S(1)}, u32[]{:S(2)}, u32[]{:S(2)}) collective-permute-start(bf16[8,2,256,128]{3,2,1,0:T(8,128)(2,1)S(1)} %slice.63), channel_id=1, source_target_pairs={{0,96},{1,25},{2,98},{3,27},{4,100},{5,29},{6,102},{7,31},{8,104},... | collective-permute-start | bytes 3145736 | tf_op jit(solution)/shard_map/ppermute | solution.py:203
  50.6 15.2 %collective-permute-start.9 = (bf16[8,2,256,128]{3,2,1,0:T(8,128)(2,1)S(1)}, bf16[8,2,256,128]{3,2,1,0:T(8,128)(2,1)S(1)}, u32[]{:S(2)}, u32[]{:S(2)}) collective-permute-start(bf16[8,2,256,128]{3,2,1,0:T(8,128)(2,1)S(1)} %slice.62), channel_id=1, source_target_pairs={{0,32},{1,9},{2,34},{3,11},{4,36},{5,13},{6,38},{7,15},{8,40},{9,1... | collective-permute-start | bytes 3145736 | tf_op jit(solution)/shard_map/ppermute | solution.py:203
  59.1 11.6 %collective-permute-start.13 = (bf16[8,4,32,256]{3,2,1,0:T(8,128)(2,1)S(1)}, bf16[8,4,32,256]{3,2,1,0:T(8,128)(2,1)S(1)}, u32[]{:S(2)}, u32[]{:S(2)}) collective-permute-start(bf16[8,4,32,256]{3,2,1,0:T(8,128)(2,1)S(1)} %pad_maximum_fusion.2), channel_id=1, source_target_pairs={{0,2},{1,3},{2,4},{3,5},{4,6},{5,7},{6,0},{7,1},{8,10},{9,11},{10,... | collective-permute-start | bytes 1572872 | tf_op jit(solution)/shard_map/ppermute | solution.py:193
  59.2 11.5 %collective-permute-start.14 = (bf16[8,4,32,256]{3,2,1,0:T(8,128)(2,1)S(1)}, bf16[8,4,32,256]{3,2,1,0:T(8,128)(2,1)S(1)}, u32[]{:S(2)}, u32[]{:S(2)}) collective-permute-start(bf16[8,4,32,256]{3,2,1,0:T(8,128)(2,1)S(1)} %pad_maximum_fusion.1), channel_id=1, source_target_pairs={{0,6},{1,7},{2,0},{3,1},{4,2},{5,3},{6,4},{7,5},{8,14},{9,15},{10,... | collective-permute-start | bytes 1572872 | tf_op jit(solution)/shard_map/ppermute | solution.py:193
  64.1 6.6 %copy-start.5 = (bf16[8,2,256,128]{3,2,1,0:T(8,128)(2,1)}, bf16[8,2,256,128]{3,2,1,0:T(8,128)(2,1)S(1)}, u32[]{:S(2)}) copy-start(bf16[8,2,256,128]{3,2,1,0:T(8,128)(2,1)S(1)} %collective-permute-done.10.rest_4_) | copy-start | bytes 3145732
  65.8 5.0 %copy-start.6 = (bf16[8,2,256,128]{3,2,1,0:T(8,128)(2,1)}, bf16[8,2,256,128]{3,2,1,0:T(8,128)(2,1)S(1)}, u32[]{:S(2)}) copy-start(bf16[8,2,256,128]{3,2,1,0:T(8,128)(2,1)S(1)} %collective-permute-done.9.rest_3_) | copy-start | bytes 3145732
  72.3 25.8 %copy-start.7 = (s32[64,256]{1,0:T(8,128)S(1)}, s32[64,256]{1,0:T(8,128)}, u32[]{:S(2)}) copy-start(s32[64,256]{1,0:T(8,128)} %param.10) | copy-start | bytes 196612
  93.8 6.7 %collective-permute-start.15 = (s16[16,144,256]{2,1,0:T(8,128)(2,1)S(1)}, s16[16,144,256]{2,1,0:T(8,128)(2,1)S(1)}, u32[]{:S(2)}, u32[]{:S(2)}) collective-permute-start(s16[16,144,256]{2,1,0:T(8,128)(2,1)S(1)} %all_to_all.5.u_ref), channel_id=1, source_target_pairs={{0,1},{1,0},{2,3},{3,2},{4,5},{5,4},{6,7},{7,6},{8,9},{9,8},{10,11... | collective-permute-start | bytes 3538952 | tf_op jit(solution)/shard_map/ppermute | solution.py:190
  105.1 2.7 %collective-permute-start.16 = (f32[2,64,16,128]{3,2,1,0:T(8,128)S(1)}, f32[2,64,16,128]{3,2,1,0:T(8,128)S(1)}, u32[]{:S(2)}, u32[]{:S(2)}) collective-permute-start(f32[2,64,16,128]{3,2,1,0:T(8,128)S(1)} %get-tuple-element.36), channel_id=1, source_target_pairs={{0,1},{1,0},{2,3},{3,2},{4,5},{5,4},{6,7},{7,6},{8,9},{9,8},{10,11... | collective-permute-start | bytes 3145736 | tf_op jit(solution)/shard_map/ppermute | solution.py:190
  (1 other events, 1.2 us)

commit v5 on v4

--- a/solution.py
+++ b/solution.py
@@ -93,15 +93,15 @@
     n = len(owns)
 
     def kernel(*refs):
-        own_refs, up_refs, down_refs = refs[:n], refs[n : 2 * n], refs[2 * n : 3 * n]
-        right_ref, left_ref, table_ref, out_ref = refs[3 * n :]
+        own_refs, down_refs = refs[:n], refs[n : 2 * n]
+        up_ref, right_ref, left_ref, table_ref, out_ref = refs[2 * n :]
         line = lax.broadcasted_iota(jnp.int32, (16, 256), 0)
         lane = lax.broadcasted_iota(jnp.int32, (16, 256), 1)
         for t in range(16):
             extra = jnp.zeros((16, 256), jnp.int32)
             for k in range(4):
                 i, c = k // COUNT, k % COUNT
-                sums = own_refs[i][t, c] + (down_refs if t < 8 else up_refs)[i][t, c].astype(jnp.float32)
+                sums = own_refs[i][t, c] + (down_refs[i][t, c] if t < 8 else up_ref[t, k]).astype(jnp.float32)
                 sums = sums + (right_ref[t, k] if t < 8 else left_ref[t - 8, k]).astype(jnp.float32)
                 most = jnp.max(jnp.max(jnp.abs(sums), axis=0, keepdims=True), axis=1, keepdims=True)
                 power = jnp.floor(jnp.log2(jnp.maximum(most, 1e-30))) + 1.0
@@ -114,13 +114,13 @@
     vmem = pl.BlockSpec(memory_space=pltpu.VMEM)
     return pl.pallas_call(
         kernel,
-        in_specs=[vmem] * (3 * n + 2) + [pl.BlockSpec(memory_space=pltpu.SMEM)],
+        in_specs=[vmem] * (2 * n + 3) + [pl.BlockSpec(memory_space=pltpu.SMEM)],
         out_specs=vmem,
         out_shape=jax.ShapeDtypeStruct((16, 144, 256), jnp.int16),
         compiler_params=pltpu.CompilerParams(vmem_limit_bytes=18 * MIB),
         cost_estimate=LIGHT,
         name="code_sums",
-    )(*owns, *ups, *downs, right, left, table)
+    )(*owns, *downs, ups, right, left, table)
 
 
 def contract_virtual(k4, k2, mask, held, u, pair):
@@ -234,10 +234,11 @@
     arrived[0] = after(arrived[0], row)
     sent = [contract_occupied(coef_own, ints, first, got) for first, got in zip(chunks, arrived)]
     owns, rights, lefts = [x[0] for x in sent], [x[1] for x in sent], [x[2] for x in sent]
-    ups, downs = [along(x[3], 1) for x in sent], [along(x[4], -1) for x in sent]
-    right = [(r + x[:8].astype(jnp.float32)).astype(jnp.bfloat16) for r, x in zip(rights, ups)]
+    ups = along(jnp.concatenate([x[3] for x in sent], axis=1), 1)
+    downs = [along(x[4], -1) for x in sent]
+    right = (jnp.concatenate(rights, axis=1) + ups[:8].astype(jnp.float32)).astype(jnp.bfloat16)
     left = [(r + x[8:].astype(jnp.float32)).astype(jnp.bfloat16) for r, x in zip(lefts, downs)]
-    right, left = jnp.concatenate(right, axis=1), jnp.concatenate(left, axis=1)
+    left = jnp.concatenate(left, axis=1)
     low, high = lax.optimization_barrier((below[:8], above[8:], left))[:2]
     opposite = [onward(low, True, 1), onward(high, True, -1)]
     held = [row, below, above] + opposite

time: 110 us -> 108 us (0.982)
  waiting for transfers between devices: 34.1 us -> 31.4 us
  local copies, waits for them, and re-layouts: 3.86 us -> 5.02 us
    ppermute x6 -> x5, waiting for transfers between devices: 14.1 us -> 7.68 us  [along(): lax.ppermute(x, 'band', [(i, (i // 2 + d) % 4 * 2 + i % 2) for i in range...]
    ppermute x7, waiting for transfers between devices: 15.6 us -> 19.3 us  [onward(): return lax.ppermute(v, ('mom', 'band'), pairs)]
    unnamed x17, local copies, waits for them, and re-layouts: 1.59 us -> 2.72 us
    ppermute x6 -> x5, starting transfers between devices: 8.38 us -> 8.07 us  [along(): lax.ppermute(x, 'band', [(i, (i // 2 + d) % 4 * 2 + i % 2) for i in range...]
  transfers between devices with their start and end apart: 17 -> 16, of which waited for: 8 -> 8; matrix products, arithmetic and copies ran while one was open for 4% -> 4% of each run, Pallas kernels for 14% -> 14%
where the time goes in v5:
time: 108 us
  waiting for transfers between devices  31.4 us (29%)
  starting transfers between devices  25 us (23%)
  Pallas kernels  21.4 us (20%)
  blocking collectives  21.2 us (20%)
  local copies, waits for them, and re-layouts  5.02 us (5%)
  other arithmetic  3.27 us (3%)
    all_to_all x1, blocking collectives, per_device(): u = lax.all_to_all(coded, 'mom', split_axis=0, concat_axis=0, tiled=True)  21.2 us
    ppermute x7, waiting for transfers between devices, onward(): return lax.ppermute(v, ('mom', 'band'), pairs)  19.3 us
    pallas_call x4, Pallas kernels, contract_occupied(): pl.pallas_call(kernel, in_specs=[vmem, pl.BlockSpec(memory_space=pltpu.HB...  15.3 us
    ppermute x7, starting transfers between devices, onward(): return lax.ppermute(v, ('mom', 'band'), pairs)  9.39 us
    ppermute x5, starting transfers between devices, along(): lax.ppermute(x, 'band', [(i, (i // 2 + d) % 4 * 2 + i % 2) for i in range...  8.07 us
    ppermute x5, waiting for transfers between devices, along(): lax.ppermute(x, 'band', [(i, (i // 2 + d) % 4 * 2 + i % 2) for i in range...  7.68 us
    ppermute x4, starting transfers between devices, across(): return lax.ppermute(x, 'band', [(i, i ^ 1) for i in range(8)])  7.56 us
    pallas_call x1, Pallas kernels, contract_virtual(): pl.pallas_call(kernel, in_specs=[pl.BlockSpec(memory_space=pltpu.SMEM)] *...  4.57 us
  transfers between devices with their start and end apart: 16, of which 8 were waited for; matrix products, arithmetic and copies ran while one was open for 4% of the time, Pallas kernels for 14%

profile of v5, /device:TPU:1, one launch (start us, length us, event | category | flops | bytes accessed | tf_op | source)
XLA Modules:
  0.0 107.6 jit_solution(5796822340825167615)
XLA Ops:
  1.3 2.1 %collective-permute-start.1 = (bf16[4,2,256,128]{3,2,1,0:T(8,128)(2,1)S(1)}, bf16[4,2,256,128]{3,2,1,0:T(8,128)(2,1)S(1)}, u32[]{:S(2)}, u32[]{:S(2)}) collective-permute-start(bf16[4,2,256,128]{3,2,1,0:T(8,128)(2,1)S(1)} %constant_dynamic-slice_fusion), channel_id=1, source_target_pairs={{0,8},{1,33},{2,10},{3,35},{4,12},{5,37},{6,14},{7,39},{8,16},{9,4... | collective-permute-start | bytes 1572872 | tf_op jit(solution)/shard_map/ppermute | solution.py:203
  3.4 1.4 %collective-permute-start.2 = (bf16[4,2,256,128]{3,2,1,0:T(8,128)(2,1)S(1)}, bf16[4,2,256,128]{3,2,1,0:T(8,128)(2,1)S(1)}, u32[]{:S(2)}, u32[]{:S(2)}) collective-permute-start(bf16[4,2,256,128]{3,2,1,0:T(8,128)(2,1)S(1)} %constant_dynamic-slice_fusion), channel_id=1, source_target_pairs={{0,24},{1,97},{2,26},{3,99},{4,28},{5,101},{6,30},{7,103},{8,0},{9... | collective-permute-start | bytes 1572872 | tf_op jit(solution)/shard_map/ppermute | solution.py:203
  4.8 1.6 %collective-permute-start.3 = (bf16[4,2,256,128]{3,2,1,0:T(8,128)(2,1)S(1)}, bf16[4,2,256,128]{3,2,1,0:T(8,128)(2,1)S(1)}, u32[]{:S(2)}, u32[]{:S(2)}) collective-permute-start(bf16[4,2,256,128]{3,2,1,0:T(8,128)(2,1)S(1)} %constant_dynamic-slice_fusion), channel_id=1, source_target_pairs={{0,16},{1,65},{2,18},{3,67},{4,20},{5,69},{6,22},{7,71},{8,24},{9,... | collective-permute-start | bytes 1572872 | tf_op jit(solution)/shard_map/ppermute | solution.py:203
  9.5 3.8 %contract_partner.2 = bf16[4,16,2,32,256]{4,3,2,1,0:T(8,128)(2,1)S(1)} custom-call(bf16[4,16,64]{2,1,0:T(8,128)(2,1)S(1)} %get-tuple-element.37.coef_ref, bf16[2,4,16,256,256]{4,3,2,1,0:T(8,128)(2,1)} %bitcast.45), custom_call_target="tpu_custom_call" | custom-call | flops 1 | bytes 1 | tf_op jit(solution)/shard_map/contract_partner/pallas_call | solution.py:76
  13.4 2.4 %collective-permute-start = (bf16[4,16,2,32,256]{4,3,2,1,0:T(8,128)(2,1)S(1)}, bf16[4,16,2,32,256]{4,3,2,1,0:T(8,128)(2,1)S(1)}, u32[]{:S(2)}, u32[]{:S(2)}) collective-permute-start(bf16[4,16,2,32,256]{4,3,2,1,0:T(8,128)(2,1)S(1)} %contract_partner.2), channel_id=1, source_target_pairs={{0,1},{1,0},{2,3},{3,2},{4,5},{5,4},{6,7},{7,6},{8,9},{9,8},{10,11... | collective-permute-start | bytes 6291464 | tf_op jit(solution)/shard_map/ppermute | solution.py:190
  15.8 3.8 %contract_partner.3 = bf16[4,16,2,32,256]{4,3,2,1,0:T(8,128)(2,1)S(1)} custom-call(bf16[4,16,64]{2,1,0:T(8,128)(2,1)S(1)} %get-tuple-element.37.coef_ref, bf16[2,4,16,256,256]{4,3,2,1,0:T(8,128)(2,1)} %bitcast.46), custom_call_target="tpu_custom_call" | custom-call | flops 1 | bytes 1 | tf_op jit(solution)/shard_map/contract_partner/pallas_call | solution.py:76
  20.9 1.9 %collective-permute-start.5 = (bf16[16,2,256,128]{3,2,1,0:T(8,128)(2,1)S(1)}, bf16[16,2,256,128]{3,2,1,0:T(8,128)(2,1)S(1)}, u32[]{:S(2)}, u32[]{:S(2)}) collective-permute-start(bf16[16,2,256,128]{3,2,1,0:T(8,128)(2,1)S(1)} %pad_maximum_fusion.rest_0_), channel_id=1, source_target_pairs={{0,96},{1,25},{2,98},{3,27},{4,100},{5,29},{6,102},{7,31},{8,104},... | collective-permute-start | bytes 6291464 | tf_op jit(solution)/shard_map/ppermute | solution.py:203
  22.8 3.8 %contract_own.2 = (f32[16,2,32,256]{3,2,1,0:T(8,128)S(1)}, f32[8,2,32,256]{3,2,1,0:T(8,128)S(1)}, f32[8,2,32,256]{3,2,1,0:T(8,128)S(1)}, bf16[16,2,32,256]{3,2,1...) custom-call(bf16[4,16,64]{2,1,0:T(8,128)(2,1)S(1)} %get-tuple-element.38.coef_ref, bf16[2,4,16,256,256]{4,3,2,1,0:T(8,128)(2,1)} %bitcast.47, ...), custom_call_target="tpu_custom_call" | custom-call | flops 1 | bytes 1 | tf_op jit(solution)/shard_map/contract_own/pallas_call | solution.py:76
  26.6 2.8 %collective-permute-start.6 = (bf16[16,2,32,256]{3,2,1,0:T(8,128)(2,1)S(1)}, bf16[16,2,32,256]{3,2,1,0:T(8,128)(2,1)S(1)}, u32[]{:S(2)}, u32[]{:S(2)}) collective-permute-start(bf16[16,2,32,256]{3,2,1,0:T(8,128)(2,1)S(1)} %get-tuple-element.24), channel_id=1, source_target_pairs={{0,6},{1,7},{2,0},{3,1},{4,2},{5,3},{6,4},{7,5},{8,14},{9,15},{10,... | collective-permute-start | bytes 1572872 | tf_op jit(solution)/shard_map/ppermute | solution.py:193
  29.5 3.8 %contract_own.3 = (f32[16,2,32,256]{3,2,1,0:T(8,128)S(1)}, f32[8,2,32,256]{3,2,1,0:T(8,128)S(1)}, f32[8,2,32,256]{3,2,1,0:T(8,128)S(1)}, bf16[16,2,32,256]{3,2,1...) custom-call(bf16[4,16,64]{2,1,0:T(8,128)(2,1)S(1)} %get-tuple-element.38.coef_ref, bf16[2,4,16,256,256]{4,3,2,1,0:T(8,128)(2,1)} %bitcast.48, ...), custom_call_target="tpu_custom_call" | custom-call | flops 1 | bytes 1 | tf_op jit(solution)/shard_map/contract_own/pallas_call | solution.py:76
  35.2 11.3 %collective-permute-done.4.rest_1_ = bf16[16,2,256,128]{3,2,1,0:T(8,128)(2,1)S(1)} collective-permute-done((bf16[16,2,256,128]{3,2,1,0:T(8,128)(2,1)S(1)}, bf16[16,2,256,128]{3,2,1,0:T(8,128)(2,1)S(1)}, u32[]{:S(2)}, u32[]{:S(2)}) %collective-permute-start.4) | collective-permute-done | bytes 2097184 | tf_op jit(solution)/shard_map/ppermute | solution.py:203
  47.9 2.0 %collective-permute-done.8.refs_3_ = bf16[16,2,32,256]{3,2,1,0:T(8,128)(2,1)S(1)} collective-permute-done((bf16[16,2,32,256]{3,2,1,0:T(8,128)(2,1)S(1)}, bf16[16,2,32,256]{3,2,1,0:T(8,128)(2,1)S(1)}, u32[]{:S(2)}, u32[]{:S(2)}) %collective-permute-start.8) | collective-permute-done | bytes 524320 | tf_op jit(solution)/shard_map/ppermute | solution.py:193
  51.6 3.4 %collective-permute-start.13 = (bf16[8,4,32,256]{3,2,1,0:T(8,128)(2,1)S(1)}, bf16[8,4,32,256]{3,2,1,0:T(8,128)(2,1)S(1)}, u32[]{:S(2)}, u32[]{:S(2)}) collective-permute-start(bf16[8,4,32,256]{3,2,1,0:T(8,128)(2,1)S(1)} %pad_maximum_fusion.2), channel_id=1, source_target_pairs={{0,6},{1,7},{2,0},{3,1},{4,2},{5,3},{6,4},{7,5},{8,14},{9,15},{10,... | collective-permute-start | bytes 1572872 | tf_op jit(solution)/shard_map/ppermute | solution.py:193
  55.0 2.5 %collective-permute-done.11.refs_4_ = bf16[16,4,32,256]{3,2,1,0:T(8,128)(2,1)S(1)} collective-permute-done((bf16[16,4,32,256]{3,2,1,0:T(8,128)(2,1)S(1)}, bf16[16,4,32,256]{3,2,1,0:T(8,128)(2,1)S(1)}, u32[]{:S(2)}, u32[]{:S(2)}) %collective-permute-start.11) | collective-permute-done | bytes 1048608 | tf_op jit(solution)/shard_map/ppermute | solution.py:193
  57.8 6.3 %collective-permute-done.10.rest_4_ = bf16[8,2,256,128]{3,2,1,0:T(8,128)(2,1)S(1)} collective-permute-done((bf16[8,2,256,128]{3,2,1,0:T(8,128)(2,1)S(1)}, bf16[8,2,256,128]{3,2,1,0:T(8,128)(2,1)S(1)}, u32[]{:S(2)}, u32[]{:S(2)}) %collective-permute-start.10) | collective-permute-done | bytes 1048608 | tf_op jit(solution)/shard_map/ppermute | solution.py:203
  64.1 1.7 %collective-permute-done.9.rest_3_ = bf16[8,2,256,128]{3,2,1,0:T(8,128)(2,1)S(1)} collective-permute-done((bf16[8,2,256,128]{3,2,1,0:T(8,128)(2,1)S(1)}, bf16[8,2,256,128]{3,2,1,0:T(8,128)(2,1)S(1)}, u32[]{:S(2)}, u32[]{:S(2)}) %collective-permute-start.9) | collective-permute-done | bytes 1048608 | tf_op jit(solution)/shard_map/ppermute | solution.py:203
  65.8 3.2 %collective-permute-done.12.refs_5_ = bf16[8,4,32,256]{3,2,1,0:T(8,128)(2,1)S(1)} collective-permute-done((bf16[8,4,32,256]{3,2,1,0:T(8,128)(2,1)S(1)}, bf16[8,4,32,256]{3,2,1,0:T(8,128)(2,1)S(1)}, u32[]{:S(2)}, u32[]{:S(2)}) %collective-permute-start.12) | collective-permute-done | bytes 524320 | tf_op jit(solution)/shard_map/ppermute | solution.py:193
  69.0 1.5 %code_sums.1 = s16[16,144,256]{2,1,0:T(8,128)(2,1)S(1)} custom-call(f32[16,2,32,256]{3,2,1,0:T(8,128)S(1)} %get-tuple-element.29.refs_0_, f32[16,2,32,256]{3,2,1,0:T(8,128)S(1)} %get-tuple-element.30.refs_1_, bf16[16,2,32,256]{3,2,1,0:T(8,128)(2,1)S(1)} %collective-permute-done.6.refs_2_, bf16[16,2,32,256]{3,2,1,0:T(8,128)(2,1)S(1)} %collective-permute-done.8.refs_3_, ...), custom_call_target="tpu_custom_call" | custom-call | flops 1 | bytes 1 | tf_op jit(solution)/shard_map/code_sums/pallas_call | solution.py:115
  70.5 21.2 %all_to_all.5.u_ref = s16[16,144,256]{2,1,0:T(8,128)(2,1)S(1)} all-to-all(s16[16,144,256]{2,1,0:T(8,128)(2,1)S(1)} %code_sums.1), channel_id=1, replica_groups=mesh['mom'=16,'band'=8] {'mom'}, dimensions={0} | all-to-all | bytes 2359296 | tf_op jit(solution)/shard_map/all_to_all | solution.py:247
  91.7 4.6 %collective-permute-start.14 = (s16[16,144,256]{2,1,0:T(8,128)(2,1)S(1)}, s16[16,144,256]{2,1,0:T(8,128)(2,1)S(1)}, u32[]{:S(2)}, u32[]{:S(2)}) collective-permute-start(s16[16,144,256]{2,1,0:T(8,128)(2,1)S(1)} %all_to_all.5.u_ref), channel_id=1, source_target_pairs={{0,1},{1,0},{2,3},{3,2},{4,5},{5,4},{6,7},{7,6},{8,9},{9,8},{10,11... | collective-permute-start | bytes 3538952 | tf_op jit(solution)/shard_map/ppermute | solution.py:190
  96.6 2.1 %collective-permute-done.14.pair_ref = s16[16,144,256]{2,1,0:T(8,128)(2,1)S(1)} collective-permute-done((s16[16,144,256]{2,1,0:T(8,128)(2,1)S(1)}, s16[16,144,256]{2,1,0:T(8,128)(2,1)S(1)}, u32[]{:S(2)}, u32[]{:S(2)}) %collective-permute-start.14) | collective-permute-done | bytes 1179680 | tf_op jit(solution)/shard_map/ppermute | solution.py:190
  98.7 4.6 %contract_virtual.1 = (f32[2,64,16,128]{3,2,1,0:T(8,128)S(1)}, f32[2,64,16,128]{3,2,1,0:T(8,128)S(1)}) custom-call(s32[64]{0:T(128)S(1)} %fusion.6.k4_ref, s32[64]{0:T(128)S(1)} %select_reduce_fusion.k2_ref, f32[64,128]{1,0:T(8,128)S(1)} %dynamic-slice_convert_fusion.mask_ref, s16[16,144,256]{2,1,0:T(8,128)(2,1)S(1)} %all_to_all.5.u_ref, ...), custom_call_target="tpu_custom_call" | custom-call | flops 1 | bytes 1 | tf_op jit(solution)/shard_map/contract_virtual/pallas_call | solution.py:167
  103.8 2.3 %collective-permute-done.15 = f32[2,64,16,128]{3,2,1,0:T(8,128)S(1)} collective-permute-done((f32[2,64,16,128]{3,2,1,0:T(8,128)S(1)}, f32[2,64,16,128]{3,2,1,0:T(8,128)S(1)}, u32[]{:S(2)}, u32[]{:S(2)}) %collective-permute-start.15) | collective-permute-done | bytes 1048608 | tf_op jit(solution)/shard_map/ppermute | solution.py:190
  106.1 1.6 %maximum_select_fusion = f32[2,64,1,2,8,256]{5,4,3,2,1,0:T(8,128)} fusion(f32[2,64,1,2,8,128]{5,4,3,2,1,0:T(8,128)S(1)} %bitcast.49, f32[2,64,1,2,8,128]{5,4,3,2,1,0:T(8,128)S(1)} %bitcast.44, pred[]{:T(512)S(6)} %eq.30), kind=kLoop, calls=%fused_computation.2 | loop fusion | flops 1572864 | bytes 4194305 | tf_op jit(solution)/shard_map/jit(_where)/select_n | solution.py:255
  (64 shorter events, 11.5 us)
Async XLA Ops:
  0.0 1.2 %copy-start = (bf16[4,2,256,256]{3,2,1,0:T(8,128)(2,1)S(1)}, bf16[4,2,256,256]{3,2,1,0:T(8,128)(2,1)}, u32[]{:S(2)}) copy-start(bf16[4,2,256,256]{3,2,1,0:T(8,128)(2,1)} %param.7) | copy-start | bytes 3145732
  1.3 18.4 %collective-permute-start.1 = (bf16[4,2,256,128]{3,2,1,0:T(8,128)(2,1)S(1)}, bf16[4,2,256,128]{3,2,1,0:T(8,128)(2,1)S(1)}, u32[]{:S(2)}, u32[]{:S(2)}) collective-permute-start(bf16[4,2,256,128]{3,2,1,0:T(8,128)(2,1)S(1)} %constant_dynamic-slice_fusion), channel_id=1, source_target_pairs={{0,8},{1,33},{2,10},{3,35},{4,12},{5,37},{6,14},{7,39},{8,16},{9,4... | collective-permute-start | bytes 1572872 | tf_op jit(solution)/shard_map/ppermute | solution.py:203
  3.4 16.3 %collective-permute-start.2 = (bf16[4,2,256,128]{3,2,1,0:T(8,128)(2,1)S(1)}, bf16[4,2,256,128]{3,2,1,0:T(8,128)(2,1)S(1)}, u32[]{:S(2)}, u32[]{:S(2)}) collective-permute-start(bf16[4,2,256,128]{3,2,1,0:T(8,128)(2,1)S(1)} %constant_dynamic-slice_fusion), channel_id=1, source_target_pairs={{0,24},{1,97},{2,26},{3,99},{4,28},{5,101},{6,30},{7,103},{8,0},{9... | collective-permute-start | bytes 1572872 | tf_op jit(solution)/shard_map/ppermute | solution.py:203
  4.8 15.0 %collective-permute-start.3 = (bf16[4,2,256,128]{3,2,1,0:T(8,128)(2,1)S(1)}, bf16[4,2,256,128]{3,2,1,0:T(8,128)(2,1)S(1)}, u32[]{:S(2)}, u32[]{:S(2)}) collective-permute-start(bf16[4,2,256,128]{3,2,1,0:T(8,128)(2,1)S(1)} %constant_dynamic-slice_fusion), channel_id=1, source_target_pairs={{0,16},{1,65},{2,18},{3,67},{4,20},{5,69},{6,22},{7,71},{8,24},{9,... | collective-permute-start | bytes 1572872 | tf_op jit(solution)/shard_map/ppermute | solution.py:203
  13.4 9.4 %collective-permute-start = (bf16[4,16,2,32,256]{4,3,2,1,0:T(8,128)(2,1)S(1)}, bf16[4,16,2,32,256]{4,3,2,1,0:T(8,128)(2,1)S(1)}, u32[]{:S(2)}, u32[]{:S(2)}) collective-permute-start(bf16[4,16,2,32,256]{4,3,2,1,0:T(8,128)(2,1)S(1)} %contract_partner.2), channel_id=1, source_target_pairs={{0,1},{1,0},{2,3},{3,2},{4,5},{5,4},{6,7},{7,6},{8,9},{9,8},{10,11... | collective-permute-start | bytes 6291464 | tf_op jit(solution)/shard_map/ppermute | solution.py:190
  19.6 9.8 %collective-permute-start.7 = (bf16[4,16,2,32,256]{4,3,2,1,0:T(8,128)(2,1)S(1)}, bf16[4,16,2,32,256]{4,3,2,1,0:T(8,128)(2,1)S(1)}, u32[]{:S(2)}, u32[]{:S(2)}) collective-permute-start(bf16[4,16,2,32,256]{4,3,2,1,0:T(8,128)(2,1)S(1)} %contract_partner.3), channel_id=1, source_target_pairs={{0,1},{1,0},{2,3},{3,2},{4,5},{5,4},{6,7},{7,6},{8,9},{9,8},{10,11... | collective-permute-start | bytes 6291464 | tf_op jit(solution)/shard_map/ppermute | solution.py:190
  20.0 6.6 %copy-start.2 = (bf16[16,2,256,128]{3,2,1,0:T(8,128)(2,1)}, bf16[16,2,256,128]{3,2,1,0:T(8,128)(2,1)S(1)}, u32[]{:S(2)}) copy-start(bf16[16,2,256,128]{3,2,1,0:T(8,128)(2,1)S(1)} %pad_maximum_fusion.rest_0_) | copy-start | bytes 6291460
  20.1 26.5 %collective-permute-start.4 = (bf16[16,2,256,128]{3,2,1,0:T(8,128)(2,1)S(1)}, bf16[16,2,256,128]{3,2,1,0:T(8,128)(2,1)S(1)}, u32[]{:S(2)}, u32[]{:S(2)}) collective-permute-start(bf16[16,2,256,128]{3,2,1,0:T(8,128)(2,1)S(1)} %pad_maximum_fusion.rest_0_), channel_id=1, source_target_pairs={{0,32},{1,9},{2,34},{3,11},{4,36},{5,13},{6,38},{7,15},{8,40},{9,1... | collective-permute-start | bytes 6291464 | tf_op jit(solution)/shard_map/ppermute | solution.py:203
  20.9 25.7 %collective-permute-start.5 = (bf16[16,2,256,128]{3,2,1,0:T(8,128)(2,1)S(1)}, bf16[16,2,256,128]{3,2,1,0:T(8,128)(2,1)S(1)}, u32[]{:S(2)}, u32[]{:S(2)}) collective-permute-start(bf16[16,2,256,128]{3,2,1,0:T(8,128)(2,1)S(1)} %pad_maximum_fusion.rest_0_), channel_id=1, source_target_pairs={{0,96},{1,25},{2,98},{3,27},{4,100},{5,29},{6,102},{7,31},{8,104},... | collective-permute-start | bytes 6291464 | tf_op jit(solution)/shard_map/ppermute | solution.py:203
  26.6 21.2 %collective-permute-start.6 = (bf16[16,2,32,256]{3,2,1,0:T(8,128)(2,1)S(1)}, bf16[16,2,32,256]{3,2,1,0:T(8,128)(2,1)S(1)}, u32[]{:S(2)}, u32[]{:S(2)}) collective-permute-start(bf16[16,2,32,256]{3,2,1,0:T(8,128)(2,1)S(1)} %get-tuple-element.24), channel_id=1, source_target_pairs={{0,6},{1,7},{2,0},{3,1},{4,2},{5,3},{6,4},{7,5},{8,14},{9,15},{10,... | collective-permute-start | bytes 1572872 | tf_op jit(solution)/shard_map/ppermute | solution.py:193
  33.3 16.7 %collective-permute-start.8 = (bf16[16,2,32,256]{3,2,1,0:T(8,128)(2,1)S(1)}, bf16[16,2,32,256]{3,2,1,0:T(8,128)(2,1)S(1)}, u32[]{:S(2)}, u32[]{:S(2)}) collective-permute-start(bf16[16,2,32,256]{3,2,1,0:T(8,128)(2,1)S(1)} %get-tuple-element.26), channel_id=1, source_target_pairs={{0,6},{1,7},{2,0},{3,1},{4,2},{5,3},{6,4},{7,5},{8,14},{9,15},{10,... | collective-permute-start | bytes 1572872 | tf_op jit(solution)/shard_map/ppermute | solution.py:193
  34.1 23.4 %collective-permute-start.11 = (bf16[16,4,32,256]{3,2,1,0:T(8,128)(2,1)S(1)}, bf16[16,4,32,256]{3,2,1,0:T(8,128)(2,1)S(1)}, u32[]{:S(2)}, u32[]{:S(2)}) collective-permute-start(bf16[16,4,32,256]{3,2,1,0:T(8,128)(2,1)S(1)} %pad_maximum_fusion.1), channel_id=1, source_target_pairs={{0,2},{1,3},{2,4},{3,5},{4,6},{5,7},{6,0},{7,1},{8,10},{9,11},{10,... | collective-permute-start | bytes 3145736 | tf_op jit(solution)/shard_map/ppermute | solution.py:193
  46.5 1.3 %copy-start.3 = (bf16[16,2,256,128]{3,2,1,0:T(8,128)(2,1)}, bf16[16,2,256,128]{3,2,1,0:T(8,128)(2,1)S(1)}, u32[]{:S(2)}) copy-start(bf16[16,2,256,128]{3,2,1,0:T(8,128)(2,1)S(1)} %collective-permute-done.4.rest_1_) | copy-start | bytes 6291460
  46.6 3.4 %copy-start.4 = (bf16[16,2,256,128]{3,2,1,0:T(8,128)(2,1)}, bf16[16,2,256,128]{3,2,1,0:T(8,128)(2,1)S(1)}, u32[]{:S(2)}) copy-start(bf16[16,2,256,128]{3,2,1,0:T(8,128)(2,1)S(1)} %collective-permute-done.5.rest_2_) | copy-start | bytes 6291460
  49.9 19.0 %copy-start.1 = (s32[4,16]{1,0:T(4,128)S(1)}, s32[4,16]{1,0:T(4,128)}, u32[]{:S(2)}) copy-start(s32[4,16]{1,0:T(4,128)} %refs_7_.1) | copy-start | bytes 772
  50.1 14.0 %collective-permute-start.10 = (bf16[8,2,256,128]{3,2,1,0:T(8,128)(2,1)S(1)}, bf16[8,2,256,128]{3,2,1,0:T(8,128)(2,1)S(1)}, u32[]{:S(2)}, u32[]{:S(2)}) collective-permute-start(bf16[8,2,256,128]{3,2,1,0:T(8,128)(2,1)S(1)} %slice.59), channel_id=1, source_target_pairs={{0,96},{1,25},{2,98},{3,27},{4,100},{5,29},{6,102},{7,31},{8,104},... | collective-permute-start | bytes 3145736 | tf_op jit(solution)/shard_map/ppermute | solution.py:203
  50.6 15.2 %collective-permute-start.9 = (bf16[8,2,256,128]{3,2,1,0:T(8,128)(2,1)S(1)}, bf16[8,2,256,128]{3,2,1,0:T(8,128)(2,1)S(1)}, u32[]{:S(2)}, u32[]{:S(2)}) collective-permute-start(bf16[8,2,256,128]{3,2,1,0:T(8,128)(2,1)S(1)} %slice.58), channel_id=1, source_target_pairs={{0,32},{1,9},{2,34},{3,11},{4,36},{5,13},{6,38},{7,15},{8,40},{9,1... | collective-permute-start | bytes 3145736 | tf_op jit(solution)/shard_map/ppermute | solution.py:203
  51.6 14.1 %collective-permute-start.13 = (bf16[8,4,32,256]{3,2,1,0:T(8,128)(2,1)S(1)}, bf16[8,4,32,256]{3,2,1,0:T(8,128)(2,1)S(1)}, u32[]{:S(2)}, u32[]{:S(2)}) collective-permute-start(bf16[8,4,32,256]{3,2,1,0:T(8,128)(2,1)S(1)} %pad_maximum_fusion.2), channel_id=1, source_target_pairs={{0,6},{1,7},{2,0},{3,1},{4,2},{5,3},{6,4},{7,5},{8,14},{9,15},{10,... | collective-permute-start | bytes 1572872 | tf_op jit(solution)/shard_map/ppermute | solution.py:193
  57.7 11.3 %collective-permute-start.12 = (bf16[8,4,32,256]{3,2,1,0:T(8,128)(2,1)S(1)}, bf16[8,4,32,256]{3,2,1,0:T(8,128)(2,1)S(1)}, u32[]{:S(2)}, u32[]{:S(2)}) collective-permute-start(bf16[8,4,32,256]{3,2,1,0:T(8,128)(2,1)S(1)} %fusion), channel_id=1, source_target_pairs={{0,2},{1,3},{2,4},{3,5},{4,6},{5,7},{6,0},{7,1},{8,10},{9,11},{10,... | collective-permute-start | bytes 1572872 | tf_op jit(solution)/shard_map/ppermute | solution.py:193
  64.1 6.4 %copy-start.5 = (bf16[8,2,256,128]{3,2,1,0:T(8,128)(2,1)}, bf16[8,2,256,128]{3,2,1,0:T(8,128)(2,1)S(1)}, u32[]{:S(2)}) copy-start(bf16[8,2,256,128]{3,2,1,0:T(8,128)(2,1)S(1)} %collective-permute-done.10.rest_4_) | copy-start | bytes 3145732
  65.8 3.2 %copy-start.6 = (bf16[8,2,256,128]{3,2,1,0:T(8,128)(2,1)}, bf16[8,2,256,128]{3,2,1,0:T(8,128)(2,1)S(1)}, u32[]{:S(2)}) copy-start(bf16[8,2,256,128]{3,2,1,0:T(8,128)(2,1)S(1)} %collective-permute-done.9.rest_3_) | copy-start | bytes 3145732
  70.5 25.8 %copy-start.7 = (s32[64,256]{1,0:T(8,128)S(1)}, s32[64,256]{1,0:T(8,128)}, u32[]{:S(2)}) copy-start(s32[64,256]{1,0:T(8,128)} %param.10) | copy-start | bytes 196612
  91.7 7.0 %collective-permute-start.14 = (s16[16,144,256]{2,1,0:T(8,128)(2,1)S(1)}, s16[16,144,256]{2,1,0:T(8,128)(2,1)S(1)}, u32[]{:S(2)}, u32[]{:S(2)}) collective-permute-start(s16[16,144,256]{2,1,0:T(8,128)(2,1)S(1)} %all_to_all.5.u_ref), channel_id=1, source_target_pairs={{0,1},{1,0},{2,3},{3,2},{4,5},{5,4},{6,7},{7,6},{8,9},{9,8},{10,11... | collective-permute-start | bytes 3538952 | tf_op jit(solution)/shard_map/ppermute | solution.py:190
  103.3 2.7 %collective-permute-start.15 = (f32[2,64,16,128]{3,2,1,0:T(8,128)S(1)}, f32[2,64,16,128]{3,2,1,0:T(8,128)S(1)}, u32[]{:S(2)}, u32[]{:S(2)}) collective-permute-start(f32[2,64,16,128]{3,2,1,0:T(8,128)S(1)} %get-tuple-element.36), channel_id=1, source_target_pairs={{0,1},{1,0},{2,3},{3,2},{4,5},{5,4},{6,7},{7,6},{8,9},{9,8},{10,11... | collective-permute-start | bytes 3145736 | tf_op jit(solution)/shard_map/ppermute | solution.py:190

commit v6 on v5

--- a/solution.py
+++ b/solution.py
@@ -136,8 +136,7 @@
         for i in range(len(held)):
             copy(i).start()
 
-        @pl.loop(0, 16)
-        def _(j):
+        for j in range(16):
             for h, ref in enumerate((u_ref, pair_ref)):
                 scale = jnp.exp2(ref[j, 128:144].astype(jnp.int32).astype(jnp.float32) - 14.5)
                 for c in range(4):

time: 108 us -> 108 us (level)
  no operation moved by 1% of the time
where the time goes in v6:
time: 108 us
  waiting for transfers between devices  31.4 us (29%)
  starting transfers between devices  25 us (23%)
  Pallas kernels  21.4 us (20%)
  blocking collectives  21.2 us (20%)
  local copies, waits for them, and re-layouts  5.02 us (5%)
  other arithmetic  3.27 us (3%)
    all_to_all x1, blocking collectives, per_device(): u = lax.all_to_all(coded, 'mom', split_axis=0, concat_axis=0, tiled=True)  21.2 us
    ppermute x7, waiting for transfers between devices, onward(): return lax.ppermute(v, ('mom', 'band'), pairs)  19.3 us
    pallas_call x4, Pallas kernels, contract_occupied(): pl.pallas_call(kernel, in_specs=[vmem, pl.BlockSpec(memory_space=pltpu.HB...  15.3 us
    ppermute x7, starting transfers between devices, onward(): return lax.ppermute(v, ('mom', 'band'), pairs)  9.39 us
    ppermute x5, starting transfers between devices, along(): lax.ppermute(x, 'band', [(i, (i // 2 + d) % 4 * 2 + i % 2) for i in range...  8.07 us
    ppermute x5, waiting for transfers between devices, along(): lax.ppermute(x, 'band', [(i, (i // 2 + d) % 4 * 2 + i % 2) for i in range...  7.68 us
    ppermute x4, starting transfers between devices, across(): return lax.ppermute(x, 'band', [(i, i ^ 1) for i in range(8)])  7.56 us
    pallas_call x1, Pallas kernels, contract_virtual(): pl.pallas_call(kernel, in_specs=[pl.BlockSpec(memory_space=pltpu.SMEM)] *...  4.57 us
  transfers between devices with their start and end apart: 16, of which 8 were waited for; matrix products, arithmetic and copies ran while one was open for 4% of the time, Pallas kernels for 14%

profile of v6, /device:TPU:1, one launch (start us, length us, event | category | flops | bytes accessed | tf_op | source)
XLA Modules:
  0.0 107.6 jit_solution(15950408203747636618)
XLA Ops:
  1.3 2.1 %collective-permute-start.1 = (bf16[4,2,256,128]{3,2,1,0:T(8,128)(2,1)S(1)}, bf16[4,2,256,128]{3,2,1,0:T(8,128)(2,1)S(1)}, u32[]{:S(2)}, u32[]{:S(2)}) collective-permute-start(bf16[4,2,256,128]{3,2,1,0:T(8,128)(2,1)S(1)} %constant_dynamic-slice_fusion), channel_id=1, source_target_pairs={{0,8},{1,33},{2,10},{3,35},{4,12},{5,37},{6,14},{7,39},{8,16},{9,4... | collective-permute-start | bytes 1572872 | tf_op jit(solution)/shard_map/ppermute | solution.py:202
  3.4 1.4 %collective-permute-start.2 = (bf16[4,2,256,128]{3,2,1,0:T(8,128)(2,1)S(1)}, bf16[4,2,256,128]{3,2,1,0:T(8,128)(2,1)S(1)}, u32[]{:S(2)}, u32[]{:S(2)}) collective-permute-start(bf16[4,2,256,128]{3,2,1,0:T(8,128)(2,1)S(1)} %constant_dynamic-slice_fusion), channel_id=1, source_target_pairs={{0,24},{1,97},{2,26},{3,99},{4,28},{5,101},{6,30},{7,103},{8,0},{9... | collective-permute-start | bytes 1572872 | tf_op jit(solution)/shard_map/ppermute | solution.py:202
  4.8 1.6 %collective-permute-start.3 = (bf16[4,2,256,128]{3,2,1,0:T(8,128)(2,1)S(1)}, bf16[4,2,256,128]{3,2,1,0:T(8,128)(2,1)S(1)}, u32[]{:S(2)}, u32[]{:S(2)}) collective-permute-start(bf16[4,2,256,128]{3,2,1,0:T(8,128)(2,1)S(1)} %constant_dynamic-slice_fusion), channel_id=1, source_target_pairs={{0,16},{1,65},{2,18},{3,67},{4,20},{5,69},{6,22},{7,71},{8,24},{9,... | collective-permute-start | bytes 1572872 | tf_op jit(solution)/shard_map/ppermute | solution.py:202
  9.5 3.8 %contract_partner.2 = bf16[4,16,2,32,256]{4,3,2,1,0:T(8,128)(2,1)S(1)} custom-call(bf16[4,16,64]{2,1,0:T(8,128)(2,1)S(1)} %get-tuple-element.37.coef_ref, bf16[2,4,16,256,256]{4,3,2,1,0:T(8,128)(2,1)} %bitcast.45), custom_call_target="tpu_custom_call" | custom-call | flops 1 | bytes 1 | tf_op jit(solution)/shard_map/contract_partner/pallas_call | solution.py:76
  13.4 2.4 %collective-permute-start = (bf16[4,16,2,32,256]{4,3,2,1,0:T(8,128)(2,1)S(1)}, bf16[4,16,2,32,256]{4,3,2,1,0:T(8,128)(2,1)S(1)}, u32[]{:S(2)}, u32[]{:S(2)}) collective-permute-start(bf16[4,16,2,32,256]{4,3,2,1,0:T(8,128)(2,1)S(1)} %contract_partner.2), channel_id=1, source_target_pairs={{0,1},{1,0},{2,3},{3,2},{4,5},{5,4},{6,7},{7,6},{8,9},{9,8},{10,11... | collective-permute-start | bytes 6291464 | tf_op jit(solution)/shard_map/ppermute | solution.py:189
  15.8 3.8 %contract_partner.3 = bf16[4,16,2,32,256]{4,3,2,1,0:T(8,128)(2,1)S(1)} custom-call(bf16[4,16,64]{2,1,0:T(8,128)(2,1)S(1)} %get-tuple-element.37.coef_ref, bf16[2,4,16,256,256]{4,3,2,1,0:T(8,128)(2,1)} %bitcast.46), custom_call_target="tpu_custom_call" | custom-call | flops 1 | bytes 1 | tf_op jit(solution)/shard_map/contract_partner/pallas_call | solution.py:76
  20.9 1.9 %collective-permute-start.5 = (bf16[16,2,256,128]{3,2,1,0:T(8,128)(2,1)S(1)}, bf16[16,2,256,128]{3,2,1,0:T(8,128)(2,1)S(1)}, u32[]{:S(2)}, u32[]{:S(2)}) collective-permute-start(bf16[16,2,256,128]{3,2,1,0:T(8,128)(2,1)S(1)} %pad_maximum_fusion.rest_0_), channel_id=1, source_target_pairs={{0,96},{1,25},{2,98},{3,27},{4,100},{5,29},{6,102},{7,31},{8,104},... | collective-permute-start | bytes 6291464 | tf_op jit(solution)/shard_map/ppermute | solution.py:202
  22.8 3.8 %contract_own.2 = (f32[16,2,32,256]{3,2,1,0:T(8,128)S(1)}, f32[8,2,32,256]{3,2,1,0:T(8,128)S(1)}, f32[8,2,32,256]{3,2,1,0:T(8,128)S(1)}, bf16[16,2,32,256]{3,2,1...) custom-call(bf16[4,16,64]{2,1,0:T(8,128)(2,1)S(1)} %get-tuple-element.38.coef_ref, bf16[2,4,16,256,256]{4,3,2,1,0:T(8,128)(2,1)} %bitcast.47, ...), custom_call_target="tpu_custom_call" | custom-call | flops 1 | bytes 1 | tf_op jit(solution)/shard_map/contract_own/pallas_call | solution.py:76
  26.6 2.8 %collective-permute-start.6 = (bf16[16,2,32,256]{3,2,1,0:T(8,128)(2,1)S(1)}, bf16[16,2,32,256]{3,2,1,0:T(8,128)(2,1)S(1)}, u32[]{:S(2)}, u32[]{:S(2)}) collective-permute-start(bf16[16,2,32,256]{3,2,1,0:T(8,128)(2,1)S(1)} %get-tuple-element.24), channel_id=1, source_target_pairs={{0,6},{1,7},{2,0},{3,1},{4,2},{5,3},{6,4},{7,5},{8,14},{9,15},{10,... | collective-permute-start | bytes 1572872 | tf_op jit(solution)/shard_map/ppermute | solution.py:192
  29.5 3.8 %contract_own.3 = (f32[16,2,32,256]{3,2,1,0:T(8,128)S(1)}, f32[8,2,32,256]{3,2,1,0:T(8,128)S(1)}, f32[8,2,32,256]{3,2,1,0:T(8,128)S(1)}, bf16[16,2,32,256]{3,2,1...) custom-call(bf16[4,16,64]{2,1,0:T(8,128)(2,1)S(1)} %get-tuple-element.38.coef_ref, bf16[2,4,16,256,256]{4,3,2,1,0:T(8,128)(2,1)} %bitcast.48, ...), custom_call_target="tpu_custom_call" | custom-call | flops 1 | bytes 1 | tf_op jit(solution)/shard_map/contract_own/pallas_call | solution.py:76
  35.2 11.3 %collective-permute-done.4.rest_1_ = bf16[16,2,256,128]{3,2,1,0:T(8,128)(2,1)S(1)} collective-permute-done((bf16[16,2,256,128]{3,2,1,0:T(8,128)(2,1)S(1)}, bf16[16,2,256,128]{3,2,1,0:T(8,128)(2,1)S(1)}, u32[]{:S(2)}, u32[]{:S(2)}) %collective-permute-start.4) | collective-permute-done | bytes 2097184 | tf_op jit(solution)/shard_map/ppermute | solution.py:202
  47.9 2.0 %collective-permute-done.8.refs_3_ = bf16[16,2,32,256]{3,2,1,0:T(8,128)(2,1)S(1)} collective-permute-done((bf16[16,2,32,256]{3,2,1,0:T(8,128)(2,1)S(1)}, bf16[16,2,32,256]{3,2,1,0:T(8,128)(2,1)S(1)}, u32[]{:S(2)}, u32[]{:S(2)}) %collective-permute-start.8) | collective-permute-done | bytes 524320 | tf_op jit(solution)/shard_map/ppermute | solution.py:192
  51.6 3.4 %collective-permute-start.13 = (bf16[8,4,32,256]{3,2,1,0:T(8,128)(2,1)S(1)}, bf16[8,4,32,256]{3,2,1,0:T(8,128)(2,1)S(1)}, u32[]{:S(2)}, u32[]{:S(2)}) collective-permute-start(bf16[8,4,32,256]{3,2,1,0:T(8,128)(2,1)S(1)} %pad_maximum_fusion.2), channel_id=1, source_target_pairs={{0,6},{1,7},{2,0},{3,1},{4,2},{5,3},{6,4},{7,5},{8,14},{9,15},{10,... | collective-permute-start | bytes 1572872 | tf_op jit(solution)/shard_map/ppermute | solution.py:192
  55.0 2.5 %collective-permute-done.11.refs_4_ = bf16[16,4,32,256]{3,2,1,0:T(8,128)(2,1)S(1)} collective-permute-done((bf16[16,4,32,256]{3,2,1,0:T(8,128)(2,1)S(1)}, bf16[16,4,32,256]{3,2,1,0:T(8,128)(2,1)S(1)}, u32[]{:S(2)}, u32[]{:S(2)}) %collective-permute-start.11) | collective-permute-done | bytes 1048608 | tf_op jit(solution)/shard_map/ppermute | solution.py:192
  57.8 6.3 %collective-permute-done.10.rest_4_ = bf16[8,2,256,128]{3,2,1,0:T(8,128)(2,1)S(1)} collective-permute-done((bf16[8,2,256,128]{3,2,1,0:T(8,128)(2,1)S(1)}, bf16[8,2,256,128]{3,2,1,0:T(8,128)(2,1)S(1)}, u32[]{:S(2)}, u32[]{:S(2)}) %collective-permute-start.10) | collective-permute-done | bytes 1048608 | tf_op jit(solution)/shard_map/ppermute | solution.py:202
  64.1 1.7 %collective-permute-done.9.rest_3_ = bf16[8,2,256,128]{3,2,1,0:T(8,128)(2,1)S(1)} collective-permute-done((bf16[8,2,256,128]{3,2,1,0:T(8,128)(2,1)S(1)}, bf16[8,2,256,128]{3,2,1,0:T(8,128)(2,1)S(1)}, u32[]{:S(2)}, u32[]{:S(2)}) %collective-permute-start.9) | collective-permute-done | bytes 1048608 | tf_op jit(solution)/shard_map/ppermute | solution.py:202
  65.8 3.2 %collective-permute-done.12.refs_5_ = bf16[8,4,32,256]{3,2,1,0:T(8,128)(2,1)S(1)} collective-permute-done((bf16[8,4,32,256]{3,2,1,0:T(8,128)(2,1)S(1)}, bf16[8,4,32,256]{3,2,1,0:T(8,128)(2,1)S(1)}, u32[]{:S(2)}, u32[]{:S(2)}) %collective-permute-start.12) | collective-permute-done | bytes 524320 | tf_op jit(solution)/shard_map/ppermute | solution.py:192
  69.0 1.5 %code_sums.1 = s16[16,144,256]{2,1,0:T(8,128)(2,1)S(1)} custom-call(f32[16,2,32,256]{3,2,1,0:T(8,128)S(1)} %get-tuple-element.29.refs_0_, f32[16,2,32,256]{3,2,1,0:T(8,128)S(1)} %get-tuple-element.30.refs_1_, bf16[16,2,32,256]{3,2,1,0:T(8,128)(2,1)S(1)} %collective-permute-done.6.refs_2_, bf16[16,2,32,256]{3,2,1,0:T(8,128)(2,1)S(1)} %collective-permute-done.8.refs_3_, ...), custom_call_target="tpu_custom_call" | custom-call | flops 1 | bytes 1 | tf_op jit(solution)/shard_map/code_sums/pallas_call | solution.py:115
  70.5 21.2 %all_to_all.5.u_ref = s16[16,144,256]{2,1,0:T(8,128)(2,1)S(1)} all-to-all(s16[16,144,256]{2,1,0:T(8,128)(2,1)S(1)} %code_sums.1), channel_id=1, replica_groups=mesh['mom'=16,'band'=8] {'mom'}, dimensions={0} | all-to-all | bytes 2359296 | tf_op jit(solution)/shard_map/all_to_all | solution.py:246
  91.7 4.6 %collective-permute-start.14 = (s16[16,144,256]{2,1,0:T(8,128)(2,1)S(1)}, s16[16,144,256]{2,1,0:T(8,128)(2,1)S(1)}, u32[]{:S(2)}, u32[]{:S(2)}) collective-permute-start(s16[16,144,256]{2,1,0:T(8,128)(2,1)S(1)} %all_to_all.5.u_ref), channel_id=1, source_target_pairs={{0,1},{1,0},{2,3},{3,2},{4,5},{5,4},{6,7},{7,6},{8,9},{9,8},{10,11... | collective-permute-start | bytes 3538952 | tf_op jit(solution)/shard_map/ppermute | solution.py:189
  96.6 2.1 %collective-permute-done.14.pair_ref = s16[16,144,256]{2,1,0:T(8,128)(2,1)S(1)} collective-permute-done((s16[16,144,256]{2,1,0:T(8,128)(2,1)S(1)}, s16[16,144,256]{2,1,0:T(8,128)(2,1)S(1)}, u32[]{:S(2)}, u32[]{:S(2)}) %collective-permute-start.14) | collective-permute-done | bytes 1179680 | tf_op jit(solution)/shard_map/ppermute | solution.py:189
  98.7 4.6 %contract_virtual.1 = (f32[2,64,16,128]{3,2,1,0:T(8,128)S(1)}, f32[2,64,16,128]{3,2,1,0:T(8,128)S(1)}) custom-call(s32[64]{0:T(128)S(1)} %fusion.6.k4_ref, s32[64]{0:T(128)S(1)} %select_reduce_fusion.k2_ref, f32[64,128]{1,0:T(8,128)S(1)} %dynamic-slice_convert_fusion.mask_ref, s16[16,144,256]{2,1,0:T(8,128)(2,1)S(1)} %all_to_all.5.u_ref, ...), custom_call_target="tpu_custom_call" | custom-call | flops 1 | bytes 1 | tf_op jit(solution)/shard_map/contract_virtual/pallas_call | solution.py:166
  103.8 2.3 %collective-permute-done.15 = f32[2,64,16,128]{3,2,1,0:T(8,128)S(1)} collective-permute-done((f32[2,64,16,128]{3,2,1,0:T(8,128)S(1)}, f32[2,64,16,128]{3,2,1,0:T(8,128)S(1)}, u32[]{:S(2)}, u32[]{:S(2)}) %collective-permute-start.15) | collective-permute-done | bytes 1048608 | tf_op jit(solution)/shard_map/ppermute | solution.py:189
  106.1 1.6 %maximum_select_fusion = f32[2,64,1,2,8,256]{5,4,3,2,1,0:T(8,128)} fusion(f32[2,64,1,2,8,128]{5,4,3,2,1,0:T(8,128)S(1)} %bitcast.49, f32[2,64,1,2,8,128]{5,4,3,2,1,0:T(8,128)S(1)} %bitcast.44, pred[]{:T(512)S(6)} %eq.30), kind=kLoop, calls=%fused_computation.2 | loop fusion | flops 1572864 | bytes 4194305 | tf_op jit(solution)/shard_map/jit(_where)/select_n | solution.py:254
  (64 shorter events, 11.5 us)
Async XLA Ops:
  0.0 1.2 %copy-start = (bf16[4,2,256,256]{3,2,1,0:T(8,128)(2,1)S(1)}, bf16[4,2,256,256]{3,2,1,0:T(8,128)(2,1)}, u32[]{:S(2)}) copy-start(bf16[4,2,256,256]{3,2,1,0:T(8,128)(2,1)} %param.7) | copy-start | bytes 3145732
  1.3 18.4 %collective-permute-start.1 = (bf16[4,2,256,128]{3,2,1,0:T(8,128)(2,1)S(1)}, bf16[4,2,256,128]{3,2,1,0:T(8,128)(2,1)S(1)}, u32[]{:S(2)}, u32[]{:S(2)}) collective-permute-start(bf16[4,2,256,128]{3,2,1,0:T(8,128)(2,1)S(1)} %constant_dynamic-slice_fusion), channel_id=1, source_target_pairs={{0,8},{1,33},{2,10},{3,35},{4,12},{5,37},{6,14},{7,39},{8,16},{9,4... | collective-permute-start | bytes 1572872 | tf_op jit(solution)/shard_map/ppermute | solution.py:202
  3.4 16.3 %collective-permute-start.2 = (bf16[4,2,256,128]{3,2,1,0:T(8,128)(2,1)S(1)}, bf16[4,2,256,128]{3,2,1,0:T(8,128)(2,1)S(1)}, u32[]{:S(2)}, u32[]{:S(2)}) collective-permute-start(bf16[4,2,256,128]{3,2,1,0:T(8,128)(2,1)S(1)} %constant_dynamic-slice_fusion), channel_id=1, source_target_pairs={{0,24},{1,97},{2,26},{3,99},{4,28},{5,101},{6,30},{7,103},{8,0},{9... | collective-permute-start | bytes 1572872 | tf_op jit(solution)/shard_map/ppermute | solution.py:202
  4.8 15.0 %collective-permute-start.3 = (bf16[4,2,256,128]{3,2,1,0:T(8,128)(2,1)S(1)}, bf16[4,2,256,128]{3,2,1,0:T(8,128)(2,1)S(1)}, u32[]{:S(2)}, u32[]{:S(2)}) collective-permute-start(bf16[4,2,256,128]{3,2,1,0:T(8,128)(2,1)S(1)} %constant_dynamic-slice_fusion), channel_id=1, source_target_pairs={{0,16},{1,65},{2,18},{3,67},{4,20},{5,69},{6,22},{7,71},{8,24},{9,... | collective-permute-start | bytes 1572872 | tf_op jit(solution)/shard_map/ppermute | solution.py:202
  13.4 9.4 %collective-permute-start = (bf16[4,16,2,32,256]{4,3,2,1,0:T(8,128)(2,1)S(1)}, bf16[4,16,2,32,256]{4,3,2,1,0:T(8,128)(2,1)S(1)}, u32[]{:S(2)}, u32[]{:S(2)}) collective-permute-start(bf16[4,16,2,32,256]{4,3,2,1,0:T(8,128)(2,1)S(1)} %contract_partner.2), channel_id=1, source_target_pairs={{0,1},{1,0},{2,3},{3,2},{4,5},{5,4},{6,7},{7,6},{8,9},{9,8},{10,11... | collective-permute-start | bytes 6291464 | tf_op jit(solution)/shard_map/ppermute | solution.py:189
  19.6 9.8 %collective-permute-start.7 = (bf16[4,16,2,32,256]{4,3,2,1,0:T(8,128)(2,1)S(1)}, bf16[4,16,2,32,256]{4,3,2,1,0:T(8,128)(2,1)S(1)}, u32[]{:S(2)}, u32[]{:S(2)}) collective-permute-start(bf16[4,16,2,32,256]{4,3,2,1,0:T(8,128)(2,1)S(1)} %contract_partner.3), channel_id=1, source_target_pairs={{0,1},{1,0},{2,3},{3,2},{4,5},{5,4},{6,7},{7,6},{8,9},{9,8},{10,11... | collective-permute-start | bytes 6291464 | tf_op jit(solution)/shard_map/ppermute | solution.py:189
  20.0 6.6 %copy-start.2 = (bf16[16,2,256,128]{3,2,1,0:T(8,128)(2,1)}, bf16[16,2,256,128]{3,2,1,0:T(8,128)(2,1)S(1)}, u32[]{:S(2)}) copy-start(bf16[16,2,256,128]{3,2,1,0:T(8,128)(2,1)S(1)} %pad_maximum_fusion.rest_0_) | copy-start | bytes 6291460
  20.1 26.5 %collective-permute-start.4 = (bf16[16,2,256,128]{3,2,1,0:T(8,128)(2,1)S(1)}, bf16[16,2,256,128]{3,2,1,0:T(8,128)(2,1)S(1)}, u32[]{:S(2)}, u32[]{:S(2)}) collective-permute-start(bf16[16,2,256,128]{3,2,1,0:T(8,128)(2,1)S(1)} %pad_maximum_fusion.rest_0_), channel_id=1, source_target_pairs={{0,32},{1,9},{2,34},{3,11},{4,36},{5,13},{6,38},{7,15},{8,40},{9,1... | collective-permute-start | bytes 6291464 | tf_op jit(solution)/shard_map/ppermute | solution.py:202
  20.9 25.7 %collective-permute-start.5 = (bf16[16,2,256,128]{3,2,1,0:T(8,128)(2,1)S(1)}, bf16[16,2,256,128]{3,2,1,0:T(8,128)(2,1)S(1)}, u32[]{:S(2)}, u32[]{:S(2)}) collective-permute-start(bf16[16,2,256,128]{3,2,1,0:T(8,128)(2,1)S(1)} %pad_maximum_fusion.rest_0_), channel_id=1, source_target_pairs={{0,96},{1,25},{2,98},{3,27},{4,100},{5,29},{6,102},{7,31},{8,104},... | collective-permute-start | bytes 6291464 | tf_op jit(solution)/shard_map/ppermute | solution.py:202
  26.6 21.2 %collective-permute-start.6 = (bf16[16,2,32,256]{3,2,1,0:T(8,128)(2,1)S(1)}, bf16[16,2,32,256]{3,2,1,0:T(8,128)(2,1)S(1)}, u32[]{:S(2)}, u32[]{:S(2)}) collective-permute-start(bf16[16,2,32,256]{3,2,1,0:T(8,128)(2,1)S(1)} %get-tuple-element.24), channel_id=1, source_target_pairs={{0,6},{1,7},{2,0},{3,1},{4,2},{5,3},{6,4},{7,5},{8,14},{9,15},{10,... | collective-permute-start | bytes 1572872 | tf_op jit(solution)/shard_map/ppermute | solution.py:192
  33.3 16.7 %collective-permute-start.8 = (bf16[16,2,32,256]{3,2,1,0:T(8,128)(2,1)S(1)}, bf16[16,2,32,256]{3,2,1,0:T(8,128)(2,1)S(1)}, u32[]{:S(2)}, u32[]{:S(2)}) collective-permute-start(bf16[16,2,32,256]{3,2,1,0:T(8,128)(2,1)S(1)} %get-tuple-element.26), channel_id=1, source_target_pairs={{0,6},{1,7},{2,0},{3,1},{4,2},{5,3},{6,4},{7,5},{8,14},{9,15},{10,... | collective-permute-start | bytes 1572872 | tf_op jit(solution)/shard_map/ppermute | solution.py:192
  34.1 23.4 %collective-permute-start.11 = (bf16[16,4,32,256]{3,2,1,0:T(8,128)(2,1)S(1)}, bf16[16,4,32,256]{3,2,1,0:T(8,128)(2,1)S(1)}, u32[]{:S(2)}, u32[]{:S(2)}) collective-permute-start(bf16[16,4,32,256]{3,2,1,0:T(8,128)(2,1)S(1)} %pad_maximum_fusion.1), channel_id=1, source_target_pairs={{0,2},{1,3},{2,4},{3,5},{4,6},{5,7},{6,0},{7,1},{8,10},{9,11},{10,... | collective-permute-start | bytes 3145736 | tf_op jit(solution)/shard_map/ppermute | solution.py:192
  46.5 1.3 %copy-start.3 = (bf16[16,2,256,128]{3,2,1,0:T(8,128)(2,1)}, bf16[16,2,256,128]{3,2,1,0:T(8,128)(2,1)S(1)}, u32[]{:S(2)}) copy-start(bf16[16,2,256,128]{3,2,1,0:T(8,128)(2,1)S(1)} %collective-permute-done.4.rest_1_) | copy-start | bytes 6291460
  46.6 3.4 %copy-start.4 = (bf16[16,2,256,128]{3,2,1,0:T(8,128)(2,1)}, bf16[16,2,256,128]{3,2,1,0:T(8,128)(2,1)S(1)}, u32[]{:S(2)}) copy-start(bf16[16,2,256,128]{3,2,1,0:T(8,128)(2,1)S(1)} %collective-permute-done.5.rest_2_) | copy-start | bytes 6291460
  49.9 19.0 %copy-start.1 = (s32[4,16]{1,0:T(4,128)S(1)}, s32[4,16]{1,0:T(4,128)}, u32[]{:S(2)}) copy-start(s32[4,16]{1,0:T(4,128)} %refs_7_.1) | copy-start | bytes 772
  50.1 14.0 %collective-permute-start.10 = (bf16[8,2,256,128]{3,2,1,0:T(8,128)(2,1)S(1)}, bf16[8,2,256,128]{3,2,1,0:T(8,128)(2,1)S(1)}, u32[]{:S(2)}, u32[]{:S(2)}) collective-permute-start(bf16[8,2,256,128]{3,2,1,0:T(8,128)(2,1)S(1)} %slice.59), channel_id=1, source_target_pairs={{0,96},{1,25},{2,98},{3,27},{4,100},{5,29},{6,102},{7,31},{8,104},... | collective-permute-start | bytes 3145736 | tf_op jit(solution)/shard_map/ppermute | solution.py:202
  50.6 15.2 %collective-permute-start.9 = (bf16[8,2,256,128]{3,2,1,0:T(8,128)(2,1)S(1)}, bf16[8,2,256,128]{3,2,1,0:T(8,128)(2,1)S(1)}, u32[]{:S(2)}, u32[]{:S(2)}) collective-permute-start(bf16[8,2,256,128]{3,2,1,0:T(8,128)(2,1)S(1)} %slice.58), channel_id=1, source_target_pairs={{0,32},{1,9},{2,34},{3,11},{4,36},{5,13},{6,38},{7,15},{8,40},{9,1... | collective-permute-start | bytes 3145736 | tf_op jit(solution)/shard_map/ppermute | solution.py:202
  51.6 14.1 %collective-permute-start.13 = (bf16[8,4,32,256]{3,2,1,0:T(8,128)(2,1)S(1)}, bf16[8,4,32,256]{3,2,1,0:T(8,128)(2,1)S(1)}, u32[]{:S(2)}, u32[]{:S(2)}) collective-permute-start(bf16[8,4,32,256]{3,2,1,0:T(8,128)(2,1)S(1)} %pad_maximum_fusion.2), channel_id=1, source_target_pairs={{0,6},{1,7},{2,0},{3,1},{4,2},{5,3},{6,4},{7,5},{8,14},{9,15},{10,... | collective-permute-start | bytes 1572872 | tf_op jit(solution)/shard_map/ppermute | solution.py:192
  57.7 11.3 %collective-permute-start.12 = (bf16[8,4,32,256]{3,2,1,0:T(8,128)(2,1)S(1)}, bf16[8,4,32,256]{3,2,1,0:T(8,128)(2,1)S(1)}, u32[]{:S(2)}, u32[]{:S(2)}) collective-permute-start(bf16[8,4,32,256]{3,2,1,0:T(8,128)(2,1)S(1)} %fusion), channel_id=1, source_target_pairs={{0,2},{1,3},{2,4},{3,5},{4,6},{5,7},{6,0},{7,1},{8,10},{9,11},{10,... | collective-permute-start | bytes 1572872 | tf_op jit(solution)/shard_map/ppermute | solution.py:192
  64.1 6.4 %copy-start.5 = (bf16[8,2,256,128]{3,2,1,0:T(8,128)(2,1)}, bf16[8,2,256,128]{3,2,1,0:T(8,128)(2,1)S(1)}, u32[]{:S(2)}) copy-start(bf16[8,2,256,128]{3,2,1,0:T(8,128)(2,1)S(1)} %collective-permute-done.10.rest_4_) | copy-start | bytes 3145732
  65.8 3.2 %copy-start.6 = (bf16[8,2,256,128]{3,2,1,0:T(8,128)(2,1)}, bf16[8,2,256,128]{3,2,1,0:T(8,128)(2,1)S(1)}, u32[]{:S(2)}) copy-start(bf16[8,2,256,128]{3,2,1,0:T(8,128)(2,1)S(1)} %collective-permute-done.9.rest_3_) | copy-start | bytes 3145732
  70.5 25.8 %copy-start.7 = (s32[64,256]{1,0:T(8,128)S(1)}, s32[64,256]{1,0:T(8,128)}, u32[]{:S(2)}) copy-start(s32[64,256]{1,0:T(8,128)} %param.10) | copy-start | bytes 196612
  91.7 7.0 %collective-permute-start.14 = (s16[16,144,256]{2,1,0:T(8,128)(2,1)S(1)}, s16[16,144,256]{2,1,0:T(8,128)(2,1)S(1)}, u32[]{:S(2)}, u32[]{:S(2)}) collective-permute-start(s16[16,144,256]{2,1,0:T(8,128)(2,1)S(1)} %all_to_all.5.u_ref), channel_id=1, source_target_pairs={{0,1},{1,0},{2,3},{3,2},{4,5},{5,4},{6,7},{7,6},{8,9},{9,8},{10,11... | collective-permute-start | bytes 3538952 | tf_op jit(solution)/shard_map/ppermute | solution.py:189
  103.3 2.7 %collective-permute-start.15 = (f32[2,64,16,128]{3,2,1,0:T(8,128)S(1)}, f32[2,64,16,128]{3,2,1,0:T(8,128)S(1)}, u32[]{:S(2)}, u32[]{:S(2)}) collective-permute-start(f32[2,64,16,128]{3,2,1,0:T(8,128)S(1)} %get-tuple-element.36), channel_id=1, source_target_pairs={{0,1},{1,0},{2,3},{3,2},{4,5},{5,4},{6,7},{7,6},{8,9},{9,8},{10,11... | collective-permute-start | bytes 3145736 | tf_op jit(solution)/shard_map/ppermute | solution.py:189
